TPU v7x, 32 devices: a whole 2x2x4 slice. The times are simulated.
32 devices in a mesh: groups: 2 (over y), date: 4 (over z), tile: 2 (over x), head: 2 (over core).
Axes of the slice: x: 2, y: 2, z: 4, core: 2. Of those that a mesh axis runs over, the one named last changes fastest.
Arguments:
- tokens: bfloat16 [8, 8, 8, 64, 256], P('groups', 'tile', None, 'date'), parts along dimension 0, may hold values from -240 to 240
- cloud_mask: int32 [8, 8, 8, 64], P('groups', 'tile', None, 'date'), parts along dimension 0, may hold values from 0 to 1, as said below
- day_of_year: int32 [128], P(('groups', 'date')), parts along dimension 0, may hold values from 0 to 1460
- query: float32 [256], P('head'), may hold values from -6 to 6
- key_weight: bfloat16 [256, 256], P(None, 'head'), may hold values from -0.375 to 0.375
- value_weight: bfloat16 [256, 256], P(None, 'head'), may hold values from -0.375 to 0.375
- conv_first: bfloat16 [3, 3, 256, 256], P(None, None, None, 'head'), may hold values from -0.375 to 0.375
- conv_second: bfloat16 [3, 3, 256, 256], P(None, None, None, 'head'), may hold values from -0.1875 to 0.1875
Outputs:
- feature_map: bfloat16 [8, 8, 8, 256], P(('groups', 'date'), 'tile', None, 'head'), parts along dimension 0
There are 2 independent parts, one for each index of `groups`. A program takes and returns all parts, laid end to end along the dimension named above; an argument that names none is the same for every part. Nothing has to cross between parts.
Inputs may be any that keep to these rules, and one draw needn't show every extreme that they name: `cloud_mask`: a pixel may be clouded on all 64 dates.
All inputs are finite; a program needn't handle non-finite values.
Results may differ from a plain program's by a relative error of at most 0.012.
The roundings to bfloat16 on the way count: a program that leaves them out, or rounds other values in their place, can miss the bound.
Values may be sent and summed in bfloat16 or wider, within the bound.
No kernel may reach another device: no remote copies, remote signals or barrier semaphores. Data moves between devices by JAX's collectives and lax.ppermute only.
A program may use at most 128 MiB of HBM per device.

v0:
```python
import jax
import jax.numpy as jnp
from jax import lax
from jax.sharding import PartitionSpec as P

HSIZE = 32
TILE_DEV = 1


cloud_penalty = 6.0


def with_halo(block, sides, width):
    for axis, dim in sides:
        count = lax.axis_size(axis)
        forward = [(i, i + 1) for i in range(count - 1)]
        backward = [(target, source) for source, target in forward]
        low = lax.ppermute(
            lax.slice_in_dim(block, block.shape[dim] - width, None, axis=dim), axis, forward
        )
        high = lax.ppermute(lax.slice_in_dim(block, 0, width, axis=dim), axis, backward)
        block = jnp.concatenate([low, block, high], axis=dim)
    return block


def encoding(day_of_year, width):
    chan = jnp.arange(width)
    expo = (2 * (chan // 2)).astype(jnp.float32) / width
    freq = jnp.power(jnp.float32(1000.0), -expo)
    angle = day_of_year.astype(jnp.float32)[:, None] * freq[None, :]
    return jnp.where((chan % 2 == 0)[None, :], jnp.sin(angle), jnp.cos(angle))


def widen(scales):
    return jnp.repeat(scales, HSIZE, axis=-1)


def merge_blocks(tops, tots, parts):
    best = jnp.max(tops, axis=0)
    scales = jnp.exp(tops - best[None])
    own_totals = jnp.sum(tots * scales, axis=0)
    own_sums = jnp.sum(parts * widen(scales), axis=0)
    return (own_totals, own_sums)


def convolve(block, kernel):
    rows, cols = (block.shape[1], block.shape[2])
    padded = with_halo(block, (("tile", 1),), 1)
    whole = lax.all_gather(padded, "head", axis=3, tiled=True)
    whole = jnp.pad(whole, ((0, 0), (0, 0), (1, 1), (0, 0)))
    total = jnp.zeros((block.shape[0] * rows * cols, kernel.shape[3]), jnp.float32)
    for arow in range(3):
        for bcol in range(3):
            piece = whole[:, arow : arow + rows, bcol : bcol + cols, :].reshape(-1, whole.shape[3])
            total = total + jnp.dot(piece, kernel[arow, bcol], preferred_element_type=jnp.float32)
    return total.reshape(block.shape[0], rows, cols, kernel.shape[3])


def local(
    tokens, cloud_mask, day_of_year, query, key_weight, value_weight, conv_first, conv_second
):
    tiles, rows, cols, dates, width = tokens.shape
    heads_dev = query.shape[0] // HSIZE
    table = encoding(day_of_year, width)
    inputs = (
        (tokens.astype(jnp.float32) + table[None, None, None])
        .astype(jnp.bfloat16)
        .reshape(-1, width)
    )
    keys = jnp.dot(inputs, key_weight, preferred_element_type=jnp.float32).reshape(
        tiles, rows, cols, dates, heads_dev, HSIZE
    )
    vals = jnp.dot(inputs, value_weight, preferred_element_type=jnp.float32).reshape(
        tiles, rows, cols, dates, heads_dev, HSIZE
    )
    query_heads = query.reshape(heads_dev, HSIZE)
    score = jnp.sum(keys * query_heads, axis=-1) / jnp.sqrt(jnp.float32(HSIZE))
    score = score - cloud_penalty * (1.0 - cloud_mask[..., None].astype(jnp.float32))
    top = jnp.max(score, axis=3)
    expo = jnp.exp(score - top[:, :, :, None, :])
    totals = jnp.sum(expo, axis=3)
    sums = jnp.sum(expo[..., None] * vals, axis=3).reshape(tiles, rows, cols, heads_dev * HSIZE)
    got = (
        lax.all_to_all(top, "date", split_axis=0, concat_axis=0, tiled=True),
        lax.all_to_all(totals, "date", split_axis=0, concat_axis=0, tiled=True),
        lax.all_to_all(sums, "date", split_axis=0, concat_axis=0, tiled=True),
    )
    sources = got[0].shape[0] // TILE_DEV
    tops = got[0].reshape(sources, TILE_DEV, rows, cols, heads_dev)
    tots = got[1].reshape(sources, TILE_DEV, rows, cols, heads_dev)
    parts = got[2].reshape(sources, TILE_DEV, rows, cols, heads_dev * HSIZE)
    own_totals, own_sums = merge_blocks(tops, tots, parts)
    pooled = (own_sums / widen(own_totals)).astype(jnp.bfloat16)
    hidden = jax.nn.relu(convolve(pooled, conv_first)).astype(jnp.bfloat16)
    return convolve(hidden, conv_second).astype(jnp.bfloat16)


def solution(mesh):
    in_specs = (
        P("groups", "tile", None, "date", None),
        P("groups", "tile", None, "date"),
        P(("groups", "date")),
        P("head"),
        P(None, "head"),
        P(None, "head"),
        P(None, None, None, "head"),
        P(None, None, None, "head"),
    )
    out_specs = P(("groups", "date"), "tile", None, "head")
    return jax.shard_map(local, mesh=mesh, in_specs=in_specs, out_specs=out_specs, check_vma=False)
```

profile of v0, /device:TPU:0, one launch (start us, length us, event | category | flops | bytes accessed | tf_op | source)
XLA Modules:
  0.0 57.5 jit_solution(14288607514884827071)
XLA Ops:
  0.0 0.9 %copy.23 = bf16[256,128]{0,1:T(8,128)(2,1)S(1)} copy(bf16[256,128]{1,0:T(8,128)(2,1)} %param.12) | data formatting | bytes 131072 | tf_op args[4]
  1.0 0.7 %mul.62 = f32[4,32]{1,0:T(4,128)S(1)} reshape(f32[128]{0:T(128)} %param.11) | data formatting | bytes 1024 | tf_op jit(solution)/shard_map/mul | solution.py:77
  1.7 0.7 %convert_element_type.63 = f32[16]{0:T(128)S(1)} convert(s32[16]{0:T(128)} %param.10) | non-fusion elementwise | flops 16 | bytes 128 | tf_op jit(solution)/shard_map/convert_element_type | solution.py:30
  2.4 0.8 %subtract_multiply_fusion = f32[4,4,8,16]{3,2,1,0:T(8,128)S(1)} fusion(s32[4,4,8,16]{3,2,1,0:T(8,128)} %param.9), kind=kLoop, calls=%fused_computation.79 | loop fusion | flops 6144 | bytes 16384 | tf_op jit(solution)/shard_map/mul | solution.py:78
  3.2 0.1 fusion.47
  3.4 2.6 %multiply_reduce_fusion.1 = f32[4,4,8,16,4]{3,4,2,1,0:T(4,128)S(1)} fusion(bf16[4,32,256,1,1,1]{2,1,0,5,4,3:T(8,128)(2,1)S(1)} %bitcast.147, f32[4,32]{1,0:T(4,128)S(1)} %mul.62, bf16[4,4,8,16,256]{4,3,2,1,0:T(8,128)(2,1)} %param.8, f32[16,256]{1,0:T(8,128)S(1)} %fusion.47), kind=kOutput, calls=%fused_computation.1 | convolution fusion | flops 136306688 | bytes 1163776 | tf_op jit(solution)/shard_map/dot_general | solution.py:70
  6.0 0.2 fusion.8
  6.3 0.2 copy.25
  6.4 0.7 %reshape.252 = f32[4,1,128]{2,1,0:T(1,128)} reshape(f32[4,4,4,8]{3,2,1,0:T(4,128)S(1)} %bitcast.146) | data formatting | bytes 4096
  7.1 6.3 %all-to-all-start.1 = ((f32[4,1,128]{2,1,0:T(1,128)}), f32[4,1,128]{2,1,0:T(1,128)S(1)}, u32[]{:S(2)}, u32[]{:S(2)}) async-start(f32[4,1,128]{2,1,0:T(1,128)} %reshape.252), calls=%async_computation.1 | async-start | bytes 4096 | tf_op jit(solution)/shard_map/all_to_all | solution.py:84
  13.4 0.4 fusion.92
  14.0 1.4 %multiply_reduce_fusion = f32[4,4,8,4,32]{4,3,2,1,0:T(4,128)S(1)} fusion(bf16[4,32,256,1,1,1]{2,1,0,5,4,3:T(8,128)(2,1)S(1)} %bitcast.148, f32[4,4,8,16,4]{3,4,2,1,0:T(4,128)S(1)} %get-tuple-element.8, bf16[4,4,8,16,256]{4,3,2,1,0:T(8,128)(2,1)S(1)} %copy-done.3, f32[16,256]{1,0:T(8,128)S(1)} %fusion.47), kind=kOutput, calls=%fused_computation | convolution fusion | flops 136298496 | bytes 1228800 | tf_op jit(solution)/shard_map/dot_general | solution.py:73
  15.4 0.2 copy.27
  15.6 0.7 %reshape.250 = f32[4,1,128]{2,1,0:T(1,128)} reshape(f32[4,4,4,8]{3,2,1,0:T(4,128)S(1)} %bitcast.145) | data formatting | bytes 4096
  16.2 0.8 %reshape.228 = f32[4,4,8,128]{3,2,1,0:T(8,128)} reshape(f32[4,4,8,4,32]{4,3,2,1,0:T(4,128)S(1)} %multiply_reduce_fusion) | data formatting | bytes 131072 | tf_op jit(solution)/shard_map/reshape | solution.py:82
  17.0 1.9 %all-to-all-done.1 = f32[4,1,128]{2,1,0:T(1,128)S(1)} async-done(((f32[4,1,128]{2,1,0:T(1,128)}), f32[4,1,128]{2,1,0:T(1,128)S(1)}, u32[]{:S(2)}, u32[]{:S(2)}) %all-to-all-start.1) | async-done | bytes 2080 | tf_op jit(solution)/shard_map/all_to_all | solution.py:84
  18.9 3.2 %all-to-all-start.2 = ((f32[4,1,128]{2,1,0:T(1,128)}), f32[4,1,128]{2,1,0:T(1,128)S(1)}, u32[]{:S(2)}, u32[]{:S(2)}) async-start(f32[4,1,128]{2,1,0:T(1,128)} %reshape.250), calls=%async_computation.2 | async-start | bytes 4096 | tf_op jit(solution)/shard_map/all_to_all | solution.py:85
  22.1 0.5 broadcast.137
  22.6 0.7 %reduce.6 = f32[4,128]{1,0:T(4,128)S(1)} reduce(f32[4,1,128]{2,1,0:T(1,128)S(1)} %all-to-all-done.1, f32[]{:T(128)} %broadcast.137), dimensions={1}, to_apply=%all_to_all.10.reduce_sub_computation | reduce | bytes 4100 | tf_op jit(solution)/shard_map/all_to_all | solution.py:84
  23.4 4.1 %all-to-all-done.2 = f32[4,1,128]{2,1,0:T(1,128)S(1)} async-done(((f32[4,1,128]{2,1,0:T(1,128)}), f32[4,1,128]{2,1,0:T(1,128)S(1)}, u32[]{:S(2)}, u32[]{:S(2)}) %all-to-all-start.2) | async-done | bytes 2080 | tf_op jit(solution)/shard_map/all_to_all | solution.py:85
  27.5 3.3 %all-to-all-start = ((f32[4,4,8,128]{3,2,1,0:T(8,128)}), f32[4,4,8,128]{3,2,1,0:T(8,128)S(1)}, u32[]{:S(2)}, u32[]{:S(2)}) async-start(f32[4,4,8,128]{3,2,1,0:T(8,128)} %reshape.228), calls=%async_computation | async-start | bytes 131072 | tf_op jit(solution)/shard_map/all_to_all | solution.py:86
  30.8 0.7 %reduce.7 = f32[4,128]{1,0:T(4,128)S(1)} reduce(f32[4,1,128]{2,1,0:T(1,128)S(1)} %all-to-all-done.2, f32[]{:T(128)} %broadcast.137), dimensions={1}, to_apply=%all_to_all.11.reduce_sub_computation | reduce | bytes 4100 | tf_op jit(solution)/shard_map/all_to_all | solution.py:85
  31.9 0.2 copy.26
  32.1 0.2 broadcast_in_dim.27
  32.3 0.2 broadcast_in_dim.28
  32.5 4.1 %all-to-all-done = f32[4,4,8,128]{3,2,1,0:T(8,128)S(1)} async-done(((f32[4,4,8,128]{3,2,1,0:T(8,128)}), f32[4,4,8,128]{3,2,1,0:T(8,128)S(1)}, u32[]{:S(2)}, u32[]{:S(2)}) %all-to-all-start) | async-done | bytes 65568 | tf_op jit(solution)/shard_map/all_to_all | solution.py:86
  36.5 1.3 %collective-permute-start.1 = (bf16[1,1,8,128]{3,2,1,0:T(8,128)(2,1)S(1)}, bf16[1,1,8,128]{3,2,1,0:T(8,128)(2,1)S(1)}, u32[]{:S(2)}, u32[]{:S(2)}) collective-permute-start(bf16[1,1,8,128]{3,2,1,0:T(8,128)(2,1)S(1)} %get-tuple-element.12), channel_id=1, source_target_pairs={{2,0},{3,1},{6,4},{7,5},{10,8},{11,9},{14,12},{15,13},{18,16},{19,... | collective-permute-start | bytes 6152 | tf_op jit(solution)/shard_map/ppermute | solution.py:21
  37.8 4.5 %collective-permute-start = (bf16[1,1,8,128]{3,2,1,0:T(8,128)(2,1)S(1)}, bf16[1,1,8,128]{3,2,1,0:T(8,128)(2,1)S(1)}, u32[]{:S(2)}, u32[]{:S(2)}) collective-permute-start(bf16[1,1,8,128]{3,2,1,0:T(8,128)(2,1)S(1)} %get-tuple-element.11), channel_id=1, source_target_pairs={{0,2},{1,3},{4,6},{5,7},{8,10},{9,11},{12,14},{13,15},{16,18},{17,... | collective-permute-start | bytes 6152 | tf_op jit(solution)/shard_map/ppermute | solution.py:18
  42.4 1.3 %collective-permute-done = bf16[1,1,8,128]{3,2,1,0:T(8,128)(2,1)S(1)} collective-permute-done((bf16[1,1,8,128]{3,2,1,0:T(8,128)(2,1)S(1)}, bf16[1,1,8,128]{3,2,1,0:T(8,128)(2,1)S(1)}, u32[]{:S(2)}, u32[]{:S(2)}) %collective-permute-start) | collective-permute-done | bytes 2080 | tf_op jit(solution)/shard_map/ppermute | solution.py:18
  43.7 1.8 %all_gather.6 = bf16[1,6,8,256]{3,2,1,0:T(8,128)(2,1)S(1)} all-gather(bf16[1,6,8,128]{3,2,1,0:T(8,128)(2,1)S(1)} %pad_maximum_fusion), channel_id=1, replica_groups=mesh['groups'=2,'date'=4,'tile'=2,'head'=2] {'head'}, dimensions={3}, use_global_device_ids=true | all-gather | bytes 36864 | tf_op jit(solution)/shard_map/all_gather | solution.py:49
  45.8 0.1 convolution_add_fusion.14
  45.9 0.1 convolution_add_fusion.13
  46.0 0.1 convolution_add_fusion.12
  46.2 0.1 convolution_add_fusion.11
  46.3 0.1 convolution_add_fusion.10
  46.5 0.1 convolution_add_fusion.9
  46.6 0.1 fusion.4
  46.7 1.3 %collective-permute-start.3 = (bf16[1,1,8,128]{3,2,1,0:T(8,128)(2,1)S(1)}, bf16[1,1,8,128]{3,2,1,0:T(8,128)(2,1)S(1)}, u32[]{:S(2)}, u32[]{:S(2)}) collective-permute-start(bf16[1,1,8,128]{3,2,1,0:T(8,128)(2,1)S(1)} %get-tuple-element.10), channel_id=1, source_target_pairs={{2,0},{3,1},{6,4},{7,5},{10,8},{11,9},{14,12},{15,13},{18,16},{19,... | collective-permute-start | bytes 6152 | tf_op jit(solution)/shard_map/ppermute | solution.py:21
  48.0 4.5 %collective-permute-start.2 = (bf16[1,1,8,128]{3,2,1,0:T(8,128)(2,1)S(1)}, bf16[1,1,8,128]{3,2,1,0:T(8,128)(2,1)S(1)}, u32[]{:S(2)}, u32[]{:S(2)}) collective-permute-start(bf16[1,1,8,128]{3,2,1,0:T(8,128)(2,1)S(1)} %get-tuple-element.9), channel_id=1, source_target_pairs={{0,2},{1,3},{4,6},{5,7},{8,10},{9,11},{12,14},{13,15},{16,18},{17,... | collective-permute-start | bytes 6152 | tf_op jit(solution)/shard_map/ppermute | solution.py:18
  52.6 1.3 %collective-permute-done.2 = bf16[1,1,8,128]{3,2,1,0:T(8,128)(2,1)S(1)} collective-permute-done((bf16[1,1,8,128]{3,2,1,0:T(8,128)(2,1)S(1)}, bf16[1,1,8,128]{3,2,1,0:T(8,128)(2,1)S(1)}, u32[]{:S(2)}, u32[]{:S(2)}) %collective-permute-start.2) | collective-permute-done | bytes 2080 | tf_op jit(solution)/shard_map/ppermute | solution.py:18
  53.9 1.8 %all_gather.7 = bf16[1,6,8,256]{3,2,1,0:T(8,128)(2,1)S(1)} all-gather(bf16[1,6,8,128]{3,2,1,0:T(8,128)(2,1)S(1)} %pad_maximum_fusion.1), channel_id=1, replica_groups=mesh['groups'=2,'date'=4,'tile'=2,'head'=2] {'head'}, dimensions={3}, use_global_device_ids=true | all-gather | bytes 36864 | tf_op jit(solution)/shard_map/all_gather | solution.py:49
  56.0 0.1 convolution_add_fusion.6
  56.1 0.1 convolution_add_fusion.5
  56.2 0.1 convolution_add_fusion.4
  56.4 0.1 convolution_add_fusion.3
  56.5 0.1 convolution_add_fusion.2
  56.7 0.1 convolution_add_fusion.1
  56.8 0.7 %fusion.3 = bf16[1,4,8,128]{3,2,1,0:T(8,128)(2,1)} fusion(f32[32,128]{1,0:T(8,128)S(1)} %convolution_add_fusion.1, bf16[3,3,256,128]{3,2,1,0:T(8,128)(2,1)S(1)} %copy-done.1, bf16[1,6,8,256]{3,2,1,0:T(8,128)(2,1)S(1)} %all_gather.7), kind=kOutput, calls=%fused_computation.22 | convolution fusion | flops 2105344 | bytes 114688 | tf_op jit(solution)/shard_map/dot_general | solution.py:55
  (30 shorter events, 1.3 us)
Async XLA Ops:
  6.0 7.8 %copy-start.2 = (bf16[256,128]{1,0:T(8,128)(2,1)S(1)}, bf16[256,128]{1,0:T(8,128)(2,1)}, u32[]{:S(2)}) copy-start(bf16[256,128]{1,0:T(8,128)(2,1)} %param.13) | copy-start | bytes 196612
  6.0 7.9 %copy-start.3 = (bf16[4,4,8,16,256]{4,3,2,1,0:T(8,128)(2,1)S(1)}, bf16[4,4,8,16,256]{4,3,2,1,0:T(8,128)(2,1)}, u32[]{:S(2)}) copy-start(bf16[4,4,8,16,256]{4,3,2,1,0:T(8,128)(2,1)} %param.8) | copy-start | bytes 3145732
  7.1 11.8 %all-to-all-start.1 = ((f32[4,1,128]{2,1,0:T(1,128)}), f32[4,1,128]{2,1,0:T(1,128)S(1)}, u32[]{:S(2)}, u32[]{:S(2)}) async-start(f32[4,1,128]{2,1,0:T(1,128)} %reshape.252), calls=%async_computation.1 | async-start | bytes 4096 | tf_op jit(solution)/shard_map/all_to_all | solution.py:84
  15.4 30.1 %copy-start = (bf16[3,3,256,128]{3,2,1,0:T(8,128)(2,1)S(1)}, bf16[3,3,256,128]{3,2,1,0:T(8,128)(2,1)}, u32[]{:S(2)}) copy-start(bf16[3,3,256,128]{3,2,1,0:T(8,128)(2,1)} %param.14) | copy-start | bytes 1769476
  18.9 8.6 %all-to-all-start.2 = ((f32[4,1,128]{2,1,0:T(1,128)}), f32[4,1,128]{2,1,0:T(1,128)S(1)}, u32[]{:S(2)}, u32[]{:S(2)}) async-start(f32[4,1,128]{2,1,0:T(1,128)} %reshape.250), calls=%async_computation.2 | async-start | bytes 4096 | tf_op jit(solution)/shard_map/all_to_all | solution.py:85
  27.5 9.0 %all-to-all-start = ((f32[4,4,8,128]{3,2,1,0:T(8,128)}), f32[4,4,8,128]{3,2,1,0:T(8,128)S(1)}, u32[]{:S(2)}, u32[]{:S(2)}) async-start(f32[4,4,8,128]{3,2,1,0:T(8,128)} %reshape.228), calls=%async_computation | async-start | bytes 131072 | tf_op jit(solution)/shard_map/all_to_all | solution.py:86
  31.9 23.8 %copy-start.1 = (bf16[3,3,256,128]{3,2,1,0:T(8,128)(2,1)S(1)}, bf16[3,3,256,128]{3,2,1,0:T(8,128)(2,1)}, u32[]{:S(2)}) copy-start(bf16[3,3,256,128]{3,2,1,0:T(8,128)(2,1)} %param.15) | copy-start | bytes 1769476
  36.5 5.9 %collective-permute-start.1 = (bf16[1,1,8,128]{3,2,1,0:T(8,128)(2,1)S(1)}, bf16[1,1,8,128]{3,2,1,0:T(8,128)(2,1)S(1)}, u32[]{:S(2)}, u32[]{:S(2)}) collective-permute-start(bf16[1,1,8,128]{3,2,1,0:T(8,128)(2,1)S(1)} %get-tuple-element.12), channel_id=1, source_target_pairs={{2,0},{3,1},{6,4},{7,5},{10,8},{11,9},{14,12},{15,13},{18,16},{19,... | collective-permute-start | bytes 6152 | tf_op jit(solution)/shard_map/ppermute | solution.py:21
  37.8 5.8 %collective-permute-start = (bf16[1,1,8,128]{3,2,1,0:T(8,128)(2,1)S(1)}, bf16[1,1,8,128]{3,2,1,0:T(8,128)(2,1)S(1)}, u32[]{:S(2)}, u32[]{:S(2)}) collective-permute-start(bf16[1,1,8,128]{3,2,1,0:T(8,128)(2,1)S(1)} %get-tuple-element.11), channel_id=1, source_target_pairs={{0,2},{1,3},{4,6},{5,7},{8,10},{9,11},{12,14},{13,15},{16,18},{17,... | collective-permute-start | bytes 6152 | tf_op jit(solution)/shard_map/ppermute | solution.py:18
  46.7 5.9 %collective-permute-start.3 = (bf16[1,1,8,128]{3,2,1,0:T(8,128)(2,1)S(1)}, bf16[1,1,8,128]{3,2,1,0:T(8,128)(2,1)S(1)}, u32[]{:S(2)}, u32[]{:S(2)}) collective-permute-start(bf16[1,1,8,128]{3,2,1,0:T(8,128)(2,1)S(1)} %get-tuple-element.10), channel_id=1, source_target_pairs={{2,0},{3,1},{6,4},{7,5},{10,8},{11,9},{14,12},{15,13},{18,16},{19,... | collective-permute-start | bytes 6152 | tf_op jit(solution)/shard_map/ppermute | solution.py:21
  48.0 5.8 %collective-permute-start.2 = (bf16[1,1,8,128]{3,2,1,0:T(8,128)(2,1)S(1)}, bf16[1,1,8,128]{3,2,1,0:T(8,128)(2,1)S(1)}, u32[]{:S(2)}, u32[]{:S(2)}) collective-permute-start(bf16[1,1,8,128]{3,2,1,0:T(8,128)(2,1)S(1)} %get-tuple-element.9), channel_id=1, source_target_pairs={{0,2},{1,3},{4,6},{5,7},{8,10},{9,11},{12,14},{13,15},{16,18},{17,... | collective-permute-start | bytes 6152 | tf_op jit(solution)/shard_map/ppermute | solution.py:18
where the time goes:
time: 58.1 us; the launch traced here: 57.5 us
  starting transfers between devices  24.5 us (42%)
  waiting for transfers between devices  12.6 us (22%)
  matrix products  7.09 us (12%)
  local copies, waits for them, and re-layouts  5.82 us (10%)
  other arithmetic  3.7 us (6%)
  blocking collectives  3.62 us (6%)
    ppermute x2, starting transfers between devices, with_halo(): lax.ppermute(lax.slice_in_dim(block, block.shape[dim] - width, None, axis...  9.08 us
    all_to_all x1, starting transfers between devices, local(): lax.all_to_all(top, 'date', split_axis=0, concat_axis=0, tiled=True)  6.32 us
    all_to_all x1, waiting for transfers between devices, local(): lax.all_to_all(totals, 'date', split_axis=0, concat_axis=0, tiled=True)  4.08 us
    all_to_all x1, waiting for transfers between devices, local(): lax.all_to_all(sums, 'date', split_axis=0, concat_axis=0, tiled=True)  4.05 us
    all_gather x2, blocking collectives, convolve(): whole = lax.all_gather(padded, 'head', axis=3, tiled=True)  3.62 us
    all_to_all x1, starting transfers between devices, local(): lax.all_to_all(sums, 'date', split_axis=0, concat_axis=0, tiled=True)  3.28 us
    all_to_all x1, starting transfers between devices, local(): lax.all_to_all(totals, 'date', split_axis=0, concat_axis=0, tiled=True)  3.2 us
    dot_general x18, matrix products, convolve(): jnp.dot(piece, kernel[arow, bcol], preferred_element_type=jnp.float32)  3.05 us
  transfers between devices with their start and end apart: 7, of which 5 were waited for; matrix products, arithmetic and copies ran while one was open for 11% of the time, Pallas kernels for 0%

commit v1 on v0

v1 whole, which is shorter than its diff:
```python
import functools

import jax
import jax.numpy as jnp
from jax import lax
from jax.experimental import pallas as pl
from jax.experimental.pallas import tpu as pltpu
from jax.sharding import PartitionSpec as P

HSIZE = 32
LANES = 128
PENALTY = 6.0
F32 = jnp.float32
BF16 = jnp.bfloat16


def encoding(day_of_year, width):
    chan = jnp.arange(width)
    expo = (2 * (chan // 2)).astype(F32) / width
    freq = jnp.power(F32(1000.0), -expo)
    angle = day_of_year.astype(F32)[:, None] * freq[None, :]
    return jnp.where((chan % 2 == 0)[None, :], jnp.sin(angle), jnp.cos(angle))


def iota(shape, dim):
    return lax.broadcasted_iota(jnp.int32, shape, dim)


def split3(value):
    high = value.astype(BF16)
    rest = value - high.astype(F32)
    mid = rest.astype(BF16)
    low = (rest - mid.astype(F32)).astype(BF16)
    return high, mid, low


def same_head(rows):
    row = lax.rem(iota((rows, LANES), 0), LANES)
    return (row // HSIZE == iota((rows, LANES), 1) // HSIZE).astype(BF16)


def dot(a, b):
    return jnp.dot(a, b, preferred_element_type=F32)


def attend_kernel(
    pixels, dates, copies, tokens, mask, table, query, keyw, valw, out, weights, score, vals
):
    @pl.when(pl.program_id(0) == 0)
    def _():
        scaled = keyw[...].astype(F32) * (query[...] * F32(HSIZE**-0.5))
        spread = same_head(LANES)
        high, mid, low = split3(scaled)
        folded = dot(high, spread) + (dot(mid, spread) + dot(low, spread))
        high, mid, low = split3(folded)
        weights[:, 0:LANES] = high
        weights[:, LANES : 2 * LANES] = mid
        weights[:, 2 * LANES : 3 * LANES] = low
        weights[:, 3 * LANES : 4 * LANES] = valw[...]

    width = tokens.shape[-1]
    feats = tokens[...].reshape(pixels, dates, width).astype(F32) + table[...][None]
    inputs = feats.astype(BF16).reshape(pixels * dates, width)
    both = dot(inputs, weights[...])
    score[...] = both[:, 0:LANES] + (both[:, LANES : 2 * LANES] + both[:, 2 * LANES : 3 * LANES])
    vals[...] = both[:, 3 * LANES : 4 * LANES]
    clear = mask[...].reshape(pixels, dates).astype(F32)
    cloud = PENALTY * (1.0 - clear)
    rows = [
        score[pl.ds(t, pixels, stride=dates), :] - cloud[:, t : t + 1] for t in range(dates)
    ]
    top = functools.reduce(jnp.maximum, rows)
    total = jnp.zeros((pixels, LANES), F32)
    summed = jnp.zeros((pixels, LANES), F32)
    for t in range(dates):
        expo = jnp.exp(rows[t] - top)
        total = total + expo
        summed = summed + expo * vals[pl.ds(t, pixels, stride=dates), :]
    part = (summed / total).astype(BF16)
    level = top + jnp.log(total)
    own = lax.rem(iota((pixels, LANES), 1), HSIZE) == iota((pixels, LANES), 0)
    packed = jnp.sum(jnp.where(own, level, 0.0), axis=0, keepdims=True)
    high, mid, low = split3(packed)
    row = iota((16, LANES), 0)
    tail = jnp.where(
        row == 0,
        high.astype(F32),
        jnp.where(row == 1, mid.astype(F32), jnp.where(row == 2, low.astype(F32), 0.0)),
    ).astype(BF16)
    for copy in range(copies):
        out[0, copy, 0:pixels, :] = part
        out[0, copy, pixels : pixels + 16, :] = tail


def attend(tokens, cloud_mask, table, query, key_weight, value_weight, copies):
    tiles, rows, cols, dates, width = tokens.shape
    pixels = rows * cols
    tokens = tokens.reshape(tiles, pixels * dates, width)
    mask = cloud_mask.reshape(tiles, pixels, dates)
    whole = lambda *shape: pl.BlockSpec(shape, lambda i: (0,) * len(shape))
    return pl.pallas_call(
        functools.partial(attend_kernel, pixels, dates, copies),
        grid=(tiles,),
        in_specs=[
            pl.BlockSpec((1, pixels * dates, width), lambda i: (i, 0, 0)),
            pl.BlockSpec((1, pixels, dates), lambda i: (i, 0, 0)),
            whole(dates, width),
            whole(1, LANES),
            whole(width, LANES),
            whole(width, LANES),
        ],
        out_specs=pl.BlockSpec((1, copies, pixels + 16, LANES), lambda i: (i, 0, 0, 0)),
        out_shape=jax.ShapeDtypeStruct((tiles, copies, pixels + 16, LANES), BF16),
        scratch_shapes=[
            pltpu.VMEM((width, 4 * LANES), BF16),
            pltpu.VMEM((pixels * dates, LANES), F32),
            pltpu.VMEM((pixels * dates, LANES), F32),
        ],
        compiler_params=pltpu.CompilerParams(vmem_limit_bytes=16 * 2**20),
    )(tokens, mask, table, query.reshape(1, LANES), key_weight, value_weight)


def merge(blocks, pixels, first, count):
    levels = [jnp.sum(block[pixels : pixels + 16, :].astype(F32), axis=0, keepdims=True) for block in blocks]
    best = functools.reduce(jnp.maximum, levels)
    shares = [jnp.exp(level - best) for level in levels]
    total = functools.reduce(jnp.add, shares)
    own = lax.rem(iota((count, LANES), 1), HSIZE) == iota((count, LANES), 0) + first
    spread = same_head(2 * LANES)
    pooled = jnp.zeros((count, LANES), F32)
    for block, share in zip(blocks, shares):
        share = share / total
        high = share.astype(BF16).astype(F32)
        both = jnp.concatenate([jnp.where(own, high, 0.0), jnp.where(own, share - high, 0.0)], axis=1)
        pooled = pooled + dot(both.astype(BF16), spread) * block[first : first + count, :].astype(F32)
    return pooled.astype(BF16).astype(F32)


def columns(field, cols):
    count = field.shape[0]
    col = lax.rem(iota(field.shape, 0), cols)
    left = jnp.where(col == 0, 0.0, pltpu.roll(field, 1, 0))
    right = jnp.where(col == cols - 1, 0.0, pltpu.roll(field, count - 1, 0))
    return jnp.concatenate([left, field, right], axis=1).astype(BF16)


def stencil(field, kernel, cols):
    count = field.shape[0] - 2 * cols
    return sum(dot(field, kernel[a])[a * cols : a * cols + count] for a in range(3))


def convolve_kernel(pixels, cols, place, got, first, other, second, out):
    dates, slabs, heads = got.shape[:3]
    slab, head = place[0], place[1]
    above, below = jnp.maximum(slab - 1, 0), jnp.minimum(slab + 1, slabs - 1)
    halo = 2 * cols

    def region(source, start, count):
        return jnp.concatenate(
            [merge([got[d, source, h] for d in range(dates)], pixels, start, count) for h in range(heads)],
            axis=1,
        )

    field = jnp.concatenate(
        [
            jnp.where(slab > 0, region(above, pixels - halo, halo), 0.0),
            region(slab, 0, pixels),
            jnp.where(slab < slabs - 1, region(below, 0, halo), 0.0),
        ],
        axis=0,
    )
    wide = columns(field, cols)
    mine = stencil(wide, first, cols)
    theirs = stencil(wide, other, cols)
    hidden = jnp.concatenate(
        [jnp.where(head == 0, mine, theirs), jnp.where(head == 0, theirs, mine)], axis=1
    )
    count = pixels + 2 * cols
    row = iota(hidden.shape, 0)
    inside = jnp.logical_and(
        jnp.logical_or(row >= cols, slab > 0), jnp.logical_or(row < count - cols, slab < slabs - 1)
    )
    hidden = jnp.where(inside, jnp.maximum(hidden, 0.0), 0.0).astype(BF16).astype(F32)
    out[...] = stencil(columns(hidden, cols), second, cols).astype(BF16)


def convolve(got, place, first, other, second, pixels, cols):
    return pl.pallas_call(
        functools.partial(convolve_kernel, pixels, cols),
        in_specs=[pl.BlockSpec(memory_space=pltpu.SMEM)] + [pl.BlockSpec(memory_space=pltpu.VMEM)] * 4,
        out_specs=pl.BlockSpec(memory_space=pltpu.VMEM),
        out_shape=jax.ShapeDtypeStruct((pixels, second.shape[-1]), BF16),
        compiler_params=pltpu.CompilerParams(vmem_limit_bytes=32 * 2**20),
    )(place, got, first, other, second)


def local(slabs, heads, tokens, cloud_mask, day_of_year, query, key_weight, value_weight, conv_first, conv_second):
    tiles, rows, cols, dates, width = tokens.shape
    pixels = rows * cols
    first = conv_first.reshape(3, 3 * width, -1)
    second = conv_second.reshape(3, 3 * width, -1)
    other = lax.ppermute(first, "head", [(i, heads - 1 - i) for i in range(heads)])
    table = encoding(day_of_year, width)
    sent = attend(tokens, cloud_mask, table, query, key_weight, value_weight, slabs * heads)
    got = lax.all_to_all(
        sent.reshape(tiles * slabs * heads, pixels + 16, LANES),
        ("date", "tile", "head"),
        split_axis=0,
        concat_axis=0,
        tiled=True,
    ).reshape(tiles, slabs, heads, pixels + 16, LANES)
    place = jnp.stack([lax.axis_index("tile"), lax.axis_index("head")]).astype(jnp.int32)
    out = convolve(got, place, first, other, second, pixels, cols)
    return out.reshape(1, rows, cols, -1)


def solution(mesh):
    in_specs = (
        P("groups", "tile", None, "date", None),
        P("groups", "tile", None, "date"),
        P(("groups", "date")),
        P("head"),
        P(None, "head"),
        P(None, "head"),
        P(None, None, None, "head"),
        P(None, None, None, "head"),
    )
    out_specs = P(("groups", "date"), "tile", None, "head")
    body = functools.partial(local, mesh.shape["tile"], mesh.shape["head"])
    return jax.shard_map(body, mesh=mesh, in_specs=in_specs, out_specs=out_specs, check_vma=False)
```

time: 58.1 us -> 26.8 us (0.46)
  starting transfers between devices: 24.5 us -> 7.47 us
  matrix products: 7.09 us -> 0 us
  Pallas kernels: 0 us -> 4.74 us
  waiting for transfers between devices: 12.6 us -> 8.92 us
  blocking collectives: 3.62 us -> 0 us
  other arithmetic: 3.7 us -> 0.24 us
  local copies, waits for them, and re-layouts: 5.82 us -> 5.05 us
    ppermute x4 -> x1, starting transfers between devices: 11.7 us -> 0.45 us  [local(): lax.ppermute(first, 'head', [(i, heads - 1 - i) for i in range(heads)])]
    dot_general x20 -> x0, matrix products: 7.09 us -> none  [the longest x18 3.05 us: convolve(): jnp.dot(piece, kernel[arow, bcol], preferred_element_type=jnp.float32)]
    all_to_all x3 -> x1, starting transfers between devices: 12.8 us -> 7.02 us  [local(): lax.all_to_all(sent.reshape(tiles * slabs * heads, pixels + 16, LANES), (...]
    pallas_call x0 -> x2, Pallas kernels: none -> 4.74 us  [the longest x1 2.74 us: attend(): pl.pallas_call(functools.partial(attend_kernel, pixels, dates, copies), g...]
    all_gather x2 -> x0, blocking collectives: 3.62 us -> none  [convolve(): whole = lax.all_gather(padded, 'head', axis=3, tiled=True)]
    ppermute x4 -> x1, waiting for transfers between devices: 2.57 us -> 0.01 us  [local(): lax.ppermute(first, 'head', [(i, heads - 1 - i) for i in range(heads)])]
    unnamed x14 -> x16, local copies, waits for them, and re-layouts: 2.64 us -> 5.05 us
    all_to_all x2 -> x0, other arithmetic: 1.33 us -> none  [the longest x1 0.67 us: local(): lax.all_to_all(totals, 'date', split_axis=0, concat_axis=0, tiled=True)]
  transfers between devices with their start and end apart: 7 -> 2, of which waited for: 5 -> 1; matrix products, arithmetic and copies ran while one was open for 11% -> 1% of each run, Pallas kernels for 0% -> 10%
where the time goes in v1:
time: 26.8 us; the launch traced here: 26.4 us
  waiting for transfers between devices  8.92 us (33%)
  starting transfers between devices  7.47 us (28%)
  local copies, waits for them, and re-layouts  5.05 us (19%)
  Pallas kernels  4.74 us (18%)
    all_to_all x1, waiting for transfers between devices, local(): lax.all_to_all(sent.reshape(tiles * slabs * heads, pixels + 16, LANES), (...  8.91 us
    all_to_all x1, starting transfers between devices, local(): lax.all_to_all(sent.reshape(tiles * slabs * heads, pixels + 16, LANES), (...  7.02 us
    unnamed x16, local copies, waits for them, and re-layouts  5.05 us
    pallas_call x1, Pallas kernels, attend(): pl.pallas_call(functools.partial(attend_kernel, pixels, dates, copies), g...  2.74 us
    pallas_call x1, Pallas kernels, convolve(): pl.pallas_call(functools.partial(convolve_kernel, pixels, cols), in_specs...  2 us
  transfers between devices with their start and end apart: 2, of which 1 were waited for; matrix products, arithmetic and copies ran while one was open for 1% of the time, Pallas kernels for 10%

profile of v1, /device:TPU:0, one launch (start us, length us, event | category | flops | bytes accessed | tf_op | source)
XLA Modules:
  0.0 26.4 jit_solution(15292326624305894077)
XLA Ops:
  0.0 0.5 %collective-permute-start = (bf16[3,768,128]{2,1,0:T(8,128)(2,1)}, bf16[3,768,128]{2,1,0:T(8,128)(2,1)S(1)}, u32[]{:S(2)}, u32[]{:S(2)}) collective-permute-start(bf16[3,768,128]{2,1,0:T(8,128)(2,1)} %bitcast.12), channel_id=1, source_target_pairs={{0,1},{1,0},{2,3},{3,2},{4,5},{5,4},{6,7},{7,6},{8,9},{9,8},{10,11... | collective-permute-start | bytes 1769480 | tf_op jit(solution)/shard_map/ppermute | solution.py:202
  0.5 0.0 copy-start.7
  0.5 0.6 %copy-done.7 = s32[16]{0:T(128)S(1)} copy-done((s32[16]{0:T(128)S(1)}, s32[16]{0:T(128)}, u32[]{:S(2)}) %copy-start.7) | copy-done | bytes 88
  1.1 0.1 fusion.table
  1.3 0.0 copy-start.6
  1.3 0.6 %copy-done.6 = f32[128]{0:T(128)S(1)} copy-done((f32[128]{0:T(128)S(1)}, f32[128]{0:T(128)}, u32[]{:S(2)}) %copy-start.6) | copy-done | bytes 536
  1.9 0.0 copy-start
  1.9 1.2 %copy-done = bf16[4,4,8,16,256]{4,3,2,1,0:T(8,128)(2,1)S(1)} copy-done((bf16[4,4,8,16,256]{4,3,2,1,0:T(8,128)(2,1)S(1)}, bf16[4,4,8,16,256]{4,3,2,1,0:T(8,128)(2,1)}, u32[]{:S(2)}) %copy-start) | copy-done | bytes 1048600
  3.2 0.0 copy-start.3
  3.2 0.8 %copy-done.3 = s32[4,4,8,16]{3,2,1,0:T(8,128)S(1)} copy-done((s32[4,4,8,16]{3,2,1,0:T(8,128)S(1)}, s32[4,4,8,16]{3,2,1,0:T(8,128)}, u32[]{:S(2)}) %copy-start.3) | copy-done | bytes 8216
  4.0 0.0 copy-start.4
  4.0 0.8 %copy-done.4 = bf16[256,128]{1,0:T(8,128)(2,1)S(1)} copy-done((bf16[256,128]{1,0:T(8,128)(2,1)S(1)}, bf16[256,128]{1,0:T(8,128)(2,1)}, u32[]{:S(2)}) %copy-start.4) | copy-done | bytes 65560
  4.8 0.0 copy-start.5
  4.8 0.8 %copy-done.5 = bf16[256,128]{1,0:T(8,128)(2,1)S(1)} copy-done((bf16[256,128]{1,0:T(8,128)(2,1)S(1)}, bf16[256,128]{1,0:T(8,128)(2,1)}, u32[]{:S(2)}) %copy-start.5) | copy-done | bytes 65560
  5.7 0.0 copy-start.1
  5.7 0.0 copy-start.2
  5.7 2.7 %shard_map.82 = bf16[4,4,48,128]{3,2,1,0:T(8,128)(2,1)} custom-call(bf16[4,512,256]{2,1,0:T(8,128)(2,1)S(1)} %bitcast.10, s32[4,32,16]{2,1,0:T(8,128)S(1)} %bitcast.15, f32[16,256]{1,0:T(8,128)S(1)} %fusion.table, f32[1,128]{1,0:T(1,128)S(1)} %bitcast.16, bf16[256,128]{1,0:T(8,128)(2,1)S(1)} %copy-done.4, bf16[256,128]{1,0:T(8,128)(2,1)S(1)} %copy-done.5), custom_call_target="tpu_custom_call" | custom-call | tf_op jit(solution)/shard_map/pallas_call | solution.py:101
  8.4 7.0 %all-to-all-start = ((bf16[16,48,128]{2,1,0:T(8,128)(2,1)}), bf16[16,48,128]{2,1,0:T(8,128)(2,1)S(1)}, u32[]{:S(2)}, u32[]{:S(2)}) async-start(bf16[16,48,128]{2,1,0:T(8,128)(2,1)} %bitcast.5), calls=%async_computation | async-start | bytes 393216 | tf_op jit(solution)/shard_map/all_to_all | solution.py:205
  15.4 0.1 pad_add_fusion.place
  15.5 8.9 %all-to-all-done = bf16[16,48,128]{2,1,0:T(8,128)(2,1)S(1)} async-done(((bf16[16,48,128]{2,1,0:T(8,128)(2,1)}), bf16[16,48,128]{2,1,0:T(8,128)(2,1)S(1)}, u32[]{:S(2)}, u32[]{:S(2)}) %all-to-all-start) | async-done | bytes 196640 | tf_op jit(solution)/shard_map/all_to_all | solution.py:205
  24.4 0.0 collective-permute-done.other
  24.4 0.0 copy-done.1
  24.4 0.0 copy-done.2
  24.4 2.0 %shard_map.83 = bf16[32,128]{1,0:T(8,128)(2,1)} custom-call(s32[2]{0:T(128)S(1)} %pad_add_fusion.place, bf16[4,2,2,48,128]{4,3,2,1,0:T(8,128)(2,1)S(1)} %bitcast.11, bf16[3,768,128]{2,1,0:T(8,128)(2,1)S(1)} %bitcast.13, bf16[3,768,128]{2,1,0:T(8,128)(2,1)S(1)} %collective-permute-done.other, bf16[3,768,128]{2,1,0:T(8,128)(2,1)S(1)} %bitcast.14), custom_call_target="tpu_custom_call" | custom-call | tf_op jit(solution)/shard_map/pallas_call | solution.py:188
  (3 shorter events, 0.0 us)
Async XLA Ops:
  0.0 24.4 %collective-permute-start = (bf16[3,768,128]{2,1,0:T(8,128)(2,1)}, bf16[3,768,128]{2,1,0:T(8,128)(2,1)S(1)}, u32[]{:S(2)}, u32[]{:S(2)}) collective-permute-start(bf16[3,768,128]{2,1,0:T(8,128)(2,1)} %bitcast.12), channel_id=1, source_target_pairs={{0,1},{1,0},{2,3},{3,2},{4,5},{5,4},{6,7},{7,6},{8,9},{9,8},{10,11... | collective-permute-start | bytes 1769480 | tf_op jit(solution)/shard_map/ppermute | solution.py:202
  0.5 0.7 %copy-start.7 = (s32[16]{0:T(128)S(1)}, s32[16]{0:T(128)}, u32[]{:S(2)}) copy-start(s32[16]{0:T(128)} %param.10) | copy-start | bytes 196
  1.3 0.7 %copy-start.6 = (f32[128]{0:T(128)S(1)}, f32[128]{0:T(128)}, u32[]{:S(2)}) copy-start(f32[128]{0:T(128)} %param.11) | copy-start | bytes 1540
  1.9 1.2 %copy-start = (bf16[4,4,8,16,256]{4,3,2,1,0:T(8,128)(2,1)S(1)}, bf16[4,4,8,16,256]{4,3,2,1,0:T(8,128)(2,1)}, u32[]{:S(2)}) copy-start(bf16[4,4,8,16,256]{4,3,2,1,0:T(8,128)(2,1)} %param.8) | copy-start | bytes 3145732
  3.2 0.8 %copy-start.3 = (s32[4,4,8,16]{3,2,1,0:T(8,128)S(1)}, s32[4,4,8,16]{3,2,1,0:T(8,128)}, u32[]{:S(2)}) copy-start(s32[4,4,8,16]{3,2,1,0:T(8,128)} %param.9) | copy-start | bytes 24580
  4.0 0.8 %copy-start.4 = (bf16[256,128]{1,0:T(8,128)(2,1)S(1)}, bf16[256,128]{1,0:T(8,128)(2,1)}, u32[]{:S(2)}) copy-start(bf16[256,128]{1,0:T(8,128)(2,1)} %keyw.1) | copy-start | bytes 196612
  4.8 0.8 %copy-start.5 = (bf16[256,128]{1,0:T(8,128)(2,1)S(1)}, bf16[256,128]{1,0:T(8,128)(2,1)}, u32[]{:S(2)}) copy-start(bf16[256,128]{1,0:T(8,128)(2,1)} %valw.1) | copy-start | bytes 196612
  5.7 18.8 %copy-start.1 = (bf16[3,3,256,128]{3,2,1,0:T(8,128)(2,1)S(1)}, bf16[3,3,256,128]{3,2,1,0:T(8,128)(2,1)}, u32[]{:S(2)}) copy-start(bf16[3,3,256,128]{3,2,1,0:T(8,128)(2,1)} %param.14) | copy-start | bytes 1769476
  5.7 18.8 %copy-start.2 = (bf16[3,3,256,128]{3,2,1,0:T(8,128)(2,1)S(1)}, bf16[3,3,256,128]{3,2,1,0:T(8,128)(2,1)}, u32[]{:S(2)}) copy-start(bf16[3,3,256,128]{3,2,1,0:T(8,128)(2,1)} %param.15) | copy-start | bytes 1769476
  8.4 16.0 %all-to-all-start = ((bf16[16,48,128]{2,1,0:T(8,128)(2,1)}), bf16[16,48,128]{2,1,0:T(8,128)(2,1)S(1)}, u32[]{:S(2)}, u32[]{:S(2)}) async-start(bf16[16,48,128]{2,1,0:T(8,128)(2,1)} %bitcast.5), calls=%async_computation | async-start | bytes 393216 | tf_op jit(solution)/shard_map/all_to_all | solution.py:205

commit v2 on v1

v2 whole, which is shorter than its diff:
```python
import functools
import math

import jax
import jax.numpy as jnp
from jax import lax
from jax.experimental import pallas as pl
from jax.experimental.pallas import tpu as pltpu
from jax.sharding import PartitionSpec as P

HSIZE = 32
LANES = 128
PENALTY = 6.0
F32 = jnp.float32
BF16 = jnp.bfloat16


def iota(shape, dim):
    return lax.broadcasted_iota(jnp.int32, shape, dim)


def split3(value):
    high = value.astype(BF16)
    rest = value - high.astype(F32)
    mid = rest.astype(BF16)
    low = (rest - mid.astype(F32)).astype(BF16)
    return high, mid, low


def same_head(rows):
    row = lax.rem(iota((rows, LANES), 0), LANES)
    return (row // HSIZE == iota((rows, LANES), 1) // HSIZE).astype(BF16)


def dot(a, b):
    return jnp.dot(a, b, preferred_element_type=F32)


def encoding_rows(days, dates, width):
    row, chan = iota((dates, width), 0), iota((dates, width), 1)
    even = lax.rem(chan, 2) == 0
    expo = (chan - lax.rem(chan, 2)).astype(F32) * F32(math.log(1000.0) / width)
    day = jnp.zeros((dates, width), F32)
    for t in range(dates):
        day = jnp.where(row == t, days[t].astype(F32), day)
    angle = day * jnp.exp(-expo)
    return jnp.where(even, jnp.sin(angle), jnp.cos(angle))


def attend_kernel(
    pixels, dates, copies, tokens_hbm, mask_hbm, days_hbm, query_hbm, keyw_hbm, valw_hbm, out,
    tokens, mask, days, query, keyw, weights, score, vals, sems, token_sems,
):
    tiles, width = tokens.shape[0], tokens.shape[-1]
    columns = pl.ds(3 * LANES, LANES)
    small = [
        pltpu.make_async_copy(days_hbm, days, sems.at[0]),
        pltpu.make_async_copy(query_hbm, query, sems.at[1]),
        pltpu.make_async_copy(keyw_hbm, keyw, sems.at[2]),
        pltpu.make_async_copy(valw_hbm, weights.at[:, columns], sems.at[3]),
        pltpu.make_async_copy(mask_hbm, mask, sems.at[4]),
    ]
    for copy in small:
        copy.start()
    loads = lambda i: pltpu.make_async_copy(tokens_hbm.at[i], tokens.at[i], token_sems.at[i])
    for i in range(tiles):
        loads(i).start()
    small[0].wait()
    table = encoding_rows(days, dates, width)
    small[1].wait()
    small[2].wait()
    scaled = keyw[...].astype(F32) * (query[...] * F32(HSIZE**-0.5))
    spread = same_head(LANES)
    high, mid, low = split3(scaled)
    folded = dot(high, spread) + (dot(mid, spread) + dot(low, spread))
    high, mid, low = split3(folded)
    weights[:, 0:LANES] = high
    weights[:, LANES : 2 * LANES] = mid
    weights[:, 2 * LANES : 3 * LANES] = low
    small[3].wait()
    small[4].wait()

    def one(i):
        loads(i).wait()
        feats = tokens[i].reshape(pixels, dates, width).astype(F32) + table[None]
        inputs = feats.astype(BF16).reshape(pixels * dates, width)
        both = dot(inputs, weights[...])
        score[...] = both[:, 0:LANES] + (both[:, LANES : 2 * LANES] + both[:, 2 * LANES : 3 * LANES])
        vals[...] = both[:, 3 * LANES : 4 * LANES]
        cloud = PENALTY * (1.0 - mask[i].astype(F32))
        rows = [
            score[pl.ds(t, pixels, stride=dates), :] - cloud[:, t : t + 1] for t in range(dates)
        ]
        top = functools.reduce(jnp.maximum, rows)
        total = jnp.zeros((pixels, LANES), F32)
        summed = jnp.zeros((pixels, LANES), F32)
        for t in range(dates):
            expo = jnp.exp(rows[t] - top)
            total = total + expo
            summed = summed + expo * vals[pl.ds(t, pixels, stride=dates), :]
        part = (summed / total).astype(BF16)
        level = top + jnp.log(total)
        own = lax.rem(iota((pixels, LANES), 1), HSIZE) == iota((pixels, LANES), 0)
        packed = jnp.sum(jnp.where(own, level, 0.0), axis=0, keepdims=True)
        high, mid, low = split3(packed)
        row = iota((16, LANES), 0)
        tail = jnp.where(
            row == 0,
            high.astype(F32),
            jnp.where(row == 1, mid.astype(F32), jnp.where(row == 2, low.astype(F32), 0.0)),
        ).astype(BF16)
        for copy in range(copies):
            out[i, copy, 0:pixels, :] = part
            out[i, copy, pixels : pixels + 16, :] = tail

    if tiles <= 4:
        for i in range(tiles):
            one(i)
    else:
        pl.loop(0, tiles)(one)


def attend(tokens, cloud_mask, day_of_year, query, key_weight, value_weight, copies):
    tiles, rows, cols, dates, width = tokens.shape
    pixels = rows * cols
    tokens = tokens.reshape(tiles, pixels * dates, width)
    mask = cloud_mask.reshape(tiles, pixels, dates)
    return pl.pallas_call(
        functools.partial(attend_kernel, pixels, dates, copies),
        in_specs=[pl.BlockSpec(memory_space=pltpu.HBM)] * 6,
        out_specs=pl.BlockSpec(memory_space=pltpu.VMEM),
        out_shape=jax.ShapeDtypeStruct((tiles, copies, pixels + 16, LANES), BF16),
        scratch_shapes=[
            pltpu.VMEM(tokens.shape, BF16),
            pltpu.VMEM(mask.shape, jnp.int32),
            pltpu.SMEM(day_of_year.shape, jnp.int32),
            pltpu.VMEM((1, LANES), F32),
            pltpu.VMEM((width, LANES), BF16),
            pltpu.VMEM((width, 4 * LANES), BF16),
            pltpu.VMEM((pixels * dates, LANES), F32),
            pltpu.VMEM((pixels * dates, LANES), F32),
            pltpu.SemaphoreType.DMA((5,)),
            pltpu.SemaphoreType.DMA((tiles,)),
        ],
        compiler_params=pltpu.CompilerParams(vmem_limit_bytes=60 * 2**20),
    )(tokens, mask, day_of_year, query.reshape(1, LANES), key_weight, value_weight)


def merge(blocks, pixels, first, count):
    levels = [jnp.sum(block[pixels : pixels + 16, :].astype(F32), axis=0, keepdims=True) for block in blocks]
    best = functools.reduce(jnp.maximum, levels)
    shares = [jnp.exp(level - best) for level in levels]
    total = functools.reduce(jnp.add, shares)
    own = lax.rem(iota((count, LANES), 1), HSIZE) == iota((count, LANES), 0) + first
    spread = same_head(2 * LANES)
    pooled = jnp.zeros((count, LANES), F32)
    for block, share in zip(blocks, shares):
        share = share / total
        high = share.astype(BF16).astype(F32)
        both = jnp.concatenate([jnp.where(own, high, 0.0), jnp.where(own, share - high, 0.0)], axis=1)
        pooled = pooled + dot(both.astype(BF16), spread) * block[first : first + count, :].astype(F32)
    return pooled.astype(BF16).astype(F32)


def columns(field, cols):
    count = field.shape[0]
    col = lax.rem(iota(field.shape, 0), cols)
    left = jnp.where(col == 0, 0.0, pltpu.roll(field, 1, 0))
    right = jnp.where(col == cols - 1, 0.0, pltpu.roll(field, count - 1, 0))
    return jnp.concatenate([left, field, right], axis=1).astype(BF16)


def stencil(field, kernel, cols):
    count = field.shape[0] - 2 * cols
    return sum(dot(field, kernel[a])[a * cols : a * cols + count] for a in range(3))


def convolve_kernel(pixels, cols, place, got, swapped, first, other, second, out):
    dates, slabs = got.shape[:2]
    slab, head = place[0], place[1]
    above, below = jnp.maximum(slab - 1, 0), jnp.minimum(slab + 1, slabs - 1)
    halo = 2 * cols

    def in_order(mine, theirs):
        return jnp.concatenate(
            [jnp.where(head == 0, mine, theirs), jnp.where(head == 0, theirs, mine)], axis=1
        )

    def region(source, start, count):
        mine, theirs = (
            merge([half[d, source] for d in range(dates)], pixels, start, count) for half in (got, swapped)
        )
        return in_order(mine, theirs)

    field = jnp.concatenate(
        [
            jnp.where(slab > 0, region(above, pixels - halo, halo), 0.0),
            region(slab, 0, pixels),
            jnp.where(slab < slabs - 1, region(below, 0, halo), 0.0),
        ],
        axis=0,
    )
    wide = columns(field, cols)
    mine = stencil(wide, first, cols)
    theirs = stencil(wide, other, cols)
    hidden = in_order(mine, theirs)
    count = pixels + 2 * cols
    row = iota(hidden.shape, 0)
    inside = jnp.logical_and(
        jnp.logical_or(row >= cols, slab > 0), jnp.logical_or(row < count - cols, slab < slabs - 1)
    )
    hidden = jnp.where(inside, jnp.maximum(hidden, 0.0), 0.0).astype(BF16).astype(F32)
    out[...] = stencil(columns(hidden, cols), second, cols).astype(BF16)


def convolve(got, swapped, place, first, other, second, pixels, cols):
    return pl.pallas_call(
        functools.partial(convolve_kernel, pixels, cols),
        in_specs=[pl.BlockSpec(memory_space=pltpu.SMEM)] + [pl.BlockSpec(memory_space=pltpu.VMEM)] * 5,
        out_specs=pl.BlockSpec(memory_space=pltpu.VMEM),
        out_shape=jax.ShapeDtypeStruct((pixels, second.shape[-1]), BF16),
        compiler_params=pltpu.CompilerParams(vmem_limit_bytes=32 * 2**20),
    )(place, got, swapped, first, other, second)


def local(slabs, heads, tokens, cloud_mask, day_of_year, query, key_weight, value_weight, conv_first, conv_second):
    tiles, rows, cols, dates, width = tokens.shape
    pixels = rows * cols
    first = conv_first.reshape(3, 3 * width, -1)
    second = conv_second.reshape(3, 3 * width, -1)
    swap = [(i, heads - 1 - i) for i in range(heads)]
    other = lax.ppermute(first, "head", swap)
    sent = attend(tokens, cloud_mask, day_of_year, query, key_weight, value_weight, slabs)
    got = lax.all_to_all(
        sent.reshape(tiles * slabs, pixels + 16, LANES),
        ("date", "tile"),
        split_axis=0,
        concat_axis=0,
        tiled=True,
    ).reshape(tiles, slabs, pixels + 16, LANES)
    swapped = lax.ppermute(got, "head", swap)
    place = jnp.stack([lax.axis_index("tile"), lax.axis_index("head")]).astype(jnp.int32)
    out = convolve(got, swapped, place, first, other, second, pixels, cols)
    return out.reshape(1, rows, cols, -1)


def solution(mesh):
    in_specs = (
        P("groups", "tile", None, "date", None),
        P("groups", "tile", None, "date"),
        P(("groups", "date")),
        P("head"),
        P(None, "head"),
        P(None, "head"),
        P(None, None, None, "head"),
        P(None, None, None, "head"),
    )
    out_specs = P(("groups", "date"), "tile", None, "head")
    body = functools.partial(local, mesh.shape["tile"], mesh.shape["head"])
    return jax.shard_map(body, mesh=mesh, in_specs=in_specs, out_specs=out_specs, check_vma=False)
```

time: 26.8 us -> 21.7 us (0.81)
  local copies, waits for them, and re-layouts: 5.05 us -> 0.01 us
  Pallas kernels: 4.74 us -> 5.68 us
  waiting for transfers between devices: 8.92 us -> 8.39 us
    unnamed x16 -> x4, local copies, waits for them, and re-layouts: 5.05 us -> 0.01 us
    all_to_all x1, waiting for transfers between devices: 8.91 us -> 7.16 us  [local(): lax.all_to_all(sent.reshape(tiles * slabs, pixels + 16, LANES), ('date',...]
    ppermute x1 -> x2, waiting for transfers between devices: 0.01 us -> 1.23 us  [the longest x1 1.22 us: local(): swapped = lax.ppermute(got, 'head', swap)]
    pallas_call x1, Pallas kernels: 2.74 us -> 3.68 us  [attend(): pl.pallas_call(functools.partial(attend_kernel, pixels, dates, copies), i...]
  transfers between devices with their start and end apart: 2 -> 3, of which waited for: 1 -> 2; matrix products, arithmetic and copies ran while one was open for 1% -> 0% of each run, Pallas kernels for 10% -> 17%
where the time goes in v2:
time: 21.7 us; the launch traced here: 21.4 us
  waiting for transfers between devices  8.39 us (39%)
  starting transfers between devices  7.28 us (34%)
  Pallas kernels  5.68 us (26%)
    all_to_all x1, waiting for transfers between devices, local(): lax.all_to_all(sent.reshape(tiles * slabs, pixels + 16, LANES), ('date',...  7.16 us
    all_to_all x1, starting transfers between devices, local(): lax.all_to_all(sent.reshape(tiles * slabs, pixels + 16, LANES), ('date',...  6.82 us
    pallas_call x1, Pallas kernels, attend(): pl.pallas_call(functools.partial(attend_kernel, pixels, dates, copies), i...  3.68 us
    pallas_call x1, Pallas kernels, convolve(): pl.pallas_call(functools.partial(convolve_kernel, pixels, cols), in_specs...  2 us
    ppermute x1, waiting for transfers between devices, local(): swapped = lax.ppermute(got, 'head', swap)  1.22 us
    ppermute x1, starting transfers between devices, local(): other = lax.ppermute(first, 'head', swap)  0.45 us
  transfers between devices with their start and end apart: 3, of which 2 were waited for; matrix products, arithmetic and copies ran while one was open for 0% of the time, Pallas kernels for 17%

profile of v2, /device:TPU:0, one launch (start us, length us, event | category | flops | bytes accessed | tf_op | source)
XLA Modules:
  0.0 21.4 jit_solution(9884217500640556515)
XLA Ops:
  0.0 0.5 %collective-permute-start.1 = (bf16[3,768,128]{2,1,0:T(8,128)(2,1)}, bf16[3,768,128]{2,1,0:T(8,128)(2,1)S(1)}, u32[]{:S(2)}, u32[]{:S(2)}) collective-permute-start(bf16[3,768,128]{2,1,0:T(8,128)(2,1)} %bitcast.10), channel_id=1, source_target_pairs={{0,1},{1,0},{2,3},{3,2},{4,5},{5,4},{6,7},{7,6},{8,9},{9,8},{10,11... | collective-permute-start | bytes 1769480 | tf_op jit(solution)/shard_map/ppermute | solution.py:232
  0.5 0.0 copy-start
  0.5 0.0 copy-start.1
  0.5 3.7 %shard_map.82 = bf16[4,2,48,128]{3,2,1,0:T(8,128)(2,1)} custom-call(bf16[4,512,256]{2,1,0:T(8,128)(2,1)} %bitcast.15, s32[4,32,16]{2,1,0:T(8,128)} %bitcast.17, s32[16]{0:T(128)} %days_hbm.1, f32[1,128]{1,0:T(1,128)} %bitcast.18, bf16[256,128]{1,0:T(8,128)(2,1)} %keyw_hbm.1, bf16[256,128]{1,0:T(8,128)(2,1)} %valw_hbm.1), custom_call_target="tpu_custom_call" | custom-call | tf_op jit(solution)/shard_map/pallas_call | solution.py:128
  4.1 6.8 %all-to-all-start = ((bf16[8,48,128]{2,1,0:T(8,128)(2,1)}), bf16[8,48,128]{2,1,0:T(8,128)(2,1)S(1)}, u32[]{:S(2)}, u32[]{:S(2)}) async-start(bf16[8,48,128]{2,1,0:T(8,128)(2,1)} %bitcast.16), calls=%async_computation | async-start | bytes 196608 | tf_op jit(solution)/shard_map/all_to_all | solution.py:234
  11.0 7.2 %all-to-all-done = bf16[8,48,128]{2,1,0:T(8,128)(2,1)S(1)} async-done(((bf16[8,48,128]{2,1,0:T(8,128)(2,1)}), bf16[8,48,128]{2,1,0:T(8,128)(2,1)S(1)}, u32[]{:S(2)}, u32[]{:S(2)}) %all-to-all-start) | async-done | bytes 98336 | tf_op jit(solution)/shard_map/all_to_all | solution.py:234
  18.1 0.0 collective-permute-start
  18.1 0.1 pad_add_fusion.place
  18.2 1.2 %collective-permute-done.swapped = bf16[4,2,48,128]{3,2,1,0:T(8,128)(2,1)S(1)} collective-permute-done((bf16[4,2,48,128]{3,2,1,0:T(8,128)(2,1)S(1)}, bf16[4,2,48,128]{3,2,1,0:T(8,128)(2,1)S(1)}, u32[]{:S(2)}, u32[]{:S(2)}) %collective-permute-start) | collective-permute-done | bytes 98336 | tf_op jit(solution)/shard_map/ppermute | solution.py:241
  19.4 0.0 collective-permute-done.1.other
  19.4 0.0 copy-done
  19.4 0.0 copy-done.1
  19.4 2.0 %shard_map.83 = bf16[32,128]{1,0:T(8,128)(2,1)} custom-call(s32[2]{0:T(128)S(1)} %pad_add_fusion.place, bf16[4,2,48,128]{3,2,1,0:T(8,128)(2,1)S(1)} %bitcast.14, bf16[4,2,48,128]{3,2,1,0:T(8,128)(2,1)S(1)} %collective-permute-done.swapped, bf16[3,768,128]{2,1,0:T(8,128)(2,1)S(1)} %bitcast.11, bf16[3,768,128]{2,1,0:T(8,128)(2,1)S(1)} %collective-permute-done.1.other, ...), custom_call_target="tpu_custom_call" | custom-call | tf_op jit(solution)/shard_map/pallas_call | solution.py:217
Async XLA Ops:
  0.0 19.4 %collective-permute-start.1 = (bf16[3,768,128]{2,1,0:T(8,128)(2,1)}, bf16[3,768,128]{2,1,0:T(8,128)(2,1)S(1)}, u32[]{:S(2)}, u32[]{:S(2)}) collective-permute-start(bf16[3,768,128]{2,1,0:T(8,128)(2,1)} %bitcast.10), channel_id=1, source_target_pairs={{0,1},{1,0},{2,3},{3,2},{4,5},{5,4},{6,7},{7,6},{8,9},{9,8},{10,11... | collective-permute-start | bytes 1769480 | tf_op jit(solution)/shard_map/ppermute | solution.py:232
  0.5 19.0 %copy-start = (bf16[3,3,256,128]{3,2,1,0:T(8,128)(2,1)S(1)}, bf16[3,3,256,128]{3,2,1,0:T(8,128)(2,1)}, u32[]{:S(2)}) copy-start(bf16[3,3,256,128]{3,2,1,0:T(8,128)(2,1)} %param.14) | copy-start | bytes 1769476
  0.5 19.0 %copy-start.1 = (bf16[3,3,256,128]{3,2,1,0:T(8,128)(2,1)S(1)}, bf16[3,3,256,128]{3,2,1,0:T(8,128)(2,1)}, u32[]{:S(2)}) copy-start(bf16[3,3,256,128]{3,2,1,0:T(8,128)(2,1)} %param.15) | copy-start | bytes 1769476
  4.1 14.0 %all-to-all-start = ((bf16[8,48,128]{2,1,0:T(8,128)(2,1)}), bf16[8,48,128]{2,1,0:T(8,128)(2,1)S(1)}, u32[]{:S(2)}, u32[]{:S(2)}) async-start(bf16[8,48,128]{2,1,0:T(8,128)(2,1)} %bitcast.16), calls=%async_computation | async-start | bytes 196608 | tf_op jit(solution)/shard_map/all_to_all | solution.py:234
  18.1 1.3 %collective-permute-start = (bf16[4,2,48,128]{3,2,1,0:T(8,128)(2,1)S(1)}, bf16[4,2,48,128]{3,2,1,0:T(8,128)(2,1)S(1)}, u32[]{:S(2)}, u32[]{:S(2)}) collective-permute-start(bf16[4,2,48,128]{3,2,1,0:T(8,128)(2,1)S(1)} %bitcast.13), channel_id=1, source_target_pairs={{0,1},{1,0},{2,3},{3,2},{4,5},{5,4},{6,7},{7,6},{8,9},{9,8},{10,11... | collective-permute-start | bytes 294920 | tf_op jit(solution)/shard_map/ppermute | solution.py:241

commit v3 on v2

v3 whole, which is shorter than its diff:
```python
import functools
import math

import jax
import jax.numpy as jnp
from jax import lax
from jax.experimental import pallas as pl
from jax.experimental.pallas import tpu as pltpu
from jax.sharding import PartitionSpec as P

HSIZE = 32
LANES = 128
PENALTY = 6.0
F32 = jnp.float32
BF16 = jnp.bfloat16


def iota(shape, dim):
    return lax.broadcasted_iota(jnp.int32, shape, dim)


def split3(value):
    high = value.astype(BF16)
    rest = value - high.astype(F32)
    mid = rest.astype(BF16)
    low = (rest - mid.astype(F32)).astype(BF16)
    return high, mid, low


def same_head(rows):
    row = lax.rem(iota((rows, LANES), 0), LANES)
    return (row // HSIZE == iota((rows, LANES), 1) // HSIZE).astype(BF16)


def dot(a, b):
    return jnp.dot(a, b, preferred_element_type=F32)


def encoding_rows(days, dates, width):
    row, chan = iota((dates, width), 0), iota((dates, width), 1)
    even = lax.rem(chan, 2) == 0
    expo = (chan - lax.rem(chan, 2)).astype(F32) * F32(math.log(1000.0) / width)
    day = jnp.zeros((dates, width), F32)
    for t in range(dates):
        day = jnp.where(row == t, days[t].astype(F32), day)
    angle = day * jnp.exp(-expo)
    return jnp.where(even, jnp.sin(angle), jnp.cos(angle))


def fold_dates(value, join):
    pixels, dates, lanes = value.shape
    value = functools.reduce(join, [value[:, t : t + 8] for t in range(0, dates, 8)])
    for step in (1, 2, 4):
        value = value.reshape(-1, 2, 8, lanes)
        first, second = value[:, 0], value[:, 1]
        low = (iota(first.shape, 1) & step) == 0
        value = join(
            jnp.where(low, first, second),
            pltpu.roll(jnp.where(low, second, first), 8 - step, 1),
        )
    return value.reshape(pixels, lanes)


def attend_kernel(
    pixels, dates, tokens_hbm, mask_hbm, days_hbm, query_hbm, keyw_hbm, valw_hbm, out,
    tokens, mask, days, query, keyw, weights, sems, token_sems,
):
    tiles, width = tokens.shape[0], tokens.shape[-1]
    date = lax.axis_index("date")
    columns = pl.ds(3 * LANES, LANES)
    small = [
        pltpu.make_async_copy(days_hbm, days, sems.at[0]),
        pltpu.make_async_copy(query_hbm, query, sems.at[1]),
        pltpu.make_async_copy(keyw_hbm, keyw, sems.at[2]),
        pltpu.make_async_copy(valw_hbm, weights.at[:, columns], sems.at[3]),
        pltpu.make_async_copy(mask_hbm, mask, sems.at[4]),
    ]
    for copy in small:
        copy.start()
    loads = lambda i: pltpu.make_async_copy(tokens_hbm.at[date ^ i], tokens.at[i], token_sems.at[i])
    for i in range(tiles):
        loads(i).start()
    small[0].wait()
    table = encoding_rows(days, dates, width)
    small[1].wait()
    small[2].wait()
    scaled = keyw[...].astype(F32) * (query[...] * F32(HSIZE**-0.5))
    spread = same_head(LANES)
    high, mid, low = split3(scaled)
    folded = dot(high, spread) + (dot(mid, spread) + dot(low, spread))
    high, mid, low = split3(folded)
    weights[:, 0:LANES] = high
    weights[:, LANES : 2 * LANES] = mid
    weights[:, 2 * LANES : 3 * LANES] = low
    small[3].wait()
    small[4].wait()

    def one(i):
        feats = tokens[i].reshape(pixels, dates, width).astype(F32) + table[None]
        inputs = feats.astype(BF16).reshape(pixels * dates, width)
        both = dot(inputs, weights[...])
        score = both[:, 0:LANES] + (both[:, LANES : 2 * LANES] + both[:, 2 * LANES : 3 * LANES])
        vals = both[:, 3 * LANES : 4 * LANES]
        cloud = PENALTY * (1.0 - mask[date ^ i].astype(F32))
        score = score.reshape(pixels, dates, LANES) - lax.broadcast_in_dim(
            cloud, (pixels, dates, LANES), (0, 1)
        )
        top = jnp.max(score, axis=1)
        expo = jnp.exp(score - top[:, None, :])
        total = fold_dates(expo, jnp.add)
        summed = fold_dates(expo * vals.reshape(pixels, dates, LANES), jnp.add)
        part = (summed / total).astype(BF16)
        level = top + jnp.log(total)
        own = lax.rem(iota((pixels, LANES), 1), HSIZE) == iota((pixels, LANES), 0)
        packed = jnp.sum(jnp.where(own, level, 0.0), axis=0, keepdims=True)
        high, mid, low = split3(packed)
        row = iota((16, LANES), 0)
        tail = jnp.where(
            row == 0,
            high.astype(F32),
            jnp.where(row == 1, mid.astype(F32), jnp.where(row == 2, low.astype(F32), 0.0)),
        ).astype(BF16)
        out[i, 0:pixels, :] = part
        out[i, pixels : pixels + 16, :] = tail

    for i in range(tiles):
        loads(i).wait()
    if tiles <= 4:
        for i in range(tiles):
            one(i)
    else:
        pl.loop(0, tiles)(one)


def attend(tokens, cloud_mask, day_of_year, query, key_weight, value_weight):
    tiles, rows, cols, dates, width = tokens.shape
    pixels = rows * cols
    tokens = tokens.reshape(tiles, pixels * dates, width)
    mask = cloud_mask.reshape(tiles, pixels, dates)
    return pl.pallas_call(
        functools.partial(attend_kernel, pixels, dates),
        in_specs=[pl.BlockSpec(memory_space=pltpu.HBM)] * 6,
        out_specs=pl.BlockSpec(memory_space=pltpu.VMEM),
        out_shape=pltpu.VMEM((tiles, pixels + 16, LANES), BF16),
        scratch_shapes=[
            pltpu.VMEM(tokens.shape, BF16),
            pltpu.VMEM(mask.shape, jnp.int32),
            pltpu.SMEM(day_of_year.shape, jnp.int32),
            pltpu.VMEM((1, LANES), F32),
            pltpu.VMEM((width, LANES), BF16),
            pltpu.VMEM((width, 4 * LANES), BF16),
            pltpu.SemaphoreType.DMA((5,)),
            pltpu.SemaphoreType.DMA((tiles,)),
        ],
        compiler_params=pltpu.CompilerParams(vmem_limit_bytes=60 * 2**20),
    )(tokens, mask, day_of_year, query.reshape(1, LANES), key_weight, value_weight)


def merge(blocks, pixels, first, count):
    levels = [jnp.sum(tail.astype(F32), axis=0, keepdims=True) for _, tail in blocks]
    best = functools.reduce(jnp.maximum, levels)
    shares = [jnp.exp(level - best) for level in levels]
    total = functools.reduce(jnp.add, shares)
    own = lax.rem(iota((count, LANES), 1), HSIZE) == iota((count, LANES), 0) + first
    spread = same_head(2 * LANES)
    pooled = jnp.zeros((count, LANES), F32)
    for (part, _), share in zip(blocks, shares):
        share = share / total
        high = share.astype(BF16).astype(F32)
        both = jnp.concatenate([jnp.where(own, high, 0.0), jnp.where(own, share - high, 0.0)], axis=1)
        pooled = pooled + dot(both.astype(BF16), spread) * part.astype(F32)
    return pooled.astype(BF16).astype(F32)


def columns(field, cols):
    count = field.shape[0]
    col = lax.rem(iota(field.shape, 0), cols)
    left = jnp.where(col == 0, 0.0, pltpu.roll(field, 1, 0))
    right = jnp.where(col == cols - 1, 0.0, pltpu.roll(field, count - 1, 0))
    return jnp.concatenate([left, field, right], axis=1).astype(BF16)


def stencil(field, kernel, cols):
    count = field.shape[0] - 2 * cols
    return sum(dot(field, kernel[a])[a * cols : a * cols + count] for a in range(3))


def convolve_kernel(pixels, cols, slabs, slots, mine, theirs, got, swapped, first, other, second, out):
    dates = mine.shape[0]
    slab, head = lax.axis_index("tile"), lax.axis_index("head")
    odd = lax.rem(slab, 2) == 1
    halo = 2 * cols

    def in_order(own, partner):
        return jnp.concatenate(
            [jnp.where(head == 0, own, partner), jnp.where(head == 0, partner, own)], axis=1
        )

    starts, size = positions(dates)

    def block(core, slot, k, half, start, count):
        if k == 0:
            core = half
        place = slot * size + starts[k] + ((half if core == 0 else 1 - half) if k > 0 else 0)
        return tuple(
            jnp.where(head == core, got[place, rows], swapped[place, rows])
            for rows in (pl.ds(start, count), pl.ds(pixels, 16))
        )

    def kept(half):
        return tuple(
            jnp.where(head == half, mine[0, rows], theirs[0, rows])
            for rows in (pl.ds(0, pixels), pl.ds(pixels, 16))
        )

    centre = jnp.concatenate(
        [
            merge([kept(half)] + [block(0, 0, k, half, 0, pixels) for k in range(1, dates)], pixels, 0, pixels)
            for half in range(2)
        ],
        axis=1,
    )

    def neighbour(slot):
        above = odd if slot == 0 else jnp.logical_not(odd)
        start = pl.multiple_of(jnp.where(above, pixels - halo, 0), 16)
        return jnp.concatenate(
            [
                merge([block(1, slot, k, half, start, halo) for k in range(dates)], pixels, start, halo)
                for half in range(2)
            ],
            axis=1,
        )

    one = neighbour(0)
    two = neighbour(1) if slots > 1 else one
    above = jnp.where(slab > 0, jnp.where(odd, one, two), 0.0)
    below = jnp.where(slab < slabs - 1, jnp.where(odd, two, one), 0.0)
    field = jnp.concatenate([above, centre, below], axis=0)
    wide = columns(field, cols)
    hidden = in_order(stencil(wide, first, cols), stencil(wide, other, cols))
    count = pixels + 2 * cols
    row = iota(hidden.shape, 0)
    inside = jnp.logical_and(
        jnp.logical_or(row >= cols, slab > 0), jnp.logical_or(row < count - cols, slab < slabs - 1)
    )
    hidden = jnp.where(inside, jnp.maximum(hidden, 0.0), 0.0).astype(BF16).astype(F32)
    out[...] = stencil(columns(hidden, cols), second, cols).astype(BF16)


def convolve(mine, theirs, got, swapped, first, other, second, pixels, cols, slabs, slots):
    return pl.pallas_call(
        functools.partial(convolve_kernel, pixels, cols, slabs, slots),
        in_specs=[pl.BlockSpec(memory_space=pltpu.VMEM)] * 7,
        out_specs=pl.BlockSpec(memory_space=pltpu.VMEM),
        out_shape=jax.ShapeDtypeStruct((pixels, second.shape[-1]), BF16),
        compiler_params=pltpu.CompilerParams(vmem_limit_bytes=32 * 2**20),
    )(mine, theirs, got, swapped, first, other, second)


def arrangement(dates):
    return list(range(dates - 1, -1, -1))


def positions(dates):
    starts, size = {}, 0
    for k in arrangement(dates):
        starts[k] = size
        size += 2 if k > 0 else 1
    return starts, size


def routes(dates, slabs, k, slot):
    place = lambda d, t, core: (d * slabs + t) * 2 + core
    pairs = []
    for d in range(dates):
        for t in range(slabs):
            near = t ^ 1 if slot == 0 else ((t + 1) ^ 1) - 1
            if k > 0 and slot == 0:
                pairs.append((place(d, t, 0), place(d ^ k, t, 0)))
            if k == 0 and 0 <= near < slabs:
                pairs.append((place(d, t, 0), place(d, near, 0)))
            if 0 <= near < slabs:
                pairs.append((place(d, t, 1), place(d ^ k, near, 1)))
    return pairs


def local(slabs, tokens, cloud_mask, day_of_year, query, key_weight, value_weight, conv_first, conv_second):
    tiles, rows, cols, dates, width = tokens.shape
    pixels = rows * cols
    slots = 1 if slabs <= 2 else 2
    swap = [(0, 1), (1, 0)]
    first = conv_first.reshape(3, 3 * width, -1)
    second = conv_second.reshape(3, 3 * width, -1)
    other = lax.ppermute(first, "head", swap)
    mine = attend(tokens, cloud_mask, day_of_year, query, key_weight, value_weight)
    theirs = lax.ppermute(mine, "head", swap)
    pieces = []
    for slot in range(slots):
        for k in arrangement(tiles):
            block = jnp.stack([mine[k], theirs[k]]) if k > 0 else mine[:1]
            pieces.append(
                lax.ppermute(block, ("date", "tile", "head"), routes(tiles, slabs, k, slot))
            )
    got = jnp.concatenate(pieces)
    swapped = lax.ppermute(got, "head", swap)
    out = convolve(mine, theirs, got, swapped, first, other, second, pixels, cols, slabs, slots)
    return out.reshape(1, rows, cols, -1)


def solution(mesh):
    in_specs = (
        P("groups", "tile", None, "date", None),
        P("groups", "tile", None, "date"),
        P(("groups", "date")),
        P("head"),
        P(None, "head"),
        P(None, "head"),
        P(None, None, None, "head"),
        P(None, None, None, "head"),
    )
    out_specs = P(("groups", "date"), "tile", None, "head")
    body = functools.partial(local, mesh.shape["tile"])
    return jax.shard_map(body, mesh=mesh, in_specs=in_specs, out_specs=out_specs, check_vma=False)
```

time: 21.7 us -> 17.3 us (0.80)
  waiting for transfers between devices: 8.39 us -> 5.46 us
  Pallas kernels: 5.68 us -> 3.82 us
  starting transfers between devices: 7.28 us -> 7.77 us
    ppermute x0 -> x5, starting transfers between devices: none -> 7.54 us  [the longest x4 7.03 us: local(): lax.ppermute(block, ('date', 'tile', 'head'), routes(tiles, slabs, k, slot))]
    all_to_all x1 -> x0, waiting for transfers between devices: 7.16 us -> none  [local(): lax.all_to_all(sent.reshape(tiles * slabs, pixels + 16, LANES), ('date',...]
    all_to_all x1 -> x0, starting transfers between devices: 6.82 us -> none  [local(): lax.all_to_all(sent.reshape(tiles * slabs, pixels + 16, LANES), ('date',...]
    ppermute x0 -> x5, waiting for transfers between devices: none -> 4.19 us  [the longest x4 4.19 us: local(): lax.ppermute(block, ('date', 'tile', 'head'), routes(tiles, slabs, k, slot))]
    pallas_call x2, Pallas kernels: 5.68 us -> 3.82 us  [the longest x1 2.41 us: attend(): pl.pallas_call(functools.partial(attend_kernel, pixels, dates), in_specs=...]
    ppermute x1, starting transfers between devices: 0.45 us -> 0.16 us  [local(): other = lax.ppermute(first, 'head', swap)]
  transfers between devices with their start and end apart: 3 -> 7, of which waited for: 2 -> 3; matrix products, arithmetic and copies ran while one was open for 0% -> 0% of each run, Pallas kernels for 17% -> 0%
where the time goes in v3:
time: 17.3 us; the launch traced here: 17.2 us
  starting transfers between devices  7.77 us (45%)
  waiting for transfers between devices  5.46 us (32%)
  Pallas kernels  3.82 us (22%)
    ppermute x4, starting transfers between devices, local(): lax.ppermute(block, ('date', 'tile', 'head'), routes(tiles, slabs, k, slot))  7.03 us
    ppermute x4, waiting for transfers between devices, local(): lax.ppermute(block, ('date', 'tile', 'head'), routes(tiles, slabs, k, slot))  4.19 us
    pallas_call x1, Pallas kernels, attend(): pl.pallas_call(functools.partial(attend_kernel, pixels, dates), in_specs=...  2.41 us
    pallas_call x1, Pallas kernels, convolve(): pl.pallas_call(functools.partial(convolve_kernel, pixels, cols, slabs, sl...  1.42 us
    ppermute x1, waiting for transfers between devices, local(): swapped = lax.ppermute(got, 'head', swap)  1.27 us
    ppermute x1, starting transfers between devices, local(): theirs = lax.ppermute(mine, 'head', swap)  0.52 us
  transfers between devices with their start and end apart: 7, of which 3 were waited for; matrix products, arithmetic and copies ran while one was open for 0% of the time, Pallas kernels for 0%

profile of v3, /device:TPU:0, one launch (start us, length us, event | category | flops | bytes accessed | tf_op | source)
XLA Modules:
  0.0 17.2 jit_solution(13202314907015478920)
XLA Ops:
  0.0 0.0 copy-start
  0.0 0.0 copy-start.1
  0.0 2.4 %shard_map.82.mine = bf16[4,48,128]{2,1,0:T(8,128)(2,1)S(1)} custom-call(bf16[4,512,256]{2,1,0:T(8,128)(2,1)} %bitcast.9, s32[4,32,16]{2,1,0:T(8,128)} %bitcast.10, s32[16]{0:T(128)} %days_hbm.1, f32[1,128]{1,0:T(1,128)} %bitcast.11, bf16[256,128]{1,0:T(8,128)(2,1)} %keyw_hbm.1, bf16[256,128]{1,0:T(8,128)(2,1)} %valw_hbm.1), custom_call_target="tpu_custom_call" | custom-call | tf_op jit(solution)/shard_map/pallas_call | solution.py:140
  2.4 0.5 %collective-permute-start = (bf16[4,48,128]{2,1,0:T(8,128)(2,1)S(1)}, bf16[4,48,128]{2,1,0:T(8,128)(2,1)S(1)}, u32[]{:S(2)}, u32[]{:S(2)}) collective-permute-start(bf16[4,48,128]{2,1,0:T(8,128)(2,1)S(1)} %shard_map.82.mine), channel_id=1, source_target_pairs={{0,1},{1,0},{2,3},{3,2},{4,5},{5,4},{6,7},{7,6},{8,9},{9,8},{10,11... | collective-permute-start | bytes 147464 | tf_op jit(solution)/shard_map/ppermute | solution.py:297
  2.9 2.6 %collective-permute-start.4 = (bf16[1,48,128]{2,1,0:T(8,128)(2,1)S(1)}, bf16[1,48,128]{2,1,0:T(8,128)(2,1)S(1)}, u32[]{:S(2)}, u32[]{:S(2)}) collective-permute-start(bf16[1,48,128]{2,1,0:T(8,128)(2,1)S(1)} %get-tuple-element.5), channel_id=1, source_target_pairs={{0,2},{1,3},{2,0},{3,1},{4,6},{5,7},{6,4},{7,5},{8,10},{9,11},{10,... | collective-permute-start | bytes 36872 | tf_op jit(solution)/shard_map/ppermute | solution.py:303
  5.5 0.0 copy-done
  5.5 0.2 collective-permute-start.6
  5.7 0.0 collective-permute-done.theirs
  5.7 3.7 %collective-permute-start.1 = (bf16[2,48,128]{2,1,0:T(8,128)(2,1)S(1)}, bf16[2,48,128]{2,1,0:T(8,128)(2,1)S(1)}, u32[]{:S(2)}, u32[]{:S(2)}) collective-permute-start(bf16[2,48,128]{2,1,0:T(8,128)(2,1)S(1)} %pad_maximum_fusion), channel_id=1, source_target_pairs={{0,12},{1,15},{2,14},{3,13},{4,8},{5,11},{6,10},{7,9},{8,4},{9,7},... | collective-permute-start | bytes 73736 | tf_op jit(solution)/shard_map/ppermute | solution.py:303
  9.4 0.0 collective-permute-start.2
  9.4 0.8 %collective-permute-start.3 = (bf16[2,48,128]{2,1,0:T(8,128)(2,1)S(1)}, bf16[2,48,128]{2,1,0:T(8,128)(2,1)S(1)}, u32[]{:S(2)}, u32[]{:S(2)}) collective-permute-start(bf16[2,48,128]{2,1,0:T(8,128)(2,1)S(1)} %pad_maximum_fusion.2), channel_id=1, source_target_pairs={{0,4},{1,7},{2,6},{3,5},{4,0},{5,3},{6,2},{7,1},{8,12},{9,15},{10,... | collective-permute-start | bytes 73736 | tf_op jit(solution)/shard_map/ppermute | solution.py:303
  10.2 1.2 %collective-permute-done.1 = bf16[2,48,128]{2,1,0:T(8,128)(2,1)S(1)} collective-permute-done((bf16[2,48,128]{2,1,0:T(8,128)(2,1)S(1)}, bf16[2,48,128]{2,1,0:T(8,128)(2,1)S(1)}, u32[]{:S(2)}, u32[]{:S(2)}) %collective-permute-start.1) | collective-permute-done | bytes 24608 | tf_op jit(solution)/shard_map/ppermute | solution.py:303
  11.4 3.0 %collective-permute-done.2 = bf16[2,48,128]{2,1,0:T(8,128)(2,1)S(1)} collective-permute-done((bf16[2,48,128]{2,1,0:T(8,128)(2,1)S(1)}, bf16[2,48,128]{2,1,0:T(8,128)(2,1)S(1)}, u32[]{:S(2)}, u32[]{:S(2)}) %collective-permute-start.2) | collective-permute-done | bytes 24608 | tf_op jit(solution)/shard_map/ppermute | solution.py:303
  14.4 0.0 collective-permute-done.3
  14.4 0.0 collective-permute-done.4
  14.4 0.1 collective-permute-start.5
  14.5 1.3 %collective-permute-done.5.swapped = bf16[7,48,128]{2,1,0:T(8,128)(2,1)S(1)} collective-permute-done((bf16[7,48,128]{2,1,0:T(8,128)(2,1)S(1)}, bf16[7,48,128]{2,1,0:T(8,128)(2,1)S(1)}, u32[]{:S(2)}, u32[]{:S(2)}) %collective-permute-start.5) | collective-permute-done | bytes 86048 | tf_op jit(solution)/shard_map/ppermute | solution.py:306
  15.7 0.0 collective-permute-done.6.other
  15.7 0.0 copy-done.1
  15.7 1.4 %shard_map.83 = bf16[32,128]{1,0:T(8,128)(2,1)} custom-call(bf16[4,48,128]{2,1,0:T(8,128)(2,1)S(1)} %shard_map.82.mine, bf16[4,48,128]{2,1,0:T(8,128)(2,1)S(1)} %collective-permute-done.theirs, bf16[7,48,128]{2,1,0:T(8,128)(2,1)S(1)} %constant_dynamic-update-slice_fusion.got, bf16[7,48,128]{2,1,0:T(8,128)(2,1)S(1)} %collective-permute-done.5.swapped, ...), custom_call_target="tpu_custom_call" | custom-call | tf_op jit(solution)/shard_map/pallas_call | solution.py:252
  (9 shorter events, 0.1 us)
Async XLA Ops:
  0.0 5.5 %copy-start = (bf16[3,3,256,128]{3,2,1,0:T(8,128)(2,1)S(1)}, bf16[3,3,256,128]{3,2,1,0:T(8,128)(2,1)}, u32[]{:S(2)}) copy-start(bf16[3,3,256,128]{3,2,1,0:T(8,128)(2,1)} %param.14) | copy-start | bytes 1769476
  0.0 15.7 %copy-start.1 = (bf16[3,3,256,128]{3,2,1,0:T(8,128)(2,1)S(1)}, bf16[3,3,256,128]{3,2,1,0:T(8,128)(2,1)}, u32[]{:S(2)}) copy-start(bf16[3,3,256,128]{3,2,1,0:T(8,128)(2,1)} %param.15) | copy-start | bytes 1769476
  2.4 3.3 %collective-permute-start = (bf16[4,48,128]{2,1,0:T(8,128)(2,1)S(1)}, bf16[4,48,128]{2,1,0:T(8,128)(2,1)S(1)}, u32[]{:S(2)}, u32[]{:S(2)}) collective-permute-start(bf16[4,48,128]{2,1,0:T(8,128)(2,1)S(1)} %shard_map.82.mine), channel_id=1, source_target_pairs={{0,1},{1,0},{2,3},{3,2},{4,5},{5,4},{6,7},{7,6},{8,9},{9,8},{10,11... | collective-permute-start | bytes 147464 | tf_op jit(solution)/shard_map/ppermute | solution.py:297
  2.9 11.4 %collective-permute-start.4 = (bf16[1,48,128]{2,1,0:T(8,128)(2,1)S(1)}, bf16[1,48,128]{2,1,0:T(8,128)(2,1)S(1)}, u32[]{:S(2)}, u32[]{:S(2)}) collective-permute-start(bf16[1,48,128]{2,1,0:T(8,128)(2,1)S(1)} %get-tuple-element.5), channel_id=1, source_target_pairs={{0,2},{1,3},{2,0},{3,1},{4,6},{5,7},{6,4},{7,5},{8,10},{9,11},{10,... | collective-permute-start | bytes 36872 | tf_op jit(solution)/shard_map/ppermute | solution.py:303
  5.5 10.2 %collective-permute-start.6 = (bf16[3,768,128]{2,1,0:T(8,128)(2,1)S(1)}, bf16[3,768,128]{2,1,0:T(8,128)(2,1)S(1)}, u32[]{:S(2)}, u32[]{:S(2)}) collective-permute-start(bf16[3,768,128]{2,1,0:T(8,128)(2,1)S(1)} %bitcast.6), channel_id=1, source_target_pairs={{0,1},{1,0},{2,3},{3,2},{4,5},{5,4},{6,7},{7,6},{8,9},{9,8},{10,11... | collective-permute-start | bytes 1769480 | tf_op jit(solution)/shard_map/ppermute | solution.py:295
  5.7 5.7 %collective-permute-start.1 = (bf16[2,48,128]{2,1,0:T(8,128)(2,1)S(1)}, bf16[2,48,128]{2,1,0:T(8,128)(2,1)S(1)}, u32[]{:S(2)}, u32[]{:S(2)}) collective-permute-start(bf16[2,48,128]{2,1,0:T(8,128)(2,1)S(1)} %pad_maximum_fusion), channel_id=1, source_target_pairs={{0,12},{1,15},{2,14},{3,13},{4,8},{5,11},{6,10},{7,9},{8,4},{9,7},... | collective-permute-start | bytes 73736 | tf_op jit(solution)/shard_map/ppermute | solution.py:303
  9.4 5.0 %collective-permute-start.2 = (bf16[2,48,128]{2,1,0:T(8,128)(2,1)S(1)}, bf16[2,48,128]{2,1,0:T(8,128)(2,1)S(1)}, u32[]{:S(2)}, u32[]{:S(2)}) collective-permute-start(bf16[2,48,128]{2,1,0:T(8,128)(2,1)S(1)} %pad_maximum_fusion.1), channel_id=1, source_target_pairs={{0,8},{1,11},{2,10},{3,9},{4,12},{5,15},{6,14},{7,13},{8,0},{9,3},... | collective-permute-start | bytes 73736 | tf_op jit(solution)/shard_map/ppermute | solution.py:303
  9.4 5.0 %collective-permute-start.3 = (bf16[2,48,128]{2,1,0:T(8,128)(2,1)S(1)}, bf16[2,48,128]{2,1,0:T(8,128)(2,1)S(1)}, u32[]{:S(2)}, u32[]{:S(2)}) collective-permute-start(bf16[2,48,128]{2,1,0:T(8,128)(2,1)S(1)} %pad_maximum_fusion.2), channel_id=1, source_target_pairs={{0,4},{1,7},{2,6},{3,5},{4,0},{5,3},{6,2},{7,1},{8,12},{9,15},{10,... | collective-permute-start | bytes 73736 | tf_op jit(solution)/shard_map/ppermute | solution.py:303
  14.4 1.3 %collective-permute-start.5 = (bf16[7,48,128]{2,1,0:T(8,128)(2,1)S(1)}, bf16[7,48,128]{2,1,0:T(8,128)(2,1)S(1)}, u32[]{:S(2)}, u32[]{:S(2)}) collective-permute-start(bf16[7,48,128]{2,1,0:T(8,128)(2,1)S(1)} %constant_dynamic-update-slice_fusion.got), channel_id=1, source_target_pairs={{0,1},{1,0},{2,3},{3,2},{4,5},{5,4},{6,7},{7,6},{8,9},{9,8},{10,11... | collective-permute-start | bytes 258056 | tf_op jit(solution)/shard_map/ppermute | solution.py:306

commit v4 on v3

--- a/solution.py
+++ b/solution.py
@@ -11,6 +11,7 @@
 HSIZE = 32
 LANES = 128
 PENALTY = 6.0
+LOG2E = math.log2(math.e)
 F32 = jnp.float32
 BF16 = jnp.bfloat16
 
@@ -61,9 +62,48 @@
     return value.reshape(pixels, lanes)
 
 
+def pool(feats, table, weights, clear):
+    pixels, dates = clear.shape
+    width = feats.shape[-1]
+    feats = feats.reshape(pixels, dates, width).astype(F32) + table[None]
+    both = dot(feats.astype(BF16).reshape(pixels * dates, width), weights)
+    score = both[:, 0:LANES] + (both[:, LANES : 2 * LANES] + both[:, 2 * LANES : 3 * LANES])
+    vals = both[:, 3 * LANES : 4 * LANES].reshape(pixels, dates, LANES)
+    cloud = F32(PENALTY * LOG2E) * (1.0 - clear.astype(F32))
+    score = score.reshape(pixels, dates, LANES) - lax.broadcast_in_dim(
+        cloud, (pixels, dates, LANES), (0, 1)
+    )
+    top = jnp.max(score, axis=1)
+    expo = jnp.exp2(score - top[:, None, :])
+    total = fold_dates(expo, jnp.add)
+    summed = fold_dates(expo * vals, jnp.add)
+    level = top + jnp.log(total) * F32(LOG2E)
+    own = lax.rem(iota((pixels, LANES), 1), HSIZE) == iota((pixels, LANES), 0)
+    packed = jnp.sum(jnp.where(own, level, 0.0), axis=0, keepdims=True)
+    row = iota((16, LANES), 0)
+    tail = jnp.zeros((16, LANES), F32)
+    for place, piece in enumerate(split3(packed)):
+        tail = jnp.where(row == place, piece.astype(F32), tail)
+    return (summed / total).astype(BF16), tail.astype(BF16)
+
+
+def pool_all(count, out, tokens, table, weights, clear):
+    def one(i):
+        part, tail = pool(tokens[i], table[...], weights[...], clear(i))
+        pixels = part.shape[0]
+        out[i, 0:pixels, :] = part
+        out[i, pixels : pixels + 16, :] = tail
+
+    if count <= 4:
+        for i in range(count):
+            one(i)
+    else:
+        pl.loop(0, count)(one)
+
+
 def attend_kernel(
-    pixels, dates, tokens_hbm, mask_hbm, days_hbm, query_hbm, keyw_hbm, valw_hbm, out,
-    tokens, mask, days, query, keyw, weights, sems, token_sems,
+    dates, tokens_hbm, mask_hbm, days_hbm, query_hbm, keyw_hbm, valw_hbm, out,
+    tokens, mask, weights, table, days, query, keyw, sems, token_sems,
 ):
     tiles, width = tokens.shape[0], tokens.shape[-1]
     date = lax.axis_index("date")
@@ -77,59 +117,26 @@
     ]
     for copy in small:
         copy.start()
-    loads = lambda i: pltpu.make_async_copy(tokens_hbm.at[date ^ i], tokens.at[i], token_sems.at[i])
-    for i in range(tiles):
-        loads(i).start()
+    loads = [
+        pltpu.make_async_copy(tokens_hbm.at[date ^ i], tokens.at[i], token_sems.at[i]) for i in range(tiles)
+    ]
+    for copy in loads:
+        copy.start()
     small[0].wait()
-    table = encoding_rows(days, dates, width)
+    table[...] = encoding_rows(days, dates, width)
     small[1].wait()
     small[2].wait()
-    scaled = keyw[...].astype(F32) * (query[...] * F32(HSIZE**-0.5))
+    scaled = keyw[...].astype(F32) * (query[...] * F32(HSIZE**-0.5 * LOG2E))
     spread = same_head(LANES)
     high, mid, low = split3(scaled)
     folded = dot(high, spread) + (dot(mid, spread) + dot(low, spread))
-    high, mid, low = split3(folded)
-    weights[:, 0:LANES] = high
-    weights[:, LANES : 2 * LANES] = mid
-    weights[:, 2 * LANES : 3 * LANES] = low
+    for place, piece in enumerate(split3(folded)):
+        weights[:, place * LANES : (place + 1) * LANES] = piece
     small[3].wait()
     small[4].wait()
-
-    def one(i):
-        feats = tokens[i].reshape(pixels, dates, width).astype(F32) + table[None]
-        inputs = feats.astype(BF16).reshape(pixels * dates, width)
-        both = dot(inputs, weights[...])
-        score = both[:, 0:LANES] + (both[:, LANES : 2 * LANES] + both[:, 2 * LANES : 3 * LANES])
-        vals = both[:, 3 * LANES : 4 * LANES]
-        cloud = PENALTY * (1.0 - mask[date ^ i].astype(F32))
-        score = score.reshape(pixels, dates, LANES) - lax.broadcast_in_dim(
-            cloud, (pixels, dates, LANES), (0, 1)
-        )
-        top = jnp.max(score, axis=1)
-        expo = jnp.exp(score - top[:, None, :])
-        total = fold_dates(expo, jnp.add)
-        summed = fold_dates(expo * vals.reshape(pixels, dates, LANES), jnp.add)
-        part = (summed / total).astype(BF16)
-        level = top + jnp.log(total)
-        own = lax.rem(iota((pixels, LANES), 1), HSIZE) == iota((pixels, LANES), 0)
-        packed = jnp.sum(jnp.where(own, level, 0.0), axis=0, keepdims=True)
-        high, mid, low = split3(packed)
-        row = iota((16, LANES), 0)
-        tail = jnp.where(
-            row == 0,
-            high.astype(F32),
-            jnp.where(row == 1, mid.astype(F32), jnp.where(row == 2, low.astype(F32), 0.0)),
-        ).astype(BF16)
-        out[i, 0:pixels, :] = part
-        out[i, pixels : pixels + 16, :] = tail
-
-    for i in range(tiles):
-        loads(i).wait()
-    if tiles <= 4:
-        for i in range(tiles):
-            one(i)
-    else:
-        pl.loop(0, tiles)(one)
+    for copy in loads:
+        copy.wait()
+    pool_all(tiles, out, tokens, table, weights, lambda i: mask[date ^ i])
 
 
 def attend(tokens, cloud_mask, day_of_year, query, key_weight, value_weight):
@@ -138,17 +145,18 @@
     tokens = tokens.reshape(tiles, pixels * dates, width)
     mask = cloud_mask.reshape(tiles, pixels, dates)
     return pl.pallas_call(
-        functools.partial(attend_kernel, pixels, dates),
+        functools.partial(attend_kernel, dates),
         in_specs=[pl.BlockSpec(memory_space=pltpu.HBM)] * 6,
         out_specs=pl.BlockSpec(memory_space=pltpu.VMEM),
         out_shape=pltpu.VMEM((tiles, pixels + 16, LANES), BF16),
         scratch_shapes=[
             pltpu.VMEM(tokens.shape, BF16),
             pltpu.VMEM(mask.shape, jnp.int32),
+            pltpu.VMEM((width, 4 * LANES), BF16),
+            pltpu.VMEM((dates, width), F32),
             pltpu.SMEM(day_of_year.shape, jnp.int32),
             pltpu.VMEM((1, LANES), F32),
             pltpu.VMEM((width, LANES), BF16),
-            pltpu.VMEM((width, 4 * LANES), BF16),
             pltpu.SemaphoreType.DMA((5,)),
             pltpu.SemaphoreType.DMA((tiles,)),
         ],
@@ -156,16 +164,16 @@
     )(tokens, mask, day_of_year, query.reshape(1, LANES), key_weight, value_weight)
 
 
-def merge(blocks, pixels, first, count):
+def merge(blocks, pixels, start, count):
     levels = [jnp.sum(tail.astype(F32), axis=0, keepdims=True) for _, tail in blocks]
     best = functools.reduce(jnp.maximum, levels)
-    shares = [jnp.exp(level - best) for level in levels]
-    total = functools.reduce(jnp.add, shares)
-    own = lax.rem(iota((count, LANES), 1), HSIZE) == iota((count, LANES), 0) + first
+    shares = [jnp.exp2(level - best) for level in levels]
+    scale = 1.0 / functools.reduce(jnp.add, shares)
+    own = lax.rem(iota((count, LANES), 1), HSIZE) == iota((count, LANES), 0) + start
     spread = same_head(2 * LANES)
     pooled = jnp.zeros((count, LANES), F32)
     for (part, _), share in zip(blocks, shares):
-        share = share / total
+        share = share * scale
         high = share.astype(BF16).astype(F32)
         both = jnp.concatenate([jnp.where(own, high, 0.0), jnp.where(own, share - high, 0.0)], axis=1)
         pooled = pooled + dot(both.astype(BF16), spread) * part.astype(F32)
@@ -196,12 +204,14 @@
             [jnp.where(head == 0, own, partner), jnp.where(head == 0, partner, own)], axis=1
         )
 
-    starts, size = positions(dates)
+    starts = positions(dates, slots)
 
     def block(core, slot, k, half, start, count):
-        if k == 0:
-            core = half
-        place = slot * size + starts[k] + ((half if core == 0 else 1 - half) if k > 0 else 0)
+        direct = (slot, k, "halo" if core else "own")
+        if direct in starts:
+            place, core = starts[direct], half
+        else:
+            place = starts[slot, k, "both"] + (1 - half if core else half)
         return tuple(
             jnp.where(head == core, got[place, rows], swapped[place, rows])
             for rows in (pl.ds(start, count), pl.ds(pixels, 16))
@@ -222,8 +232,8 @@
     )
 
     def neighbour(slot):
-        above = odd if slot == 0 else jnp.logical_not(odd)
-        start = pl.multiple_of(jnp.where(above, pixels - halo, 0), 16)
+        up = odd if slot == 0 else jnp.logical_not(odd)
+        start = pl.multiple_of(jnp.where(up, pixels - halo, 0), 16)
         return jnp.concatenate(
             [
                 merge([block(1, slot, k, half, start, halo) for k in range(dates)], pixels, start, halo)
@@ -258,30 +268,38 @@
     )(mine, theirs, got, swapped, first, other, second)
 
 
-def arrangement(dates):
-    return list(range(dates - 1, -1, -1))
-
-
-def positions(dates):
+def messages(dates, slots):
+    found = []
+    for slot in range(slots):
+        for k in list(range(dates // 2, dates)) + list(range(dates // 2 - 1, -1, -1)):
+            if k in (0,):
+                found += [(slot, k, "own")] if k > 0 and slot == 0 else []
+                found.append((slot, k, "halo"))
+            else:
+                found.append((slot, k, "both"))
+    return found
+
+
+def positions(dates, slots):
     starts, size = {}, 0
-    for k in arrangement(dates):
-        starts[k] = size
-        size += 2 if k > 0 else 1
-    return starts, size
-
-
-def routes(dates, slabs, k, slot):
+    for message in messages(dates, slots):
+        starts[message] = size
+        size += 2 if message[2] == "both" else 1
+    return starts
+
+
+def routes(dates, slabs, slot, k, kind):
     place = lambda d, t, core: (d * slabs + t) * 2 + core
     pairs = []
     for d in range(dates):
         for t in range(slabs):
             near = t ^ 1 if slot == 0 else ((t + 1) ^ 1) - 1
-            if k > 0 and slot == 0:
-                pairs.append((place(d, t, 0), place(d ^ k, t, 0)))
-            if k == 0 and 0 <= near < slabs:
-                pairs.append((place(d, t, 0), place(d, near, 0)))
-            if 0 <= near < slabs:
-                pairs.append((place(d, t, 1), place(d ^ k, near, 1)))
+            for core in range(2):
+                own = kind == "own" or (kind == "both" and core == 0)
+                if own and slot == 0:
+                    pairs.append((place(d, t, core), place(d ^ k, t, core)))
+                if not own and 0 <= near < slabs:
+                    pairs.append((place(d, t, core), place(d ^ k, near, core)))
     return pairs
 
 
@@ -296,12 +314,10 @@
     mine = attend(tokens, cloud_mask, day_of_year, query, key_weight, value_weight)
     theirs = lax.ppermute(mine, "head", swap)
     pieces = []
-    for slot in range(slots):
-        for k in arrangement(tiles):
-            block = jnp.stack([mine[k], theirs[k]]) if k > 0 else mine[:1]
-            pieces.append(
-                lax.ppermute(block, ("date", "tile", "head"), routes(tiles, slabs, k, slot))
-            )
+    for slot, k, kind in messages(tiles, slots):
+        block = jnp.stack([mine[k], theirs[k]]) if kind == "both" else mine[k : k + 1]
+        pairs = routes(tiles, slabs, slot, k, kind)
+        pieces.append(lax.ppermute(block, ("date", "tile", "head"), pairs))
     got = jnp.concatenate(pieces)
     swapped = lax.ppermute(got, "head", swap)
     out = convolve(mine, theirs, got, swapped, first, other, second, pixels, cols, slabs, slots)

time: 17.3 us -> 17.2 us (level)
  waiting for transfers between devices: 5.46 us -> 5.26 us
    ppermute x1, starting transfers between devices: 0.07 us -> 0.34 us  [local(): swapped = lax.ppermute(got, 'head', swap)]
    ppermute x1, waiting for transfers between devices: 1.27 us -> 1 us  [local(): swapped = lax.ppermute(got, 'head', swap)]
where the time goes in v4:
time: 17.2 us; the launch traced here: 17 us
  starting transfers between devices  7.89 us (46%)
  waiting for transfers between devices  5.26 us (31%)
  Pallas kernels  3.8 us (22%)
    ppermute x4, starting transfers between devices, local(): pieces.append(lax.ppermute(block, ('date', 'tile', 'head'), pairs))  6.87 us
    ppermute x4, waiting for transfers between devices, local(): pieces.append(lax.ppermute(block, ('date', 'tile', 'head'), pairs))  4.25 us
    pallas_call x1, Pallas kernels, attend(): pl.pallas_call(functools.partial(attend_kernel, dates), in_specs=[pl.Bloc...  2.38 us
    pallas_call x1, Pallas kernels, convolve(): pl.pallas_call(functools.partial(convolve_kernel, pixels, cols, slabs, sl...  1.42 us
    ppermute x1, waiting for transfers between devices, local(): swapped = lax.ppermute(got, 'head', swap)  1 us
    ppermute x1, starting transfers between devices, local(): theirs = lax.ppermute(mine, 'head', swap)  0.52 us
    ppermute x1, starting transfers between devices, local(): swapped = lax.ppermute(got, 'head', swap)  0.34 us
  transfers between devices with their start and end apart: 7, of which 3 were waited for; matrix products, arithmetic and copies ran while one was open for 0% of the time, Pallas kernels for 0%

profile of v4, /device:TPU:0, one launch (start us, length us, event | category | flops | bytes accessed | tf_op | source)
XLA Modules:
  0.0 17.0 jit_solution(9343129774444446877)
XLA Ops:
  0.0 0.0 copy-start
  0.0 0.0 copy-start.1
  0.0 2.4 %shard_map.82.mine = bf16[4,48,128]{2,1,0:T(8,128)(2,1)S(1)} custom-call(bf16[4,512,256]{2,1,0:T(8,128)(2,1)} %bitcast.9, s32[4,32,16]{2,1,0:T(8,128)} %bitcast.10, s32[16]{0:T(128)} %days_hbm.1, f32[1,128]{1,0:T(1,128)} %bitcast.11, bf16[256,128]{1,0:T(8,128)(2,1)} %keyw_hbm.1, bf16[256,128]{1,0:T(8,128)(2,1)} %valw_hbm.1), custom_call_target="tpu_custom_call" | custom-call | tf_op jit(solution)/shard_map/pallas_call | solution.py:147
  2.4 0.5 %collective-permute-start = (bf16[4,48,128]{2,1,0:T(8,128)(2,1)S(1)}, bf16[4,48,128]{2,1,0:T(8,128)(2,1)S(1)}, u32[]{:S(2)}, u32[]{:S(2)}) collective-permute-start(bf16[4,48,128]{2,1,0:T(8,128)(2,1)S(1)} %shard_map.82.mine), channel_id=1, source_target_pairs={{0,1},{1,0},{2,3},{3,2},{4,5},{5,4},{6,7},{7,6},{8,9},{9,8},{10,11... | collective-permute-start | bytes 147464 | tf_op jit(solution)/shard_map/ppermute | solution.py:315
  2.9 2.6 %collective-permute-start.4 = (bf16[1,48,128]{2,1,0:T(8,128)(2,1)S(1)}, bf16[1,48,128]{2,1,0:T(8,128)(2,1)S(1)}, u32[]{:S(2)}, u32[]{:S(2)}) collective-permute-start(bf16[1,48,128]{2,1,0:T(8,128)(2,1)S(1)} %get-tuple-element.5), channel_id=1, source_target_pairs={{0,2},{1,3},{2,0},{3,1},{4,6},{5,7},{6,4},{7,5},{8,10},{9,11},{10,... | collective-permute-start | bytes 36872 | tf_op jit(solution)/shard_map/ppermute | solution.py:320
  5.5 0.0 copy-done
  5.5 0.2 collective-permute-start.6
  5.7 0.0 collective-permute-done.theirs
  5.7 2.6 %collective-permute-start.1 = (bf16[2,48,128]{2,1,0:T(8,128)(2,1)S(1)}, bf16[2,48,128]{2,1,0:T(8,128)(2,1)S(1)}, u32[]{:S(2)}, u32[]{:S(2)}) collective-permute-start(bf16[2,48,128]{2,1,0:T(8,128)(2,1)S(1)} %pad_maximum_fusion), channel_id=1, source_target_pairs={{0,8},{1,11},{2,10},{3,9},{4,12},{5,15},{6,14},{7,13},{8,0},{9,3},... | collective-permute-start | bytes 73736 | tf_op jit(solution)/shard_map/ppermute | solution.py:320
  8.3 1.3 %collective-permute-start.2 = (bf16[2,48,128]{2,1,0:T(8,128)(2,1)S(1)}, bf16[2,48,128]{2,1,0:T(8,128)(2,1)S(1)}, u32[]{:S(2)}, u32[]{:S(2)}) collective-permute-start(bf16[2,48,128]{2,1,0:T(8,128)(2,1)S(1)} %pad_maximum_fusion.1), channel_id=1, source_target_pairs={{0,12},{1,15},{2,14},{3,13},{4,8},{5,11},{6,10},{7,9},{8,4},{9,7},... | collective-permute-start | bytes 73736 | tf_op jit(solution)/shard_map/ppermute | solution.py:320
  9.7 0.3 %collective-permute-start.3 = (bf16[2,48,128]{2,1,0:T(8,128)(2,1)S(1)}, bf16[2,48,128]{2,1,0:T(8,128)(2,1)S(1)}, u32[]{:S(2)}, u32[]{:S(2)}) collective-permute-start(bf16[2,48,128]{2,1,0:T(8,128)(2,1)S(1)} %pad_maximum_fusion.2), channel_id=1, source_target_pairs={{0,4},{1,7},{2,6},{3,5},{4,0},{5,3},{6,2},{7,1},{8,12},{9,15},{10,... | collective-permute-start | bytes 73736 | tf_op jit(solution)/shard_map/ppermute | solution.py:320
  10.0 0.5 %collective-permute-done.1 = bf16[2,48,128]{2,1,0:T(8,128)(2,1)S(1)} collective-permute-done((bf16[2,48,128]{2,1,0:T(8,128)(2,1)S(1)}, bf16[2,48,128]{2,1,0:T(8,128)(2,1)S(1)}, u32[]{:S(2)}, u32[]{:S(2)}) %collective-permute-start.1) | collective-permute-done | bytes 24608 | tf_op jit(solution)/shard_map/ppermute | solution.py:320
  10.5 3.8 %collective-permute-done.2 = bf16[2,48,128]{2,1,0:T(8,128)(2,1)S(1)} collective-permute-done((bf16[2,48,128]{2,1,0:T(8,128)(2,1)S(1)}, bf16[2,48,128]{2,1,0:T(8,128)(2,1)S(1)}, u32[]{:S(2)}, u32[]{:S(2)}) %collective-permute-start.2) | collective-permute-done | bytes 24608 | tf_op jit(solution)/shard_map/ppermute | solution.py:320
  14.2 0.0 collective-permute-done.3
  14.2 0.0 collective-permute-done.4
  14.3 0.3 %collective-permute-start.5 = (bf16[7,48,128]{2,1,0:T(8,128)(2,1)S(1)}, bf16[7,48,128]{2,1,0:T(8,128)(2,1)S(1)}, u32[]{:S(2)}, u32[]{:S(2)}) collective-permute-start(bf16[7,48,128]{2,1,0:T(8,128)(2,1)S(1)} %constant_dynamic-update-slice_fusion.got), channel_id=1, source_target_pairs={{0,1},{1,0},{2,3},{3,2},{4,5},{5,4},{6,7},{7,6},{8,9},{9,8},{10,11... | collective-permute-start | bytes 258056 | tf_op jit(solution)/shard_map/ppermute | solution.py:322
  14.6 1.0 %collective-permute-done.5.swapped = bf16[7,48,128]{2,1,0:T(8,128)(2,1)S(1)} collective-permute-done((bf16[7,48,128]{2,1,0:T(8,128)(2,1)S(1)}, bf16[7,48,128]{2,1,0:T(8,128)(2,1)S(1)}, u32[]{:S(2)}, u32[]{:S(2)}) %collective-permute-start.5) | collective-permute-done | bytes 86048 | tf_op jit(solution)/shard_map/ppermute | solution.py:322
  15.6 0.0 collective-permute-done.6.other
  15.6 0.0 copy-done.1
  15.6 1.4 %shard_map.83 = bf16[32,128]{1,0:T(8,128)(2,1)} custom-call(bf16[4,48,128]{2,1,0:T(8,128)(2,1)S(1)} %shard_map.82.mine, bf16[4,48,128]{2,1,0:T(8,128)(2,1)S(1)} %collective-permute-done.theirs, bf16[7,48,128]{2,1,0:T(8,128)(2,1)S(1)} %constant_dynamic-update-slice_fusion.got, bf16[7,48,128]{2,1,0:T(8,128)(2,1)S(1)} %collective-permute-done.5.swapped, ...), custom_call_target="tpu_custom_call" | custom-call | tf_op jit(solution)/shard_map/pallas_call | solution.py:262
  (9 shorter events, 0.1 us)
Async XLA Ops:
  0.0 5.5 %copy-start = (bf16[3,3,256,128]{3,2,1,0:T(8,128)(2,1)S(1)}, bf16[3,3,256,128]{3,2,1,0:T(8,128)(2,1)}, u32[]{:S(2)}) copy-start(bf16[3,3,256,128]{3,2,1,0:T(8,128)(2,1)} %param.14) | copy-start | bytes 1769476
  0.0 15.6 %copy-start.1 = (bf16[3,3,256,128]{3,2,1,0:T(8,128)(2,1)S(1)}, bf16[3,3,256,128]{3,2,1,0:T(8,128)(2,1)}, u32[]{:S(2)}) copy-start(bf16[3,3,256,128]{3,2,1,0:T(8,128)(2,1)} %param.15) | copy-start | bytes 1769476
  2.4 3.3 %collective-permute-start = (bf16[4,48,128]{2,1,0:T(8,128)(2,1)S(1)}, bf16[4,48,128]{2,1,0:T(8,128)(2,1)S(1)}, u32[]{:S(2)}, u32[]{:S(2)}) collective-permute-start(bf16[4,48,128]{2,1,0:T(8,128)(2,1)S(1)} %shard_map.82.mine), channel_id=1, source_target_pairs={{0,1},{1,0},{2,3},{3,2},{4,5},{5,4},{6,7},{7,6},{8,9},{9,8},{10,11... | collective-permute-start | bytes 147464 | tf_op jit(solution)/shard_map/ppermute | solution.py:315
  2.9 11.3 %collective-permute-start.4 = (bf16[1,48,128]{2,1,0:T(8,128)(2,1)S(1)}, bf16[1,48,128]{2,1,0:T(8,128)(2,1)S(1)}, u32[]{:S(2)}, u32[]{:S(2)}) collective-permute-start(bf16[1,48,128]{2,1,0:T(8,128)(2,1)S(1)} %get-tuple-element.5), channel_id=1, source_target_pairs={{0,2},{1,3},{2,0},{3,1},{4,6},{5,7},{6,4},{7,5},{8,10},{9,11},{10,... | collective-permute-start | bytes 36872 | tf_op jit(solution)/shard_map/ppermute | solution.py:320
  5.5 10.1 %collective-permute-start.6 = (bf16[3,768,128]{2,1,0:T(8,128)(2,1)S(1)}, bf16[3,768,128]{2,1,0:T(8,128)(2,1)S(1)}, u32[]{:S(2)}, u32[]{:S(2)}) collective-permute-start(bf16[3,768,128]{2,1,0:T(8,128)(2,1)S(1)} %bitcast.6), channel_id=1, source_target_pairs={{0,1},{1,0},{2,3},{3,2},{4,5},{5,4},{6,7},{7,6},{8,9},{9,8},{10,11... | collective-permute-start | bytes 1769480 | tf_op jit(solution)/shard_map/ppermute | solution.py:313
  5.7 4.8 %collective-permute-start.1 = (bf16[2,48,128]{2,1,0:T(8,128)(2,1)S(1)}, bf16[2,48,128]{2,1,0:T(8,128)(2,1)S(1)}, u32[]{:S(2)}, u32[]{:S(2)}) collective-permute-start(bf16[2,48,128]{2,1,0:T(8,128)(2,1)S(1)} %pad_maximum_fusion), channel_id=1, source_target_pairs={{0,8},{1,11},{2,10},{3,9},{4,12},{5,15},{6,14},{7,13},{8,0},{9,3},... | collective-permute-start | bytes 73736 | tf_op jit(solution)/shard_map/ppermute | solution.py:320
  8.3 5.9 %collective-permute-start.2 = (bf16[2,48,128]{2,1,0:T(8,128)(2,1)S(1)}, bf16[2,48,128]{2,1,0:T(8,128)(2,1)S(1)}, u32[]{:S(2)}, u32[]{:S(2)}) collective-permute-start(bf16[2,48,128]{2,1,0:T(8,128)(2,1)S(1)} %pad_maximum_fusion.1), channel_id=1, source_target_pairs={{0,12},{1,15},{2,14},{3,13},{4,8},{5,11},{6,10},{7,9},{8,4},{9,7},... | collective-permute-start | bytes 73736 | tf_op jit(solution)/shard_map/ppermute | solution.py:320
  9.7 4.6 %collective-permute-start.3 = (bf16[2,48,128]{2,1,0:T(8,128)(2,1)S(1)}, bf16[2,48,128]{2,1,0:T(8,128)(2,1)S(1)}, u32[]{:S(2)}, u32[]{:S(2)}) collective-permute-start(bf16[2,48,128]{2,1,0:T(8,128)(2,1)S(1)} %pad_maximum_fusion.2), channel_id=1, source_target_pairs={{0,4},{1,7},{2,6},{3,5},{4,0},{5,3},{6,2},{7,1},{8,12},{9,15},{10,... | collective-permute-start | bytes 73736 | tf_op jit(solution)/shard_map/ppermute | solution.py:320
  14.3 1.3 %collective-permute-start.5 = (bf16[7,48,128]{2,1,0:T(8,128)(2,1)S(1)}, bf16[7,48,128]{2,1,0:T(8,128)(2,1)S(1)}, u32[]{:S(2)}, u32[]{:S(2)}) collective-permute-start(bf16[7,48,128]{2,1,0:T(8,128)(2,1)S(1)} %constant_dynamic-update-slice_fusion.got), channel_id=1, source_target_pairs={{0,1},{1,0},{2,3},{3,2},{4,5},{5,4},{6,7},{7,6},{8,9},{9,8},{10,11... | collective-permute-start | bytes 258056 | tf_op jit(solution)/shard_map/ppermute | solution.py:322

commit v5 on v4

--- a/solution.py
+++ b/solution.py
@@ -14,6 +14,16 @@
 LOG2E = math.log2(math.e)
 F32 = jnp.float32
 BF16 = jnp.bfloat16
+
+
+def along(d, k, dates):
+    if dates & (dates - 1):
+        return (d + k) % dates
+    rank, shift = d, 1
+    while shift < dates:
+        rank, shift = rank ^ (rank >> shift), 2 * shift
+    rank = (rank + k) & (dates - 1)
+    return rank ^ (rank >> 1)
 
 
 def iota(shape, dim):
@@ -118,7 +128,7 @@
     for copy in small:
         copy.start()
     loads = [
-        pltpu.make_async_copy(tokens_hbm.at[date ^ i], tokens.at[i], token_sems.at[i]) for i in range(tiles)
+        pltpu.make_async_copy(tokens_hbm.at[along(date, i, tiles)], tokens.at[i], token_sems.at[i]) for i in range(tiles)
     ]
     for copy in loads:
         copy.start()
@@ -136,7 +146,7 @@
     small[4].wait()
     for copy in loads:
         copy.wait()
-    pool_all(tiles, out, tokens, table, weights, lambda i: mask[date ^ i])
+    pool_all(tiles, out, tokens, table, weights, lambda i: mask[along(date, i, tiles)])
 
 
 def attend(tokens, cloud_mask, day_of_year, query, key_weight, value_weight):
@@ -207,11 +217,11 @@
     starts = positions(dates, slots)
 
     def block(core, slot, k, half, start, count):
-        direct = (slot, k, "halo" if core else "own")
-        if direct in starts:
-            place, core = starts[direct], half
+        place = starts[slot, k]
+        if k > 0:
+            place += 1 - half if core else half
         else:
-            place = starts[slot, k, "both"] + (1 - half if core else half)
+            core = half
         return tuple(
             jnp.where(head == core, got[place, rows], swapped[place, rows])
             for rows in (pl.ds(start, count), pl.ds(pixels, 16))
@@ -269,37 +279,29 @@
 
 
 def messages(dates, slots):
-    found = []
-    for slot in range(slots):
-        for k in list(range(dates // 2, dates)) + list(range(dates // 2 - 1, -1, -1)):
-            if k in (0,):
-                found += [(slot, k, "own")] if k > 0 and slot == 0 else []
-                found.append((slot, k, "halo"))
-            else:
-                found.append((slot, k, "both"))
-    return found
+    return [(slot, k) for slot in range(slots) for k in list(range(1, dates)) + [0]]
 
 
 def positions(dates, slots):
     starts, size = {}, 0
     for message in messages(dates, slots):
         starts[message] = size
-        size += 2 if message[2] == "both" else 1
+        size += 2 if message[1] else 1
     return starts
 
 
-def routes(dates, slabs, slot, k, kind):
+def routes(dates, slabs, slot, k):
     place = lambda d, t, core: (d * slabs + t) * 2 + core
     pairs = []
     for d in range(dates):
         for t in range(slabs):
             near = t ^ 1 if slot == 0 else ((t + 1) ^ 1) - 1
             for core in range(2):
-                own = kind == "own" or (kind == "both" and core == 0)
+                own = k > 0 and core == 0
                 if own and slot == 0:
-                    pairs.append((place(d, t, core), place(d ^ k, t, core)))
+                    pairs.append((place(d, t, core), place(along(d, k, dates), t, core)))
                 if not own and 0 <= near < slabs:
-                    pairs.append((place(d, t, core), place(d ^ k, near, core)))
+                    pairs.append((place(d, t, core), place(along(d, k, dates), near, core)))
     return pairs
 
 
@@ -314,10 +316,9 @@
     mine = attend(tokens, cloud_mask, day_of_year, query, key_weight, value_weight)
     theirs = lax.ppermute(mine, "head", swap)
     pieces = []
-    for slot, k, kind in messages(tiles, slots):
-        block = jnp.stack([mine[k], theirs[k]]) if kind == "both" else mine[k : k + 1]
-        pairs = routes(tiles, slabs, slot, k, kind)
-        pieces.append(lax.ppermute(block, ("date", "tile", "head"), pairs))
+    for slot, k in messages(tiles, slots):
+        block = jnp.stack([mine[k], theirs[k]]) if k > 0 else mine[:1]
+        pieces.append(lax.ppermute(block, ("date", "tile", "head"), routes(tiles, slabs, slot, k)))
     got = jnp.concatenate(pieces)
     swapped = lax.ppermute(got, "head", swap)
     out = convolve(mine, theirs, got, swapped, first, other, second, pixels, cols, slabs, slots)

time: 17.2 us -> 16.7 us (0.971)
  waiting for transfers between devices: 5.26 us -> 3.43 us
  starting transfers between devices: 7.89 us -> 9.28 us
    ppermute x4, waiting for transfers between devices: 4.25 us -> 2.44 us  [local(): lax.ppermute(block, ('date', 'tile', 'head'), routes(tiles, slabs, slot, k))]
    ppermute x4, starting transfers between devices: 6.87 us -> 8.25 us  [local(): lax.ppermute(block, ('date', 'tile', 'head'), routes(tiles, slabs, slot, k))]
where the time goes in v5:
time: 16.7 us; the launch traced here: 16.6 us
  starting transfers between devices  9.28 us (56%)
  Pallas kernels  3.8 us (23%)
  waiting for transfers between devices  3.43 us (21%)
    ppermute x4, starting transfers between devices, local(): lax.ppermute(block, ('date', 'tile', 'head'), routes(tiles, slabs, slot, k))  8.25 us
    ppermute x4, waiting for transfers between devices, local(): lax.ppermute(block, ('date', 'tile', 'head'), routes(tiles, slabs, slot, k))  2.44 us
    pallas_call x1, Pallas kernels, attend(): pl.pallas_call(functools.partial(attend_kernel, dates), in_specs=[pl.Bloc...  2.38 us
    pallas_call x1, Pallas kernels, convolve(): pl.pallas_call(functools.partial(convolve_kernel, pixels, cols, slabs, sl...  1.42 us
    ppermute x1, waiting for transfers between devices, local(): swapped = lax.ppermute(got, 'head', swap)  0.98 us
    ppermute x1, starting transfers between devices, local(): theirs = lax.ppermute(mine, 'head', swap)  0.52 us
    ppermute x1, starting transfers between devices, local(): swapped = lax.ppermute(got, 'head', swap)  0.36 us
  transfers between devices with their start and end apart: 7, of which 3 were waited for; matrix products, arithmetic and copies ran while one was open for 0% of the time, Pallas kernels for 0%

profile of v5, /device:TPU:0, one launch (start us, length us, event | category | flops | bytes accessed | tf_op | source)
XLA Modules:
  0.0 16.6 jit_solution(3226636092150072871)
XLA Ops:
  0.0 0.0 copy-start
  0.0 0.0 copy-start.1
  0.0 2.4 %shard_map.82.mine = bf16[4,48,128]{2,1,0:T(8,128)(2,1)S(1)} custom-call(bf16[4,512,256]{2,1,0:T(8,128)(2,1)} %bitcast.9, s32[4,32,16]{2,1,0:T(8,128)} %bitcast.10, s32[16]{0:T(128)} %days_hbm.1, f32[1,128]{1,0:T(1,128)} %bitcast.11, bf16[256,128]{1,0:T(8,128)(2,1)} %keyw_hbm.1, bf16[256,128]{1,0:T(8,128)(2,1)} %valw_hbm.1), custom_call_target="tpu_custom_call" | custom-call | tf_op jit(solution)/shard_map/pallas_call | solution.py:157
  2.4 0.5 %collective-permute-start = (bf16[4,48,128]{2,1,0:T(8,128)(2,1)S(1)}, bf16[4,48,128]{2,1,0:T(8,128)(2,1)S(1)}, u32[]{:S(2)}, u32[]{:S(2)}) collective-permute-start(bf16[4,48,128]{2,1,0:T(8,128)(2,1)S(1)} %shard_map.82.mine), channel_id=1, source_target_pairs={{0,1},{1,0},{2,3},{3,2},{4,5},{5,4},{6,7},{7,6},{8,9},{9,8},{10,11... | collective-permute-start | bytes 147464 | tf_op jit(solution)/shard_map/ppermute | solution.py:317
  2.9 2.6 %collective-permute-start.4 = (bf16[1,48,128]{2,1,0:T(8,128)(2,1)S(1)}, bf16[1,48,128]{2,1,0:T(8,128)(2,1)S(1)}, u32[]{:S(2)}, u32[]{:S(2)}) collective-permute-start(bf16[1,48,128]{2,1,0:T(8,128)(2,1)S(1)} %get-tuple-element.5), channel_id=1, source_target_pairs={{0,2},{1,3},{2,0},{3,1},{4,6},{5,7},{6,4},{7,5},{8,10},{9,11},{10,... | collective-permute-start | bytes 36872 | tf_op jit(solution)/shard_map/ppermute | solution.py:321
  5.5 0.0 copy-done
  5.5 0.2 collective-permute-start.6
  5.7 0.0 collective-permute-done.theirs
  5.7 1.6 %collective-permute-start.1 = (bf16[2,48,128]{2,1,0:T(8,128)(2,1)S(1)}, bf16[2,48,128]{2,1,0:T(8,128)(2,1)S(1)}, u32[]{:S(2)}, u32[]{:S(2)}) collective-permute-start(bf16[2,48,128]{2,1,0:T(8,128)(2,1)S(1)} %pad_maximum_fusion), channel_id=1, source_target_pairs={{0,4},{1,7},{2,6},{3,5},{4,12},{5,15},{6,14},{7,13},{8,0},{9,3},{1... | collective-permute-start | bytes 73736 | tf_op jit(solution)/shard_map/ppermute | solution.py:321
  7.3 2.5 %collective-permute-start.2 = (bf16[2,48,128]{2,1,0:T(8,128)(2,1)S(1)}, bf16[2,48,128]{2,1,0:T(8,128)(2,1)S(1)}, u32[]{:S(2)}, u32[]{:S(2)}) collective-permute-start(bf16[2,48,128]{2,1,0:T(8,128)(2,1)S(1)} %pad_maximum_fusion.1), channel_id=1, source_target_pairs={{0,12},{1,15},{2,14},{3,13},{4,8},{5,11},{6,10},{7,9},{8,4},{9,7},... | collective-permute-start | bytes 73736 | tf_op jit(solution)/shard_map/ppermute | solution.py:321
  9.8 1.6 %collective-permute-start.3 = (bf16[2,48,128]{2,1,0:T(8,128)(2,1)S(1)}, bf16[2,48,128]{2,1,0:T(8,128)(2,1)S(1)}, u32[]{:S(2)}, u32[]{:S(2)}) collective-permute-start(bf16[2,48,128]{2,1,0:T(8,128)(2,1)S(1)} %pad_maximum_fusion.2), channel_id=1, source_target_pairs={{0,8},{1,11},{2,10},{3,9},{4,0},{5,3},{6,2},{7,1},{8,12},{9,15},{1... | collective-permute-start | bytes 73736 | tf_op jit(solution)/shard_map/ppermute | solution.py:321
  11.4 0.0 collective-permute-done.1
  11.4 1.9 %collective-permute-done.2 = bf16[2,48,128]{2,1,0:T(8,128)(2,1)S(1)} collective-permute-done((bf16[2,48,128]{2,1,0:T(8,128)(2,1)S(1)}, bf16[2,48,128]{2,1,0:T(8,128)(2,1)S(1)}, u32[]{:S(2)}, u32[]{:S(2)}) %collective-permute-start.2) | collective-permute-done | bytes 24608 | tf_op jit(solution)/shard_map/ppermute | solution.py:321
  13.2 0.6 %collective-permute-done.3 = bf16[2,48,128]{2,1,0:T(8,128)(2,1)S(1)} collective-permute-done((bf16[2,48,128]{2,1,0:T(8,128)(2,1)S(1)}, bf16[2,48,128]{2,1,0:T(8,128)(2,1)S(1)}, u32[]{:S(2)}, u32[]{:S(2)}) %collective-permute-start.3) | collective-permute-done | bytes 24608 | tf_op jit(solution)/shard_map/ppermute | solution.py:321
  13.8 0.0 collective-permute-done.4
  13.8 0.4 %collective-permute-start.5 = (bf16[7,48,128]{2,1,0:T(8,128)(2,1)S(1)}, bf16[7,48,128]{2,1,0:T(8,128)(2,1)S(1)}, u32[]{:S(2)}, u32[]{:S(2)}) collective-permute-start(bf16[7,48,128]{2,1,0:T(8,128)(2,1)S(1)} %constant_dynamic-update-slice_fusion.got), channel_id=1, source_target_pairs={{0,1},{1,0},{2,3},{3,2},{4,5},{5,4},{6,7},{7,6},{8,9},{9,8},{10,11... | collective-permute-start | bytes 258056 | tf_op jit(solution)/shard_map/ppermute | solution.py:323
  14.2 1.0 %collective-permute-done.5.swapped = bf16[7,48,128]{2,1,0:T(8,128)(2,1)S(1)} collective-permute-done((bf16[7,48,128]{2,1,0:T(8,128)(2,1)S(1)}, bf16[7,48,128]{2,1,0:T(8,128)(2,1)S(1)}, u32[]{:S(2)}, u32[]{:S(2)}) %collective-permute-start.5) | collective-permute-done | bytes 86048 | tf_op jit(solution)/shard_map/ppermute | solution.py:323
  15.2 0.0 collective-permute-done.6.other
  15.2 0.0 copy-done.1
  15.2 1.4 %shard_map.83 = bf16[32,128]{1,0:T(8,128)(2,1)} custom-call(bf16[4,48,128]{2,1,0:T(8,128)(2,1)S(1)} %shard_map.82.mine, bf16[4,48,128]{2,1,0:T(8,128)(2,1)S(1)} %collective-permute-done.theirs, bf16[7,48,128]{2,1,0:T(8,128)(2,1)S(1)} %constant_dynamic-update-slice_fusion.got, bf16[7,48,128]{2,1,0:T(8,128)(2,1)S(1)} %collective-permute-done.5.swapped, ...), custom_call_target="tpu_custom_call" | custom-call | tf_op jit(solution)/shard_map/pallas_call | solution.py:272
  (9 shorter events, 0.0 us)
Async XLA Ops:
  0.0 5.5 %copy-start = (bf16[3,3,256,128]{3,2,1,0:T(8,128)(2,1)S(1)}, bf16[3,3,256,128]{3,2,1,0:T(8,128)(2,1)}, u32[]{:S(2)}) copy-start(bf16[3,3,256,128]{3,2,1,0:T(8,128)(2,1)} %param.14) | copy-start | bytes 1769476
  0.0 15.2 %copy-start.1 = (bf16[3,3,256,128]{3,2,1,0:T(8,128)(2,1)S(1)}, bf16[3,3,256,128]{3,2,1,0:T(8,128)(2,1)}, u32[]{:S(2)}) copy-start(bf16[3,3,256,128]{3,2,1,0:T(8,128)(2,1)} %param.15) | copy-start | bytes 1769476
  2.4 3.3 %collective-permute-start = (bf16[4,48,128]{2,1,0:T(8,128)(2,1)S(1)}, bf16[4,48,128]{2,1,0:T(8,128)(2,1)S(1)}, u32[]{:S(2)}, u32[]{:S(2)}) collective-permute-start(bf16[4,48,128]{2,1,0:T(8,128)(2,1)S(1)} %shard_map.82.mine), channel_id=1, source_target_pairs={{0,1},{1,0},{2,3},{3,2},{4,5},{5,4},{6,7},{7,6},{8,9},{9,8},{10,11... | collective-permute-start | bytes 147464 | tf_op jit(solution)/shard_map/ppermute | solution.py:317
  2.9 10.9 %collective-permute-start.4 = (bf16[1,48,128]{2,1,0:T(8,128)(2,1)S(1)}, bf16[1,48,128]{2,1,0:T(8,128)(2,1)S(1)}, u32[]{:S(2)}, u32[]{:S(2)}) collective-permute-start(bf16[1,48,128]{2,1,0:T(8,128)(2,1)S(1)} %get-tuple-element.5), channel_id=1, source_target_pairs={{0,2},{1,3},{2,0},{3,1},{4,6},{5,7},{6,4},{7,5},{8,10},{9,11},{10,... | collective-permute-start | bytes 36872 | tf_op jit(solution)/shard_map/ppermute | solution.py:321
  5.5 9.7 %collective-permute-start.6 = (bf16[3,768,128]{2,1,0:T(8,128)(2,1)S(1)}, bf16[3,768,128]{2,1,0:T(8,128)(2,1)S(1)}, u32[]{:S(2)}, u32[]{:S(2)}) collective-permute-start(bf16[3,768,128]{2,1,0:T(8,128)(2,1)S(1)} %bitcast.6), channel_id=1, source_target_pairs={{0,1},{1,0},{2,3},{3,2},{4,5},{5,4},{6,7},{7,6},{8,9},{9,8},{10,11... | collective-permute-start | bytes 1769480 | tf_op jit(solution)/shard_map/ppermute | solution.py:315
  5.7 5.7 %collective-permute-start.1 = (bf16[2,48,128]{2,1,0:T(8,128)(2,1)S(1)}, bf16[2,48,128]{2,1,0:T(8,128)(2,1)S(1)}, u32[]{:S(2)}, u32[]{:S(2)}) collective-permute-start(bf16[2,48,128]{2,1,0:T(8,128)(2,1)S(1)} %pad_maximum_fusion), channel_id=1, source_target_pairs={{0,4},{1,7},{2,6},{3,5},{4,12},{5,15},{6,14},{7,13},{8,0},{9,3},{1... | collective-permute-start | bytes 73736 | tf_op jit(solution)/shard_map/ppermute | solution.py:321
  7.3 5.9 %collective-permute-start.2 = (bf16[2,48,128]{2,1,0:T(8,128)(2,1)S(1)}, bf16[2,48,128]{2,1,0:T(8,128)(2,1)S(1)}, u32[]{:S(2)}, u32[]{:S(2)}) collective-permute-start(bf16[2,48,128]{2,1,0:T(8,128)(2,1)S(1)} %pad_maximum_fusion.1), channel_id=1, source_target_pairs={{0,12},{1,15},{2,14},{3,13},{4,8},{5,11},{6,10},{7,9},{8,4},{9,7},... | collective-permute-start | bytes 73736 | tf_op jit(solution)/shard_map/ppermute | solution.py:321
  9.8 4.0 %collective-permute-start.3 = (bf16[2,48,128]{2,1,0:T(8,128)(2,1)S(1)}, bf16[2,48,128]{2,1,0:T(8,128)(2,1)S(1)}, u32[]{:S(2)}, u32[]{:S(2)}) collective-permute-start(bf16[2,48,128]{2,1,0:T(8,128)(2,1)S(1)} %pad_maximum_fusion.2), channel_id=1, source_target_pairs={{0,8},{1,11},{2,10},{3,9},{4,0},{5,3},{6,2},{7,1},{8,12},{9,15},{1... | collective-permute-start | bytes 73736 | tf_op jit(solution)/shard_map/ppermute | solution.py:321
  13.8 1.3 %collective-permute-start.5 = (bf16[7,48,128]{2,1,0:T(8,128)(2,1)S(1)}, bf16[7,48,128]{2,1,0:T(8,128)(2,1)S(1)}, u32[]{:S(2)}, u32[]{:S(2)}) collective-permute-start(bf16[7,48,128]{2,1,0:T(8,128)(2,1)S(1)} %constant_dynamic-update-slice_fusion.got), channel_id=1, source_target_pairs={{0,1},{1,0},{2,3},{3,2},{4,5},{5,4},{6,7},{7,6},{8,9},{9,8},{10,11... | collective-permute-start | bytes 258056 | tf_op jit(solution)/shard_map/ppermute | solution.py:323

commit v6 on v5

--- a/solution.py
+++ b/solution.py
@@ -203,7 +203,7 @@
     return sum(dot(field, kernel[a])[a * cols : a * cols + count] for a in range(3))
 
 
-def convolve_kernel(pixels, cols, slabs, slots, mine, theirs, got, swapped, first, other, second, out):
+def convolve_kernel(pixels, cols, slabs, slots, mine, theirs, *refs):
     dates = mine.shape[0]
     slab, head = lax.axis_index("tile"), lax.axis_index("head")
     odd = lax.rem(slab, 2) == 1
@@ -214,16 +214,18 @@
             [jnp.where(head == 0, own, partner), jnp.where(head == 0, partner, own)], axis=1
         )
 
-    starts = positions(dates, slots)
+    places = positions(dates, slots)
+    parts = (len(refs) - 4) // 2
+    got, swapped, (first, other, second, out) = refs[:parts], refs[parts:-4], refs[-4:]
 
     def block(core, slot, k, half, start, count):
-        place = starts[slot, k]
+        which, place = places[slot, k]
         if k > 0:
             place += 1 - half if core else half
         else:
             core = half
         return tuple(
-            jnp.where(head == core, got[place, rows], swapped[place, rows])
+            jnp.where(head == core, got[which][place, rows], swapped[which][place, rows])
             for rows in (pl.ds(start, count), pl.ds(pixels, 16))
         )
 
@@ -271,11 +273,11 @@
 def convolve(mine, theirs, got, swapped, first, other, second, pixels, cols, slabs, slots):
     return pl.pallas_call(
         functools.partial(convolve_kernel, pixels, cols, slabs, slots),
-        in_specs=[pl.BlockSpec(memory_space=pltpu.VMEM)] * 7,
+        in_specs=[pl.BlockSpec(memory_space=pltpu.VMEM)] * (5 + 2 * len(got)),
         out_specs=pl.BlockSpec(memory_space=pltpu.VMEM),
         out_shape=jax.ShapeDtypeStruct((pixels, second.shape[-1]), BF16),
         compiler_params=pltpu.CompilerParams(vmem_limit_bytes=32 * 2**20),
-    )(mine, theirs, got, swapped, first, other, second)
+    )(mine, theirs, *got, *swapped, first, other, second)
 
 
 def messages(dates, slots):
@@ -283,11 +285,12 @@
 
 
 def positions(dates, slots):
-    starts, size = {}, 0
-    for message in messages(dates, slots):
-        starts[message] = size
-        size += 2 if message[1] else 1
-    return starts
+    places, sizes = {}, {}
+    for slot, k in messages(dates, slots):
+        which = max(k - (dates - 3), 0)
+        places[slot, k] = (which, sizes.get(which, 0))
+        sizes[which] = sizes.get(which, 0) + (2 if k else 1)
+    return places
 
 
 def routes(dates, slabs, slot, k):
@@ -315,12 +318,13 @@
     other = lax.ppermute(first, "head", swap)
     mine = attend(tokens, cloud_mask, day_of_year, query, key_weight, value_weight)
     theirs = lax.ppermute(mine, "head", swap)
-    pieces = []
-    for slot, k in messages(tiles, slots):
+    pieces = {}
+    for (slot, k), (which, _) in positions(tiles, slots).items():
         block = jnp.stack([mine[k], theirs[k]]) if k > 0 else mine[:1]
-        pieces.append(lax.ppermute(block, ("date", "tile", "head"), routes(tiles, slabs, slot, k)))
-    got = jnp.concatenate(pieces)
-    swapped = lax.ppermute(got, "head", swap)
+        piece = lax.ppermute(block, ("date", "tile", "head"), routes(tiles, slabs, slot, k))
+        pieces.setdefault(which, []).append(piece)
+    got = [jnp.concatenate(pieces[which]) for which in sorted(pieces)]
+    swapped = [lax.ppermute(part, "head", swap) for part in got]
     out = convolve(mine, theirs, got, swapped, first, other, second, pixels, cols, slabs, slots)
     return out.reshape(1, rows, cols, -1)
 

time: 16.7 us -> 16.6 us (level)
  waiting for transfers between devices: 3.43 us -> 2.65 us
  starting transfers between devices: 9.28 us -> 9.91 us
    ppermute x4, waiting for transfers between devices: 2.44 us -> 1.74 us  [local(): lax.ppermute(block, ('date', 'tile', 'head'), routes(tiles, slabs, slot, k))]
    ppermute x1 -> x3, starting transfers between devices: 0.36 us -> 0.99 us  [local(): swapped = [lax.ppermute(part, 'head', swap) for part in got]]
    ppermute x1 -> x3, waiting for transfers between devices: 0.98 us -> 0.9 us  [local(): swapped = [lax.ppermute(part, 'head', swap) for part in got]]
  transfers between devices with their start and end apart: 7 -> 9, of which waited for: 3 -> 4; matrix products, arithmetic and copies ran while one was open for 0% -> 0% of each run, Pallas kernels for 0% -> 0%
where the time goes in v6:
time: 16.6 us; the launch traced here: 16.4 us
  starting transfers between devices  9.91 us (60%)
  Pallas kernels  3.8 us (23%)
  waiting for transfers between devices  2.65 us (16%)
    ppermute x4, starting transfers between devices, local(): lax.ppermute(block, ('date', 'tile', 'head'), routes(tiles, slabs, slot, k))  8.25 us
    pallas_call x1, Pallas kernels, attend(): pl.pallas_call(functools.partial(attend_kernel, dates), in_specs=[pl.Bloc...  2.38 us
    ppermute x4, waiting for transfers between devices, local(): lax.ppermute(block, ('date', 'tile', 'head'), routes(tiles, slabs, slot, k))  1.74 us
    pallas_call x1, Pallas kernels, convolve(): pl.pallas_call(functools.partial(convolve_kernel, pixels, cols, slabs, sl...  1.42 us
    ppermute x3, starting transfers between devices, local(): swapped = [lax.ppermute(part, 'head', swap) for part in got]  0.99 us
    ppermute x3, waiting for transfers between devices, local(): swapped = [lax.ppermute(part, 'head', swap) for part in got]  0.9 us
    ppermute x1, starting transfers between devices, local(): theirs = lax.ppermute(mine, 'head', swap)  0.52 us
  transfers between devices with their start and end apart: 9, of which 4 were waited for; matrix products, arithmetic and copies ran while one was open for 0% of the time, Pallas kernels for 0%

profile of v6, /device:TPU:0, one launch (start us, length us, event | category | flops | bytes accessed | tf_op | source)
XLA Modules:
  0.0 16.4 jit_solution(8009963492118387277)
XLA Ops:
  0.0 0.0 copy-start
  0.0 0.0 copy-start.1
  0.0 2.4 %shard_map.82.mine = bf16[4,48,128]{2,1,0:T(8,128)(2,1)S(1)} custom-call(bf16[4,512,256]{2,1,0:T(8,128)(2,1)} %bitcast.9, s32[4,32,16]{2,1,0:T(8,128)} %bitcast.10, s32[16]{0:T(128)} %days_hbm.1, f32[1,128]{1,0:T(1,128)} %bitcast.11, bf16[256,128]{1,0:T(8,128)(2,1)} %keyw_hbm.1, bf16[256,128]{1,0:T(8,128)(2,1)} %valw_hbm.1), custom_call_target="tpu_custom_call" | custom-call | tf_op jit(solution)/shard_map/pallas_call | solution.py:157
  2.4 0.5 %collective-permute-start = (bf16[4,48,128]{2,1,0:T(8,128)(2,1)S(1)}, bf16[4,48,128]{2,1,0:T(8,128)(2,1)S(1)}, u32[]{:S(2)}, u32[]{:S(2)}) collective-permute-start(bf16[4,48,128]{2,1,0:T(8,128)(2,1)S(1)} %shard_map.82.mine), channel_id=1, source_target_pairs={{0,1},{1,0},{2,3},{3,2},{4,5},{5,4},{6,7},{7,6},{8,9},{9,8},{10,11... | collective-permute-start | bytes 147464 | tf_op jit(solution)/shard_map/ppermute | solution.py:320
  2.9 2.6 %collective-permute-start.2 = (bf16[1,48,128]{2,1,0:T(8,128)(2,1)S(1)}, bf16[1,48,128]{2,1,0:T(8,128)(2,1)S(1)}, u32[]{:S(2)}, u32[]{:S(2)}) collective-permute-start(bf16[1,48,128]{2,1,0:T(8,128)(2,1)S(1)} %get-tuple-element.7), channel_id=1, source_target_pairs={{0,2},{1,3},{2,0},{3,1},{4,6},{5,7},{6,4},{7,5},{8,10},{9,11},{10,... | collective-permute-start | bytes 36872 | tf_op jit(solution)/shard_map/ppermute | solution.py:324
  5.5 0.0 copy-done
  5.5 0.2 collective-permute-start.8
  5.7 0.0 collective-permute-done.theirs
  5.7 1.6 %collective-permute-start.1 = (bf16[2,48,128]{2,1,0:T(8,128)(2,1)S(1)}, bf16[2,48,128]{2,1,0:T(8,128)(2,1)S(1)}, u32[]{:S(2)}, u32[]{:S(2)}) collective-permute-start(bf16[2,48,128]{2,1,0:T(8,128)(2,1)S(1)} %pad_maximum_fusion), channel_id=1, source_target_pairs={{0,4},{1,7},{2,6},{3,5},{4,12},{5,15},{6,14},{7,13},{8,0},{9,3},{1... | collective-permute-start | bytes 73736 | tf_op jit(solution)/shard_map/ppermute | solution.py:324
  7.3 2.5 %collective-permute-start.3 = (bf16[2,48,128]{2,1,0:T(8,128)(2,1)S(1)}, bf16[2,48,128]{2,1,0:T(8,128)(2,1)S(1)}, u32[]{:S(2)}, u32[]{:S(2)}) collective-permute-start(bf16[2,48,128]{2,1,0:T(8,128)(2,1)S(1)} %pad_maximum_fusion.1), channel_id=1, source_target_pairs={{0,12},{1,15},{2,14},{3,13},{4,8},{5,11},{6,10},{7,9},{8,4},{9,7},... | collective-permute-start | bytes 73736 | tf_op jit(solution)/shard_map/ppermute | solution.py:324
  9.8 1.6 %collective-permute-start.4 = (bf16[2,48,128]{2,1,0:T(8,128)(2,1)S(1)}, bf16[2,48,128]{2,1,0:T(8,128)(2,1)S(1)}, u32[]{:S(2)}, u32[]{:S(2)}) collective-permute-start(bf16[2,48,128]{2,1,0:T(8,128)(2,1)S(1)} %pad_maximum_fusion.2), channel_id=1, source_target_pairs={{0,8},{1,11},{2,10},{3,9},{4,0},{5,3},{6,2},{7,1},{8,12},{9,15},{1... | collective-permute-start | bytes 73736 | tf_op jit(solution)/shard_map/ppermute | solution.py:324
  11.4 0.0 collective-permute-done.1
  11.4 0.0 collective-permute-done.2
  11.4 0.7 %collective-permute-start.5 = (bf16[3,48,128]{2,1,0:T(8,128)(2,1)S(1)}, bf16[3,48,128]{2,1,0:T(8,128)(2,1)S(1)}, u32[]{:S(2)}, u32[]{:S(2)}) collective-permute-start(bf16[3,48,128]{2,1,0:T(8,128)(2,1)S(1)} %constant_dynamic-update-slice_fusion.refs_0_), channel_id=1, source_target_pairs={{0,1},{1,0},{2,3},{3,2},{4,5},{5,4},{6,7},{7,6},{8,9},{9,8},{10,11... | collective-permute-start | bytes 110600 | tf_op jit(solution)/shard_map/ppermute | solution.py:327
  12.1 1.1 %collective-permute-done.3.refs_1_ = bf16[2,48,128]{2,1,0:T(8,128)(2,1)S(1)} collective-permute-done((bf16[2,48,128]{2,1,0:T(8,128)(2,1)S(1)}, bf16[2,48,128]{2,1,0:T(8,128)(2,1)S(1)}, u32[]{:S(2)}, u32[]{:S(2)}) %collective-permute-start.3) | collective-permute-done | bytes 24608 | tf_op jit(solution)/shard_map/ppermute | solution.py:324
  13.2 0.0 collective-permute-start.6
  13.2 0.6 %collective-permute-done.4.refs_2_ = bf16[2,48,128]{2,1,0:T(8,128)(2,1)S(1)} collective-permute-done((bf16[2,48,128]{2,1,0:T(8,128)(2,1)S(1)}, bf16[2,48,128]{2,1,0:T(8,128)(2,1)S(1)}, u32[]{:S(2)}, u32[]{:S(2)}) %collective-permute-start.4) | collective-permute-done | bytes 24608 | tf_op jit(solution)/shard_map/ppermute | solution.py:324
  13.8 0.3 %collective-permute-start.7 = (bf16[2,48,128]{2,1,0:T(8,128)(2,1)S(1)}, bf16[2,48,128]{2,1,0:T(8,128)(2,1)S(1)}, u32[]{:S(2)}, u32[]{:S(2)}) collective-permute-start(bf16[2,48,128]{2,1,0:T(8,128)(2,1)S(1)} %collective-permute-done.4.refs_2_), channel_id=1, source_target_pairs={{0,1},{1,0},{2,3},{3,2},{4,5},{5,4},{6,7},{7,6},{8,9},{9,8},{10,11... | collective-permute-start | bytes 73736 | tf_op jit(solution)/shard_map/ppermute | solution.py:327
  14.1 0.3 %collective-permute-done.6.refs_4_ = bf16[2,48,128]{2,1,0:T(8,128)(2,1)S(1)} collective-permute-done((bf16[2,48,128]{2,1,0:T(8,128)(2,1)S(1)}, bf16[2,48,128]{2,1,0:T(8,128)(2,1)S(1)}, u32[]{:S(2)}, u32[]{:S(2)}) %collective-permute-start.6) | collective-permute-done | bytes 24608 | tf_op jit(solution)/shard_map/ppermute | solution.py:327
  14.4 0.6 %collective-permute-done.7.refs_5_ = bf16[2,48,128]{2,1,0:T(8,128)(2,1)S(1)} collective-permute-done((bf16[2,48,128]{2,1,0:T(8,128)(2,1)S(1)}, bf16[2,48,128]{2,1,0:T(8,128)(2,1)S(1)}, u32[]{:S(2)}, u32[]{:S(2)}) %collective-permute-start.7) | collective-permute-done | bytes 24608 | tf_op jit(solution)/shard_map/ppermute | solution.py:327
  15.0 0.0 collective-permute-done.5.refs_3_
  15.0 0.0 collective-permute-done.8.refs_7_
  15.0 0.0 copy-done.1
  15.0 1.4 %shard_map.83 = bf16[32,128]{1,0:T(8,128)(2,1)} custom-call(bf16[4,48,128]{2,1,0:T(8,128)(2,1)S(1)} %shard_map.82.mine, bf16[4,48,128]{2,1,0:T(8,128)(2,1)S(1)} %collective-permute-done.theirs, bf16[3,48,128]{2,1,0:T(8,128)(2,1)S(1)} %constant_dynamic-update-slice_fusion.refs_0_, bf16[2,48,128]{2,1,0:T(8,128)(2,1)S(1)} %collective-permute-done.3.refs_1_, ...), custom_call_target="tpu_custom_call" | custom-call | tf_op jit(solution)/shard_map/pallas_call | solution.py:274
  (7 shorter events, 0.0 us)
Async XLA Ops:
  0.0 5.5 %copy-start = (bf16[3,3,256,128]{3,2,1,0:T(8,128)(2,1)S(1)}, bf16[3,3,256,128]{3,2,1,0:T(8,128)(2,1)}, u32[]{:S(2)}) copy-start(bf16[3,3,256,128]{3,2,1,0:T(8,128)(2,1)} %param.14) | copy-start | bytes 1769476
  0.0 15.0 %copy-start.1 = (bf16[3,3,256,128]{3,2,1,0:T(8,128)(2,1)S(1)}, bf16[3,3,256,128]{3,2,1,0:T(8,128)(2,1)}, u32[]{:S(2)}) copy-start(bf16[3,3,256,128]{3,2,1,0:T(8,128)(2,1)} %param.15) | copy-start | bytes 1769476
  2.4 3.3 %collective-permute-start = (bf16[4,48,128]{2,1,0:T(8,128)(2,1)S(1)}, bf16[4,48,128]{2,1,0:T(8,128)(2,1)S(1)}, u32[]{:S(2)}, u32[]{:S(2)}) collective-permute-start(bf16[4,48,128]{2,1,0:T(8,128)(2,1)S(1)} %shard_map.82.mine), channel_id=1, source_target_pairs={{0,1},{1,0},{2,3},{3,2},{4,5},{5,4},{6,7},{7,6},{8,9},{9,8},{10,11... | collective-permute-start | bytes 147464 | tf_op jit(solution)/shard_map/ppermute | solution.py:320
  2.9 8.4 %collective-permute-start.2 = (bf16[1,48,128]{2,1,0:T(8,128)(2,1)S(1)}, bf16[1,48,128]{2,1,0:T(8,128)(2,1)S(1)}, u32[]{:S(2)}, u32[]{:S(2)}) collective-permute-start(bf16[1,48,128]{2,1,0:T(8,128)(2,1)S(1)} %get-tuple-element.7), channel_id=1, source_target_pairs={{0,2},{1,3},{2,0},{3,1},{4,6},{5,7},{6,4},{7,5},{8,10},{9,11},{10,... | collective-permute-start | bytes 36872 | tf_op jit(solution)/shard_map/ppermute | solution.py:324
  5.5 9.5 %collective-permute-start.8 = (bf16[3,768,128]{2,1,0:T(8,128)(2,1)S(1)}, bf16[3,768,128]{2,1,0:T(8,128)(2,1)S(1)}, u32[]{:S(2)}, u32[]{:S(2)}) collective-permute-start(bf16[3,768,128]{2,1,0:T(8,128)(2,1)S(1)} %bitcast.6), channel_id=1, source_target_pairs={{0,1},{1,0},{2,3},{3,2},{4,5},{5,4},{6,7},{7,6},{8,9},{9,8},{10,11... | collective-permute-start | bytes 1769480 | tf_op jit(solution)/shard_map/ppermute | solution.py:318
  5.7 5.7 %collective-permute-start.1 = (bf16[2,48,128]{2,1,0:T(8,128)(2,1)S(1)}, bf16[2,48,128]{2,1,0:T(8,128)(2,1)S(1)}, u32[]{:S(2)}, u32[]{:S(2)}) collective-permute-start(bf16[2,48,128]{2,1,0:T(8,128)(2,1)S(1)} %pad_maximum_fusion), channel_id=1, source_target_pairs={{0,4},{1,7},{2,6},{3,5},{4,12},{5,15},{6,14},{7,13},{8,0},{9,3},{1... | collective-permute-start | bytes 73736 | tf_op jit(solution)/shard_map/ppermute | solution.py:324
  7.3 5.9 %collective-permute-start.3 = (bf16[2,48,128]{2,1,0:T(8,128)(2,1)S(1)}, bf16[2,48,128]{2,1,0:T(8,128)(2,1)S(1)}, u32[]{:S(2)}, u32[]{:S(2)}) collective-permute-start(bf16[2,48,128]{2,1,0:T(8,128)(2,1)S(1)} %pad_maximum_fusion.1), channel_id=1, source_target_pairs={{0,12},{1,15},{2,14},{3,13},{4,8},{5,11},{6,10},{7,9},{8,4},{9,7},... | collective-permute-start | bytes 73736 | tf_op jit(solution)/shard_map/ppermute | solution.py:324
  9.8 4.0 %collective-permute-start.4 = (bf16[2,48,128]{2,1,0:T(8,128)(2,1)S(1)}, bf16[2,48,128]{2,1,0:T(8,128)(2,1)S(1)}, u32[]{:S(2)}, u32[]{:S(2)}) collective-permute-start(bf16[2,48,128]{2,1,0:T(8,128)(2,1)S(1)} %pad_maximum_fusion.2), channel_id=1, source_target_pairs={{0,8},{1,11},{2,10},{3,9},{4,0},{5,3},{6,2},{7,1},{8,12},{9,15},{1... | collective-permute-start | bytes 73736 | tf_op jit(solution)/shard_map/ppermute | solution.py:324
  11.4 3.6 %collective-permute-start.5 = (bf16[3,48,128]{2,1,0:T(8,128)(2,1)S(1)}, bf16[3,48,128]{2,1,0:T(8,128)(2,1)S(1)}, u32[]{:S(2)}, u32[]{:S(2)}) collective-permute-start(bf16[3,48,128]{2,1,0:T(8,128)(2,1)S(1)} %constant_dynamic-update-slice_fusion.refs_0_), channel_id=1, source_target_pairs={{0,1},{1,0},{2,3},{3,2},{4,5},{5,4},{6,7},{7,6},{8,9},{9,8},{10,11... | collective-permute-start | bytes 110600 | tf_op jit(solution)/shard_map/ppermute | solution.py:327
  13.2 1.2 %collective-permute-start.6 = (bf16[2,48,128]{2,1,0:T(8,128)(2,1)S(1)}, bf16[2,48,128]{2,1,0:T(8,128)(2,1)S(1)}, u32[]{:S(2)}, u32[]{:S(2)}) collective-permute-start(bf16[2,48,128]{2,1,0:T(8,128)(2,1)S(1)} %collective-permute-done.3.refs_1_), channel_id=1, source_target_pairs={{0,1},{1,0},{2,3},{3,2},{4,5},{5,4},{6,7},{7,6},{8,9},{9,8},{10,11... | collective-permute-start | bytes 73736 | tf_op jit(solution)/shard_map/ppermute | solution.py:327
  13.8 1.2 %collective-permute-start.7 = (bf16[2,48,128]{2,1,0:T(8,128)(2,1)S(1)}, bf16[2,48,128]{2,1,0:T(8,128)(2,1)S(1)}, u32[]{:S(2)}, u32[]{:S(2)}) collective-permute-start(bf16[2,48,128]{2,1,0:T(8,128)(2,1)S(1)} %collective-permute-done.4.refs_2_), channel_id=1, source_target_pairs={{0,1},{1,0},{2,3},{3,2},{4,5},{5,4},{6,7},{7,6},{8,9},{9,8},{10,11... | collective-permute-start | bytes 73736 | tf_op jit(solution)/shard_map/ppermute | solution.py:327

commit v7 on v6

--- a/solution.py
+++ b/solution.py
@@ -125,12 +125,12 @@
         pltpu.make_async_copy(valw_hbm, weights.at[:, columns], sems.at[3]),
         pltpu.make_async_copy(mask_hbm, mask, sems.at[4]),
     ]
-    for copy in small:
+    for copy in (small[0], small[2], small[1]):
         copy.start()
     loads = [
         pltpu.make_async_copy(tokens_hbm.at[along(date, i, tiles)], tokens.at[i], token_sems.at[i]) for i in range(tiles)
     ]
-    for copy in loads:
+    for copy in loads + small[3:]:
         copy.start()
     small[0].wait()
     table[...] = encoding_rows(days, dates, width)
@@ -175,18 +175,18 @@
 
 
 def merge(blocks, pixels, start, count):
-    levels = [jnp.sum(tail.astype(F32), axis=0, keepdims=True) for _, tail in blocks]
+    own = lax.rem(iota((count, LANES), 1), HSIZE) == iota((count, LANES), 0) + start
+    masked = []
+    for _, tail in blocks:
+        tail = tail.astype(F32)
+        pieces = [jnp.where(own, tail[i : i + 1], 0.0).astype(BF16) for i in range(3)]
+        masked.append(jnp.concatenate(pieces, axis=1))
+    wide = dot(jnp.concatenate(masked, axis=0), same_head(3 * LANES))
+    levels = [wide[i * count : (i + 1) * count] for i in range(len(blocks))]
     best = functools.reduce(jnp.maximum, levels)
     shares = [jnp.exp2(level - best) for level in levels]
-    scale = 1.0 / functools.reduce(jnp.add, shares)
-    own = lax.rem(iota((count, LANES), 1), HSIZE) == iota((count, LANES), 0) + start
-    spread = same_head(2 * LANES)
-    pooled = jnp.zeros((count, LANES), F32)
-    for (part, _), share in zip(blocks, shares):
-        share = share * scale
-        high = share.astype(BF16).astype(F32)
-        both = jnp.concatenate([jnp.where(own, high, 0.0), jnp.where(own, share - high, 0.0)], axis=1)
-        pooled = pooled + dot(both.astype(BF16), spread) * part.astype(F32)
+    parts = [share * part.astype(F32) for share, (part, _) in zip(shares, blocks)]
+    pooled = functools.reduce(jnp.add, parts) / functools.reduce(jnp.add, shares)
     return pooled.astype(BF16).astype(F32)
 
 

time: 16.6 us -> 16.5 us (level)
  no operation moved by 1% of the time
where the time goes in v7:
time: 16.5 us; the launch traced here: 16.4 us
  starting transfers between devices  9.92 us (60%)
  Pallas kernels  3.73 us (23%)
  waiting for transfers between devices  2.64 us (16%)
    ppermute x4, starting transfers between devices, local(): lax.ppermute(block, ('date', 'tile', 'head'), routes(tiles, slabs, slot, k))  8.26 us
    pallas_call x1, Pallas kernels, attend(): pl.pallas_call(functools.partial(attend_kernel, dates), in_specs=[pl.Bloc...  2.35 us
    ppermute x4, waiting for transfers between devices, local(): lax.ppermute(block, ('date', 'tile', 'head'), routes(tiles, slabs, slot, k))  1.73 us
    pallas_call x1, Pallas kernels, convolve(): pl.pallas_call(functools.partial(convolve_kernel, pixels, cols, slabs, sl...  1.38 us
    ppermute x3, starting transfers between devices, local(): swapped = [lax.ppermute(part, 'head', swap) for part in got]  0.99 us
    ppermute x3, waiting for transfers between devices, local(): swapped = [lax.ppermute(part, 'head', swap) for part in got]  0.9 us
    ppermute x1, starting transfers between devices, local(): theirs = lax.ppermute(mine, 'head', swap)  0.52 us
  transfers between devices with their start and end apart: 9, of which 4 were waited for; matrix products, arithmetic and copies ran while one was open for 0% of the time, Pallas kernels for 0%

profile of v7, /device:TPU:0, one launch (start us, length us, event | category | flops | bytes accessed | tf_op | source)
XLA Modules:
  0.0 16.4 jit_solution(3277536435664428215)
XLA Ops:
  0.0 0.0 copy-start
  0.0 0.0 copy-start.1
  0.0 2.3 %shard_map.82.mine = bf16[4,48,128]{2,1,0:T(8,128)(2,1)S(1)} custom-call(bf16[4,512,256]{2,1,0:T(8,128)(2,1)} %bitcast.9, s32[4,32,16]{2,1,0:T(8,128)} %bitcast.10, s32[16]{0:T(128)} %days_hbm.1, f32[1,128]{1,0:T(1,128)} %bitcast.11, bf16[256,128]{1,0:T(8,128)(2,1)} %keyw_hbm.1, bf16[256,128]{1,0:T(8,128)(2,1)} %valw_hbm.1), custom_call_target="tpu_custom_call" | custom-call | tf_op jit(solution)/shard_map/pallas_call | solution.py:157
  2.4 0.5 %collective-permute-start = (bf16[4,48,128]{2,1,0:T(8,128)(2,1)S(1)}, bf16[4,48,128]{2,1,0:T(8,128)(2,1)S(1)}, u32[]{:S(2)}, u32[]{:S(2)}) collective-permute-start(bf16[4,48,128]{2,1,0:T(8,128)(2,1)S(1)} %shard_map.82.mine), channel_id=1, source_target_pairs={{0,1},{1,0},{2,3},{3,2},{4,5},{5,4},{6,7},{7,6},{8,9},{9,8},{10,11... | collective-permute-start | bytes 147464 | tf_op jit(solution)/shard_map/ppermute | solution.py:320
  2.9 2.6 %collective-permute-start.2 = (bf16[1,48,128]{2,1,0:T(8,128)(2,1)S(1)}, bf16[1,48,128]{2,1,0:T(8,128)(2,1)S(1)}, u32[]{:S(2)}, u32[]{:S(2)}) collective-permute-start(bf16[1,48,128]{2,1,0:T(8,128)(2,1)S(1)} %get-tuple-element.7), channel_id=1, source_target_pairs={{0,2},{1,3},{2,0},{3,1},{4,6},{5,7},{6,4},{7,5},{8,10},{9,11},{10,... | collective-permute-start | bytes 36872 | tf_op jit(solution)/shard_map/ppermute | solution.py:324
  5.5 0.0 copy-done
  5.5 0.2 collective-permute-start.8
  5.6 0.0 collective-permute-done.theirs
  5.6 1.6 %collective-permute-start.1 = (bf16[2,48,128]{2,1,0:T(8,128)(2,1)S(1)}, bf16[2,48,128]{2,1,0:T(8,128)(2,1)S(1)}, u32[]{:S(2)}, u32[]{:S(2)}) collective-permute-start(bf16[2,48,128]{2,1,0:T(8,128)(2,1)S(1)} %pad_maximum_fusion), channel_id=1, source_target_pairs={{0,4},{1,7},{2,6},{3,5},{4,12},{5,15},{6,14},{7,13},{8,0},{9,3},{1... | collective-permute-start | bytes 73736 | tf_op jit(solution)/shard_map/ppermute | solution.py:324
  7.3 2.5 %collective-permute-start.3 = (bf16[2,48,128]{2,1,0:T(8,128)(2,1)S(1)}, bf16[2,48,128]{2,1,0:T(8,128)(2,1)S(1)}, u32[]{:S(2)}, u32[]{:S(2)}) collective-permute-start(bf16[2,48,128]{2,1,0:T(8,128)(2,1)S(1)} %pad_maximum_fusion.1), channel_id=1, source_target_pairs={{0,12},{1,15},{2,14},{3,13},{4,8},{5,11},{6,10},{7,9},{8,4},{9,7},... | collective-permute-start | bytes 73736 | tf_op jit(solution)/shard_map/ppermute | solution.py:324
  9.7 1.6 %collective-permute-start.4 = (bf16[2,48,128]{2,1,0:T(8,128)(2,1)S(1)}, bf16[2,48,128]{2,1,0:T(8,128)(2,1)S(1)}, u32[]{:S(2)}, u32[]{:S(2)}) collective-permute-start(bf16[2,48,128]{2,1,0:T(8,128)(2,1)S(1)} %pad_maximum_fusion.2), channel_id=1, source_target_pairs={{0,8},{1,11},{2,10},{3,9},{4,0},{5,3},{6,2},{7,1},{8,12},{9,15},{1... | collective-permute-start | bytes 73736 | tf_op jit(solution)/shard_map/ppermute | solution.py:324
  11.3 0.0 collective-permute-done.1
  11.3 0.0 collective-permute-done.2
  11.4 0.7 %collective-permute-start.5 = (bf16[3,48,128]{2,1,0:T(8,128)(2,1)S(1)}, bf16[3,48,128]{2,1,0:T(8,128)(2,1)S(1)}, u32[]{:S(2)}, u32[]{:S(2)}) collective-permute-start(bf16[3,48,128]{2,1,0:T(8,128)(2,1)S(1)} %constant_dynamic-update-slice_fusion.refs_0_), channel_id=1, source_target_pairs={{0,1},{1,0},{2,3},{3,2},{4,5},{5,4},{6,7},{7,6},{8,9},{9,8},{10,11... | collective-permute-start | bytes 110600 | tf_op jit(solution)/shard_map/ppermute | solution.py:327
  12.0 1.1 %collective-permute-done.3.refs_1_ = bf16[2,48,128]{2,1,0:T(8,128)(2,1)S(1)} collective-permute-done((bf16[2,48,128]{2,1,0:T(8,128)(2,1)S(1)}, bf16[2,48,128]{2,1,0:T(8,128)(2,1)S(1)}, u32[]{:S(2)}, u32[]{:S(2)}) %collective-permute-start.3) | collective-permute-done | bytes 24608 | tf_op jit(solution)/shard_map/ppermute | solution.py:324
  13.2 0.0 collective-permute-start.6
  13.2 0.6 %collective-permute-done.4.refs_2_ = bf16[2,48,128]{2,1,0:T(8,128)(2,1)S(1)} collective-permute-done((bf16[2,48,128]{2,1,0:T(8,128)(2,1)S(1)}, bf16[2,48,128]{2,1,0:T(8,128)(2,1)S(1)}, u32[]{:S(2)}, u32[]{:S(2)}) %collective-permute-start.4) | collective-permute-done | bytes 24608 | tf_op jit(solution)/shard_map/ppermute | solution.py:324
  13.8 0.3 %collective-permute-start.7 = (bf16[2,48,128]{2,1,0:T(8,128)(2,1)S(1)}, bf16[2,48,128]{2,1,0:T(8,128)(2,1)S(1)}, u32[]{:S(2)}, u32[]{:S(2)}) collective-permute-start(bf16[2,48,128]{2,1,0:T(8,128)(2,1)S(1)} %collective-permute-done.4.refs_2_), channel_id=1, source_target_pairs={{0,1},{1,0},{2,3},{3,2},{4,5},{5,4},{6,7},{7,6},{8,9},{9,8},{10,11... | collective-permute-start | bytes 73736 | tf_op jit(solution)/shard_map/ppermute | solution.py:327
  14.1 0.3 %collective-permute-done.6.refs_4_ = bf16[2,48,128]{2,1,0:T(8,128)(2,1)S(1)} collective-permute-done((bf16[2,48,128]{2,1,0:T(8,128)(2,1)S(1)}, bf16[2,48,128]{2,1,0:T(8,128)(2,1)S(1)}, u32[]{:S(2)}, u32[]{:S(2)}) %collective-permute-start.6) | collective-permute-done | bytes 24608 | tf_op jit(solution)/shard_map/ppermute | solution.py:327
  14.4 0.6 %collective-permute-done.7.refs_5_ = bf16[2,48,128]{2,1,0:T(8,128)(2,1)S(1)} collective-permute-done((bf16[2,48,128]{2,1,0:T(8,128)(2,1)S(1)}, bf16[2,48,128]{2,1,0:T(8,128)(2,1)S(1)}, u32[]{:S(2)}, u32[]{:S(2)}) %collective-permute-start.7) | collective-permute-done | bytes 24608 | tf_op jit(solution)/shard_map/ppermute | solution.py:327
  15.0 0.0 collective-permute-done.5.refs_3_
  15.0 0.0 collective-permute-done.8.refs_7_
  15.0 0.0 copy-done.1
  15.0 1.4 %shard_map.83 = bf16[32,128]{1,0:T(8,128)(2,1)} custom-call(bf16[4,48,128]{2,1,0:T(8,128)(2,1)S(1)} %shard_map.82.mine, bf16[4,48,128]{2,1,0:T(8,128)(2,1)S(1)} %collective-permute-done.theirs, bf16[3,48,128]{2,1,0:T(8,128)(2,1)S(1)} %constant_dynamic-update-slice_fusion.refs_0_, bf16[2,48,128]{2,1,0:T(8,128)(2,1)S(1)} %collective-permute-done.3.refs_1_, ...), custom_call_target="tpu_custom_call" | custom-call | tf_op jit(solution)/shard_map/pallas_call | solution.py:274
  (7 shorter events, 0.0 us)
Async XLA Ops:
  0.0 5.5 %copy-start = (bf16[3,3,256,128]{3,2,1,0:T(8,128)(2,1)S(1)}, bf16[3,3,256,128]{3,2,1,0:T(8,128)(2,1)}, u32[]{:S(2)}) copy-start(bf16[3,3,256,128]{3,2,1,0:T(8,128)(2,1)} %param.14) | copy-start | bytes 1769476
  0.0 15.0 %copy-start.1 = (bf16[3,3,256,128]{3,2,1,0:T(8,128)(2,1)S(1)}, bf16[3,3,256,128]{3,2,1,0:T(8,128)(2,1)}, u32[]{:S(2)}) copy-start(bf16[3,3,256,128]{3,2,1,0:T(8,128)(2,1)} %param.15) | copy-start | bytes 1769476
  2.4 3.3 %collective-permute-start = (bf16[4,48,128]{2,1,0:T(8,128)(2,1)S(1)}, bf16[4,48,128]{2,1,0:T(8,128)(2,1)S(1)}, u32[]{:S(2)}, u32[]{:S(2)}) collective-permute-start(bf16[4,48,128]{2,1,0:T(8,128)(2,1)S(1)} %shard_map.82.mine), channel_id=1, source_target_pairs={{0,1},{1,0},{2,3},{3,2},{4,5},{5,4},{6,7},{7,6},{8,9},{9,8},{10,11... | collective-permute-start | bytes 147464 | tf_op jit(solution)/shard_map/ppermute | solution.py:320
  2.9 8.5 %collective-permute-start.2 = (bf16[1,48,128]{2,1,0:T(8,128)(2,1)S(1)}, bf16[1,48,128]{2,1,0:T(8,128)(2,1)S(1)}, u32[]{:S(2)}, u32[]{:S(2)}) collective-permute-start(bf16[1,48,128]{2,1,0:T(8,128)(2,1)S(1)} %get-tuple-element.7), channel_id=1, source_target_pairs={{0,2},{1,3},{2,0},{3,1},{4,6},{5,7},{6,4},{7,5},{8,10},{9,11},{10,... | collective-permute-start | bytes 36872 | tf_op jit(solution)/shard_map/ppermute | solution.py:324
  5.5 9.5 %collective-permute-start.8 = (bf16[3,768,128]{2,1,0:T(8,128)(2,1)S(1)}, bf16[3,768,128]{2,1,0:T(8,128)(2,1)S(1)}, u32[]{:S(2)}, u32[]{:S(2)}) collective-permute-start(bf16[3,768,128]{2,1,0:T(8,128)(2,1)S(1)} %bitcast.6), channel_id=1, source_target_pairs={{0,1},{1,0},{2,3},{3,2},{4,5},{5,4},{6,7},{7,6},{8,9},{9,8},{10,11... | collective-permute-start | bytes 1769480 | tf_op jit(solution)/shard_map/ppermute | solution.py:318
  5.6 5.7 %collective-permute-start.1 = (bf16[2,48,128]{2,1,0:T(8,128)(2,1)S(1)}, bf16[2,48,128]{2,1,0:T(8,128)(2,1)S(1)}, u32[]{:S(2)}, u32[]{:S(2)}) collective-permute-start(bf16[2,48,128]{2,1,0:T(8,128)(2,1)S(1)} %pad_maximum_fusion), channel_id=1, source_target_pairs={{0,4},{1,7},{2,6},{3,5},{4,12},{5,15},{6,14},{7,13},{8,0},{9,3},{1... | collective-permute-start | bytes 73736 | tf_op jit(solution)/shard_map/ppermute | solution.py:324
  7.3 5.9 %collective-permute-start.3 = (bf16[2,48,128]{2,1,0:T(8,128)(2,1)S(1)}, bf16[2,48,128]{2,1,0:T(8,128)(2,1)S(1)}, u32[]{:S(2)}, u32[]{:S(2)}) collective-permute-start(bf16[2,48,128]{2,1,0:T(8,128)(2,1)S(1)} %pad_maximum_fusion.1), channel_id=1, source_target_pairs={{0,12},{1,15},{2,14},{3,13},{4,8},{5,11},{6,10},{7,9},{8,4},{9,7},... | collective-permute-start | bytes 73736 | tf_op jit(solution)/shard_map/ppermute | solution.py:324
  9.7 4.0 %collective-permute-start.4 = (bf16[2,48,128]{2,1,0:T(8,128)(2,1)S(1)}, bf16[2,48,128]{2,1,0:T(8,128)(2,1)S(1)}, u32[]{:S(2)}, u32[]{:S(2)}) collective-permute-start(bf16[2,48,128]{2,1,0:T(8,128)(2,1)S(1)} %pad_maximum_fusion.2), channel_id=1, source_target_pairs={{0,8},{1,11},{2,10},{3,9},{4,0},{5,3},{6,2},{7,1},{8,12},{9,15},{1... | collective-permute-start | bytes 73736 | tf_op jit(solution)/shard_map/ppermute | solution.py:324
  11.4 3.6 %collective-permute-start.5 = (bf16[3,48,128]{2,1,0:T(8,128)(2,1)S(1)}, bf16[3,48,128]{2,1,0:T(8,128)(2,1)S(1)}, u32[]{:S(2)}, u32[]{:S(2)}) collective-permute-start(bf16[3,48,128]{2,1,0:T(8,128)(2,1)S(1)} %constant_dynamic-update-slice_fusion.refs_0_), channel_id=1, source_target_pairs={{0,1},{1,0},{2,3},{3,2},{4,5},{5,4},{6,7},{7,6},{8,9},{9,8},{10,11... | collective-permute-start | bytes 110600 | tf_op jit(solution)/shard_map/ppermute | solution.py:327
  13.2 1.2 %collective-permute-start.6 = (bf16[2,48,128]{2,1,0:T(8,128)(2,1)S(1)}, bf16[2,48,128]{2,1,0:T(8,128)(2,1)S(1)}, u32[]{:S(2)}, u32[]{:S(2)}) collective-permute-start(bf16[2,48,128]{2,1,0:T(8,128)(2,1)S(1)} %collective-permute-done.3.refs_1_), channel_id=1, source_target_pairs={{0,1},{1,0},{2,3},{3,2},{4,5},{5,4},{6,7},{7,6},{8,9},{9,8},{10,11... | collective-permute-start | bytes 73736 | tf_op jit(solution)/shard_map/ppermute | solution.py:327
  13.8 1.2 %collective-permute-start.7 = (bf16[2,48,128]{2,1,0:T(8,128)(2,1)S(1)}, bf16[2,48,128]{2,1,0:T(8,128)(2,1)S(1)}, u32[]{:S(2)}, u32[]{:S(2)}) collective-permute-start(bf16[2,48,128]{2,1,0:T(8,128)(2,1)S(1)} %collective-permute-done.4.refs_2_), channel_id=1, source_target_pairs={{0,1},{1,0},{2,3},{3,2},{4,5},{5,4},{6,7},{7,6},{8,9},{9,8},{10,11... | collective-permute-start | bytes 73736 | tf_op jit(solution)/shard_map/ppermute | solution.py:327

commit v8 on v7

--- a/solution.py
+++ b/solution.py
@@ -130,8 +130,8 @@
     loads = [
         pltpu.make_async_copy(tokens_hbm.at[along(date, i, tiles)], tokens.at[i], token_sems.at[i]) for i in range(tiles)
     ]
-    for copy in loads + small[3:]:
-        copy.start()
+    for i, copy in enumerate(loads + small[3:]):
+        copy.start(priority=i % 2)
     small[0].wait()
     table[...] = encoding_rows(days, dates, width)
     small[1].wait()

time: 16.5 us -> 16.5 us (level)
  no operation moved by 1% of the time
where the time goes in v8:
time: 16.5 us; the launch traced here: 16.4 us
  starting transfers between devices  9.92 us (60%)
  Pallas kernels  3.73 us (23%)
  waiting for transfers between devices  2.64 us (16%)
    ppermute x4, starting transfers between devices, local(): lax.ppermute(block, ('date', 'tile', 'head'), routes(tiles, slabs, slot, k))  8.26 us
    pallas_call x1, Pallas kernels, attend(): pl.pallas_call(functools.partial(attend_kernel, dates), in_specs=[pl.Bloc...  2.35 us
    ppermute x4, waiting for transfers between devices, local(): lax.ppermute(block, ('date', 'tile', 'head'), routes(tiles, slabs, slot, k))  1.73 us
    pallas_call x1, Pallas kernels, convolve(): pl.pallas_call(functools.partial(convolve_kernel, pixels, cols, slabs, sl...  1.38 us
    ppermute x3, starting transfers between devices, local(): swapped = [lax.ppermute(part, 'head', swap) for part in got]  0.99 us
    ppermute x3, waiting for transfers between devices, local(): swapped = [lax.ppermute(part, 'head', swap) for part in got]  0.9 us
    ppermute x1, starting transfers between devices, local(): theirs = lax.ppermute(mine, 'head', swap)  0.52 us
  transfers between devices with their start and end apart: 9, of which 4 were waited for; matrix products, arithmetic and copies ran while one was open for 0% of the time, Pallas kernels for 0%

profile of v8, /device:TPU:0, one launch (start us, length us, event | category | flops | bytes accessed | tf_op | source)
XLA Modules:
  0.0 16.4 jit_solution(14659835142281826204)
XLA Ops:
  0.0 0.0 copy-start
  0.0 0.0 copy-start.1
  0.0 2.3 %shard_map.82.mine = bf16[4,48,128]{2,1,0:T(8,128)(2,1)S(1)} custom-call(bf16[4,512,256]{2,1,0:T(8,128)(2,1)} %bitcast.9, s32[4,32,16]{2,1,0:T(8,128)} %bitcast.10, s32[16]{0:T(128)} %days_hbm.1, f32[1,128]{1,0:T(1,128)} %bitcast.11, bf16[256,128]{1,0:T(8,128)(2,1)} %keyw_hbm.1, bf16[256,128]{1,0:T(8,128)(2,1)} %valw_hbm.1), custom_call_target="tpu_custom_call" | custom-call | tf_op jit(solution)/shard_map/pallas_call | solution.py:157
  2.4 0.5 %collective-permute-start = (bf16[4,48,128]{2,1,0:T(8,128)(2,1)S(1)}, bf16[4,48,128]{2,1,0:T(8,128)(2,1)S(1)}, u32[]{:S(2)}, u32[]{:S(2)}) collective-permute-start(bf16[4,48,128]{2,1,0:T(8,128)(2,1)S(1)} %shard_map.82.mine), channel_id=1, source_target_pairs={{0,1},{1,0},{2,3},{3,2},{4,5},{5,4},{6,7},{7,6},{8,9},{9,8},{10,11... | collective-permute-start | bytes 147464 | tf_op jit(solution)/shard_map/ppermute | solution.py:320
  2.9 2.6 %collective-permute-start.2 = (bf16[1,48,128]{2,1,0:T(8,128)(2,1)S(1)}, bf16[1,48,128]{2,1,0:T(8,128)(2,1)S(1)}, u32[]{:S(2)}, u32[]{:S(2)}) collective-permute-start(bf16[1,48,128]{2,1,0:T(8,128)(2,1)S(1)} %get-tuple-element.7), channel_id=1, source_target_pairs={{0,2},{1,3},{2,0},{3,1},{4,6},{5,7},{6,4},{7,5},{8,10},{9,11},{10,... | collective-permute-start | bytes 36872 | tf_op jit(solution)/shard_map/ppermute | solution.py:324
  5.5 0.0 copy-done
  5.5 0.2 collective-permute-start.8
  5.6 0.0 collective-permute-done.theirs
  5.6 1.6 %collective-permute-start.1 = (bf16[2,48,128]{2,1,0:T(8,128)(2,1)S(1)}, bf16[2,48,128]{2,1,0:T(8,128)(2,1)S(1)}, u32[]{:S(2)}, u32[]{:S(2)}) collective-permute-start(bf16[2,48,128]{2,1,0:T(8,128)(2,1)S(1)} %pad_maximum_fusion), channel_id=1, source_target_pairs={{0,4},{1,7},{2,6},{3,5},{4,12},{5,15},{6,14},{7,13},{8,0},{9,3},{1... | collective-permute-start | bytes 73736 | tf_op jit(solution)/shard_map/ppermute | solution.py:324
  7.3 2.5 %collective-permute-start.3 = (bf16[2,48,128]{2,1,0:T(8,128)(2,1)S(1)}, bf16[2,48,128]{2,1,0:T(8,128)(2,1)S(1)}, u32[]{:S(2)}, u32[]{:S(2)}) collective-permute-start(bf16[2,48,128]{2,1,0:T(8,128)(2,1)S(1)} %pad_maximum_fusion.1), channel_id=1, source_target_pairs={{0,12},{1,15},{2,14},{3,13},{4,8},{5,11},{6,10},{7,9},{8,4},{9,7},... | collective-permute-start | bytes 73736 | tf_op jit(solution)/shard_map/ppermute | solution.py:324
  9.7 1.6 %collective-permute-start.4 = (bf16[2,48,128]{2,1,0:T(8,128)(2,1)S(1)}, bf16[2,48,128]{2,1,0:T(8,128)(2,1)S(1)}, u32[]{:S(2)}, u32[]{:S(2)}) collective-permute-start(bf16[2,48,128]{2,1,0:T(8,128)(2,1)S(1)} %pad_maximum_fusion.2), channel_id=1, source_target_pairs={{0,8},{1,11},{2,10},{3,9},{4,0},{5,3},{6,2},{7,1},{8,12},{9,15},{1... | collective-permute-start | bytes 73736 | tf_op jit(solution)/shard_map/ppermute | solution.py:324
  11.3 0.0 collective-permute-done.1
  11.3 0.0 collective-permute-done.2
  11.4 0.7 %collective-permute-start.5 = (bf16[3,48,128]{2,1,0:T(8,128)(2,1)S(1)}, bf16[3,48,128]{2,1,0:T(8,128)(2,1)S(1)}, u32[]{:S(2)}, u32[]{:S(2)}) collective-permute-start(bf16[3,48,128]{2,1,0:T(8,128)(2,1)S(1)} %constant_dynamic-update-slice_fusion.refs_0_), channel_id=1, source_target_pairs={{0,1},{1,0},{2,3},{3,2},{4,5},{5,4},{6,7},{7,6},{8,9},{9,8},{10,11... | collective-permute-start | bytes 110600 | tf_op jit(solution)/shard_map/ppermute | solution.py:327
  12.0 1.1 %collective-permute-done.3.refs_1_ = bf16[2,48,128]{2,1,0:T(8,128)(2,1)S(1)} collective-permute-done((bf16[2,48,128]{2,1,0:T(8,128)(2,1)S(1)}, bf16[2,48,128]{2,1,0:T(8,128)(2,1)S(1)}, u32[]{:S(2)}, u32[]{:S(2)}) %collective-permute-start.3) | collective-permute-done | bytes 24608 | tf_op jit(solution)/shard_map/ppermute | solution.py:324
  13.2 0.0 collective-permute-start.6
  13.2 0.6 %collective-permute-done.4.refs_2_ = bf16[2,48,128]{2,1,0:T(8,128)(2,1)S(1)} collective-permute-done((bf16[2,48,128]{2,1,0:T(8,128)(2,1)S(1)}, bf16[2,48,128]{2,1,0:T(8,128)(2,1)S(1)}, u32[]{:S(2)}, u32[]{:S(2)}) %collective-permute-start.4) | collective-permute-done | bytes 24608 | tf_op jit(solution)/shard_map/ppermute | solution.py:324
  13.8 0.3 %collective-permute-start.7 = (bf16[2,48,128]{2,1,0:T(8,128)(2,1)S(1)}, bf16[2,48,128]{2,1,0:T(8,128)(2,1)S(1)}, u32[]{:S(2)}, u32[]{:S(2)}) collective-permute-start(bf16[2,48,128]{2,1,0:T(8,128)(2,1)S(1)} %collective-permute-done.4.refs_2_), channel_id=1, source_target_pairs={{0,1},{1,0},{2,3},{3,2},{4,5},{5,4},{6,7},{7,6},{8,9},{9,8},{10,11... | collective-permute-start | bytes 73736 | tf_op jit(solution)/shard_map/ppermute | solution.py:327
  14.1 0.3 %collective-permute-done.6.refs_4_ = bf16[2,48,128]{2,1,0:T(8,128)(2,1)S(1)} collective-permute-done((bf16[2,48,128]{2,1,0:T(8,128)(2,1)S(1)}, bf16[2,48,128]{2,1,0:T(8,128)(2,1)S(1)}, u32[]{:S(2)}, u32[]{:S(2)}) %collective-permute-start.6) | collective-permute-done | bytes 24608 | tf_op jit(solution)/shard_map/ppermute | solution.py:327
  14.4 0.6 %collective-permute-done.7.refs_5_ = bf16[2,48,128]{2,1,0:T(8,128)(2,1)S(1)} collective-permute-done((bf16[2,48,128]{2,1,0:T(8,128)(2,1)S(1)}, bf16[2,48,128]{2,1,0:T(8,128)(2,1)S(1)}, u32[]{:S(2)}, u32[]{:S(2)}) %collective-permute-start.7) | collective-permute-done | bytes 24608 | tf_op jit(solution)/shard_map/ppermute | solution.py:327
  15.0 0.0 collective-permute-done.5.refs_3_
  15.0 0.0 collective-permute-done.8.refs_7_
  15.0 0.0 copy-done.1
  15.0 1.4 %shard_map.83 = bf16[32,128]{1,0:T(8,128)(2,1)} custom-call(bf16[4,48,128]{2,1,0:T(8,128)(2,1)S(1)} %shard_map.82.mine, bf16[4,48,128]{2,1,0:T(8,128)(2,1)S(1)} %collective-permute-done.theirs, bf16[3,48,128]{2,1,0:T(8,128)(2,1)S(1)} %constant_dynamic-update-slice_fusion.refs_0_, bf16[2,48,128]{2,1,0:T(8,128)(2,1)S(1)} %collective-permute-done.3.refs_1_, ...), custom_call_target="tpu_custom_call" | custom-call | tf_op jit(solution)/shard_map/pallas_call | solution.py:274
  (7 shorter events, 0.0 us)
Async XLA Ops:
  0.0 5.5 %copy-start = (bf16[3,3,256,128]{3,2,1,0:T(8,128)(2,1)S(1)}, bf16[3,3,256,128]{3,2,1,0:T(8,128)(2,1)}, u32[]{:S(2)}) copy-start(bf16[3,3,256,128]{3,2,1,0:T(8,128)(2,1)} %param.14) | copy-start | bytes 1769476
  0.0 15.0 %copy-start.1 = (bf16[3,3,256,128]{3,2,1,0:T(8,128)(2,1)S(1)}, bf16[3,3,256,128]{3,2,1,0:T(8,128)(2,1)}, u32[]{:S(2)}) copy-start(bf16[3,3,256,128]{3,2,1,0:T(8,128)(2,1)} %param.15) | copy-start | bytes 1769476
  2.4 3.3 %collective-permute-start = (bf16[4,48,128]{2,1,0:T(8,128)(2,1)S(1)}, bf16[4,48,128]{2,1,0:T(8,128)(2,1)S(1)}, u32[]{:S(2)}, u32[]{:S(2)}) collective-permute-start(bf16[4,48,128]{2,1,0:T(8,128)(2,1)S(1)} %shard_map.82.mine), channel_id=1, source_target_pairs={{0,1},{1,0},{2,3},{3,2},{4,5},{5,4},{6,7},{7,6},{8,9},{9,8},{10,11... | collective-permute-start | bytes 147464 | tf_op jit(solution)/shard_map/ppermute | solution.py:320
  2.9 8.5 %collective-permute-start.2 = (bf16[1,48,128]{2,1,0:T(8,128)(2,1)S(1)}, bf16[1,48,128]{2,1,0:T(8,128)(2,1)S(1)}, u32[]{:S(2)}, u32[]{:S(2)}) collective-permute-start(bf16[1,48,128]{2,1,0:T(8,128)(2,1)S(1)} %get-tuple-element.7), channel_id=1, source_target_pairs={{0,2},{1,3},{2,0},{3,1},{4,6},{5,7},{6,4},{7,5},{8,10},{9,11},{10,... | collective-permute-start | bytes 36872 | tf_op jit(solution)/shard_map/ppermute | solution.py:324
  5.5 9.5 %collective-permute-start.8 = (bf16[3,768,128]{2,1,0:T(8,128)(2,1)S(1)}, bf16[3,768,128]{2,1,0:T(8,128)(2,1)S(1)}, u32[]{:S(2)}, u32[]{:S(2)}) collective-permute-start(bf16[3,768,128]{2,1,0:T(8,128)(2,1)S(1)} %bitcast.6), channel_id=1, source_target_pairs={{0,1},{1,0},{2,3},{3,2},{4,5},{5,4},{6,7},{7,6},{8,9},{9,8},{10,11... | collective-permute-start | bytes 1769480 | tf_op jit(solution)/shard_map/ppermute | solution.py:318
  5.6 5.7 %collective-permute-start.1 = (bf16[2,48,128]{2,1,0:T(8,128)(2,1)S(1)}, bf16[2,48,128]{2,1,0:T(8,128)(2,1)S(1)}, u32[]{:S(2)}, u32[]{:S(2)}) collective-permute-start(bf16[2,48,128]{2,1,0:T(8,128)(2,1)S(1)} %pad_maximum_fusion), channel_id=1, source_target_pairs={{0,4},{1,7},{2,6},{3,5},{4,12},{5,15},{6,14},{7,13},{8,0},{9,3},{1... | collective-permute-start | bytes 73736 | tf_op jit(solution)/shard_map/ppermute | solution.py:324
  7.3 5.9 %collective-permute-start.3 = (bf16[2,48,128]{2,1,0:T(8,128)(2,1)S(1)}, bf16[2,48,128]{2,1,0:T(8,128)(2,1)S(1)}, u32[]{:S(2)}, u32[]{:S(2)}) collective-permute-start(bf16[2,48,128]{2,1,0:T(8,128)(2,1)S(1)} %pad_maximum_fusion.1), channel_id=1, source_target_pairs={{0,12},{1,15},{2,14},{3,13},{4,8},{5,11},{6,10},{7,9},{8,4},{9,7},... | collective-permute-start | bytes 73736 | tf_op jit(solution)/shard_map/ppermute | solution.py:324
  9.7 4.0 %collective-permute-start.4 = (bf16[2,48,128]{2,1,0:T(8,128)(2,1)S(1)}, bf16[2,48,128]{2,1,0:T(8,128)(2,1)S(1)}, u32[]{:S(2)}, u32[]{:S(2)}) collective-permute-start(bf16[2,48,128]{2,1,0:T(8,128)(2,1)S(1)} %pad_maximum_fusion.2), channel_id=1, source_target_pairs={{0,8},{1,11},{2,10},{3,9},{4,0},{5,3},{6,2},{7,1},{8,12},{9,15},{1... | collective-permute-start | bytes 73736 | tf_op jit(solution)/shard_map/ppermute | solution.py:324
  11.4 3.6 %collective-permute-start.5 = (bf16[3,48,128]{2,1,0:T(8,128)(2,1)S(1)}, bf16[3,48,128]{2,1,0:T(8,128)(2,1)S(1)}, u32[]{:S(2)}, u32[]{:S(2)}) collective-permute-start(bf16[3,48,128]{2,1,0:T(8,128)(2,1)S(1)} %constant_dynamic-update-slice_fusion.refs_0_), channel_id=1, source_target_pairs={{0,1},{1,0},{2,3},{3,2},{4,5},{5,4},{6,7},{7,6},{8,9},{9,8},{10,11... | collective-permute-start | bytes 110600 | tf_op jit(solution)/shard_map/ppermute | solution.py:327
  13.2 1.2 %collective-permute-start.6 = (bf16[2,48,128]{2,1,0:T(8,128)(2,1)S(1)}, bf16[2,48,128]{2,1,0:T(8,128)(2,1)S(1)}, u32[]{:S(2)}, u32[]{:S(2)}) collective-permute-start(bf16[2,48,128]{2,1,0:T(8,128)(2,1)S(1)} %collective-permute-done.3.refs_1_), channel_id=1, source_target_pairs={{0,1},{1,0},{2,3},{3,2},{4,5},{5,4},{6,7},{7,6},{8,9},{9,8},{10,11... | collective-permute-start | bytes 73736 | tf_op jit(solution)/shard_map/ppermute | solution.py:327
  13.8 1.2 %collective-permute-start.7 = (bf16[2,48,128]{2,1,0:T(8,128)(2,1)S(1)}, bf16[2,48,128]{2,1,0:T(8,128)(2,1)S(1)}, u32[]{:S(2)}, u32[]{:S(2)}) collective-permute-start(bf16[2,48,128]{2,1,0:T(8,128)(2,1)S(1)} %collective-permute-done.4.refs_2_), channel_id=1, source_target_pairs={{0,1},{1,0},{2,3},{3,2},{4,5},{5,4},{6,7},{7,6},{8,9},{9,8},{10,11... | collective-permute-start | bytes 73736 | tf_op jit(solution)/shard_map/ppermute | solution.py:327
